TPU v7x, 32 devices: a whole 2x2x4 slice. The times are simulated.
32 devices in a mesh: head: 4 (over y, x), seq: 8 (over z, core).
Axes of the slice: x: 2, y: 2, z: 4, core: 2. Of those that a mesh axis runs over, the one named last changes fastest.
Arguments:
- inputs: bfloat16 [2, 2048, 2048], P(None, ('seq', 'head')), may hold values from -6 to 6
- cotangent: bfloat16 [2, 2048, 2048], P(None, ('seq', 'head')), may hold values from -6 to 6
- routes: int32 [2, 2048, 6], P(None, 'seq'), may hold values from 0 to 15, all different within a row; in each aligned block of 256 rows (0 to 255, 256 to 511, ..., all dimensions but the last counted through in order) at most 128 rows name the same one
- gate_weights: float32 [2, 2048, 6], P(None, 'seq'), may hold values from 0.2 to 0.8
- attn_gain: bfloat16 [2048], P('seq'), may hold values from 0.099609375 to 1.8984375
- latent_gain: bfloat16 [512], P('seq'), may hold values from 0.099609375 to 1.8984375
- ffn_gain: bfloat16 [2048], P('seq'), may hold values from 0.099609375 to 1.8984375
- query_proj: bfloat16 [2048, 3072], P('seq', 'head'), may hold values from -0.125 to 0.125
- latent_proj: bfloat16 [2048, 576], P('seq'), may hold values from -0.125 to 0.125
- expand_proj: bfloat16 [512, 4096], P('seq', 'head'), may hold values from -0.25 to 0.25
- out_proj: bfloat16 [2048, 2048], P('head', 'seq'), may hold values from -3 to 3
- shared_gate: bfloat16 [2048, 2816], P('seq', 'head'), may hold values from -0.125 to 0.125
- shared_up: bfloat16 [2048, 2816], P('seq', 'head'), may hold values from -0.125 to 0.125
- shared_down: bfloat16 [2816, 2048], P('head', 'seq'), may hold values from -0.109375 to 0.109375
- expert_gate: bfloat16 [32, 2048, 704], P(('seq', 'head')), may hold values from -0.125 to 0.125
- expert_up_weight: bfloat16 [32, 2048, 704], P(('seq', 'head')), may hold values from -0.125 to 0.125
- expert_down: bfloat16 [32, 704, 2048], P(('seq', 'head')), may hold values from -0.15625 to 0.15625
Outputs:
- output: bfloat16 [2, 2048, 2048], P(None, ('seq', 'head'))
- inputs_grad: bfloat16 [2, 2048, 2048], P(None, ('seq', 'head'))
- query_grad: float32 [2048, 3072], P('seq', 'head')
- latent_grad: float32 [2048, 576], P('seq')
- expand_grad: float32 [512, 4096], P('seq', 'head')
- outproj_grad: float32 [2048, 2048], P('head', 'seq')
- shgate_grad: float32 [2048, 2816], P('seq', 'head')
- shup_grad: float32 [2048, 2816], P('seq', 'head')
- shdown_grad: float32 [2816, 2048], P('head', 'seq')
- exgate_grad: float32 [32, 2048, 704], P(('seq', 'head'))
- exup_grad: float32 [32, 2048, 704], P(('seq', 'head'))
- exdown_grad: float32 [32, 704, 2048], P(('seq', 'head'))
- attngain_grad: float32 [2048], P('seq')
- latgain_grad: float32 [512], P('seq')
- ffngain_grad: float32 [2048], P('seq')
Inputs may be any that keep to these rules, and one draw needn't show every extreme that they name: `routes`: in each aligned block of 256 rows along a sequence, no expert is named by more than 128 rows, and in some block one expert is named by exactly 128.
All inputs are finite; a program needn't handle non-finite values.
Results may differ from a plain program's by a relative error of at most 0.03.
Values may be sent and summed in bfloat16 or wider, within the bound.
No kernel may reach another device: no remote copies, remote signals or barrier semaphores. Data moves between devices by JAX's collectives and lax.ppermute only.
A program may use at most 320 MiB of HBM per device.

v0:
```python
import jax
import jax.numpy as jnp
from jax import lax
from jax.sharding import PartitionSpec as P

HDIM = 128
RDIM = 64
RANK = 512
TOPK = 6
BLOCK = 256
QDIM = 192


EPSILON = 1e-06
ROPE_BASE = 10000.0
NEG_LARGE = -1e30


def rms_inverse(values):
    return lax.rsqrt(jnp.mean(values * values, axis=-1, keepdims=True) + EPSILON)


def rope_tables(positions, half_dim):
    frequency = ROPE_BASE ** (-jnp.arange(half_dim, dtype=jnp.float32) / half_dim)
    angles = positions.astype(jnp.float32)[:, None] * frequency[None, :]
    return (jnp.cos(angles), jnp.sin(angles))


def rope_turn(values, cosine_table, sine_table):
    half_dim = values.shape[-1] // 2
    first_half = values[..., :half_dim]
    second_half = values[..., half_dim:]
    return jnp.concatenate(
        [
            first_half * cosine_table - second_half * sine_table,
            first_half * sine_table + second_half * cosine_table,
        ],
        axis=-1,
    )


def rope_back(grad_values, cosine_table, sine_table):
    return rope_turn(grad_values, cosine_table, -sine_table)


def silu_parts(pre_values):
    sigmoid_val = jax.nn.sigmoid(pre_values)
    return (pre_values * sigmoid_val, sigmoid_val * (1.0 + pre_values * (1.0 - sigmoid_val)))


def norm_back(grad_normed, hat_rows, inverse, gain_vec):
    scaled = grad_normed * gain_vec
    gain_term = jnp.sum(grad_normed * hat_rows, axis=0)
    grad_rows = inverse * (scaled - hat_rows * jnp.mean(scaled * hat_rows, axis=-1, keepdims=True))
    return (grad_rows, gain_term)


def score_grads(
    queries, grad_att, log_sums, deltas, key_piece, value_piece, query_pos, key_pos, score_scale
):
    batch_size = queries.shape[0]
    heads_here = queries.shape[2]
    key_len = key_piece.shape[1]
    key_blocks = key_piece.reshape(batch_size, key_len, heads_here, QDIM)
    value_blocks = value_piece.reshape(batch_size, key_len, heads_here, HDIM)
    scores = (
        jnp.einsum("bqhd,bkhd->bhqk", queries, key_blocks, preferred_element_type=jnp.float32)
        * score_scale
    )
    allowed = (key_pos // BLOCK)[None, :] <= (query_pos // BLOCK)[:, None]
    probs = jnp.where(allowed, jnp.exp(scores - log_sums[..., None]), 0.0)
    grad_probs = jnp.einsum(
        "bqhd,bkhd->bhqk", grad_att, value_blocks, preferred_element_type=jnp.float32
    )
    grad_scores = (probs * (grad_probs - deltas[..., None])).astype(jnp.bfloat16)
    return (grad_scores, probs, key_blocks)


def local(
    inputs,
    cotangent,
    routes,
    gate_weights,
    attn_gain,
    latent_gain,
    ffn_gain,
    query_proj,
    latent_proj,
    expand_proj,
    out_proj,
    shared_gate,
    shared_up,
    shared_down,
    expert_gate,
    expert_up_weight,
    expert_down,
):
    seq_count = lax.axis_size("seq")
    head_count = lax.axis_size("head")
    seq_index = lax.axis_index("seq")
    head_index = lax.axis_index("head")
    batch_size, local_len, model_width = inputs.shape
    group_len = local_len * head_count
    row_count = batch_size * group_len
    heads_here = out_proj.shape[0] // HDIM
    score_scale = QDIM ** (-0.5)
    gathered = (
        lax.all_gather(query_proj, "seq", axis=0, tiled=True),
        lax.all_gather(latent_proj, "seq", axis=0, tiled=True),
        lax.all_gather(expand_proj, "seq", axis=0, tiled=True),
        lax.all_gather(out_proj, "seq", axis=1, tiled=True),
        lax.all_gather(shared_gate, "seq", axis=0, tiled=True),
        lax.all_gather(shared_up, "seq", axis=0, tiled=True),
        lax.all_gather(shared_down, "seq", axis=1, tiled=True),
        lax.all_gather(attn_gain, "seq", axis=0, tiled=True),
        lax.all_gather(latent_gain, "seq", axis=0, tiled=True),
        lax.all_gather(ffn_gain, "seq", axis=0, tiled=True),
    )
    query_full, latent_full, expand_full, outproj_full, sgate_full, sup_full, sdown_full = gathered[
        :7
    ]
    attention_norm_gain = gathered[7].astype(jnp.float32)
    latent_norm_gain = gathered[8].astype(jnp.float32)
    feedforward_gain = gathered[9].astype(jnp.float32)
    own_rows = inputs.astype(jnp.float32)
    own_normed = (own_rows * rms_inverse(own_rows) * attention_norm_gain).astype(jnp.bfloat16)
    own_latent = jnp.einsum(
        "bld,dk->blk", own_normed, latent_full, preferred_element_type=jnp.float32
    ).astype(jnp.bfloat16)
    group_inputs, group_cot, group_latent = (
        lax.all_gather(inputs, "head", axis=1, tiled=True),
        lax.all_gather(cotangent, "head", axis=1, tiled=True),
        lax.all_gather(own_latent, "head", axis=1, tiled=True),
    )
    input_rows = group_inputs.astype(jnp.float32).reshape(row_count, model_width)
    input_inverse = rms_inverse(input_rows)
    input_hat = input_rows * input_inverse
    normed = (input_hat * attention_norm_gain).astype(jnp.bfloat16)
    positions = seq_index * group_len + jnp.arange(group_len, dtype=jnp.int32)
    cosine_table, sine_table = rope_tables(positions, RDIM // 2)
    latent_rows = group_latent.astype(jnp.float32).reshape(row_count, RANK + RDIM)
    compressed = latent_rows[:, :RANK]
    comp_inverse = rms_inverse(compressed)
    comp_hat = compressed * comp_inverse
    comp_normed = (comp_hat * latent_norm_gain).astype(jnp.bfloat16)
    rope_key = rope_turn(
        latent_rows[:, RANK:].reshape(batch_size, group_len, RDIM), cosine_table, sine_table
    ).astype(jnp.bfloat16)
    query_lin = jnp.dot(normed, query_full, preferred_element_type=jnp.float32).reshape(
        batch_size, group_len, heads_here, QDIM
    )
    query_rows = jnp.concatenate(
        [
            query_lin[..., :HDIM],
            rope_turn(query_lin[..., HDIM:], cosine_table[:, None, :], sine_table[:, None, :]),
        ],
        axis=-1,
    ).astype(jnp.bfloat16)
    expanded = jnp.dot(comp_normed, expand_full, preferred_element_type=jnp.float32).reshape(
        batch_size, group_len, heads_here, 2 * HDIM
    )
    key_rows = jnp.concatenate(
        [
            expanded[..., :HDIM].astype(jnp.bfloat16),
            jnp.broadcast_to(rope_key[:, :, None, :], (batch_size, group_len, heads_here, RDIM)),
        ],
        axis=-1,
    )
    value_rows = expanded[..., HDIM:].astype(jnp.bfloat16)
    key_flat = key_rows.reshape(batch_size, group_len, heads_here * QDIM)
    value_flat = value_rows.reshape(batch_size, group_len, heads_here * HDIM)
    query_block = positions // BLOCK
    last_block = (seq_index * group_len + group_len - 1) // BLOCK

    def attend_piece(state_now, key_piece, value_piece, offset):
        piece_len = key_piece.shape[1]

        def attend_compute(state_in):
            acc_sum, row_max, row_sum = state_in
            key_blocks = key_piece.reshape(batch_size, piece_len, heads_here, QDIM)
            value_blocks = value_piece.reshape(batch_size, piece_len, heads_here, HDIM)
            scores = (
                jnp.einsum(
                    "bqhd,bkhd->bhqk", query_rows, key_blocks, preferred_element_type=jnp.float32
                )
                * score_scale
            )
            allowed = ((offset + jnp.arange(piece_len, dtype=jnp.int32)) // BLOCK)[
                None, :
            ] <= query_block[:, None]
            new_max = jnp.maximum(row_max, jnp.max(jnp.where(allowed, scores, NEG_LARGE), axis=-1))
            weights = jnp.where(allowed, jnp.exp(scores - new_max[..., None]), 0.0)
            rescale = jnp.exp(row_max - new_max)
            acc_sum = acc_sum * rescale[..., None] + jnp.einsum(
                "bhqk,bkhd->bhqd",
                weights.astype(jnp.bfloat16),
                value_blocks,
                preferred_element_type=jnp.float32,
            )
            return (acc_sum, new_max, row_sum * rescale + jnp.sum(weights, axis=-1))

        return lax.cond(
            offset // BLOCK > last_block, lambda state_in: state_in, attend_compute, state_now
        )

    start_state = (
        jnp.zeros((batch_size, heads_here, group_len, HDIM), jnp.float32),
        jnp.full((batch_size, heads_here, group_len), NEG_LARGE, jnp.float32),
        jnp.zeros((batch_size, heads_here, group_len), jnp.float32),
    )
    key_whole, value_whole = (
        lax.all_gather(key_flat, "seq", axis=1, tiled=True),
        lax.all_gather(value_flat, "seq", axis=1, tiled=True),
    )

    def scan_forward(state_now, piece_index):
        offset = piece_index * group_len
        key_piece = lax.dynamic_slice_in_dim(key_whole, offset, group_len, 1)
        value_piece = lax.dynamic_slice_in_dim(value_whole, offset, group_len, 1)
        return (attend_piece(state_now, key_piece, value_piece, offset), None)

    final_state, _ = lax.scan(scan_forward, start_state, jnp.arange(seq_count, dtype=jnp.int32))
    acc_sum, row_max, row_sum = final_state
    log_total = row_max + jnp.log(row_sum)
    attended_full = jnp.transpose(acc_sum / row_sum[..., None], (0, 2, 1, 3))
    attended = attended_full.astype(jnp.bfloat16).reshape(row_count, heads_here * HDIM)
    attn_part = jnp.dot(attended, outproj_full, preferred_element_type=jnp.float32)
    attention = lax.psum(attn_part.astype(jnp.bfloat16), "head").astype(jnp.float32)
    residual = input_rows + attention
    ffn_inverse = rms_inverse(residual)
    ffn_hat = residual * ffn_inverse
    ffn_in = (ffn_hat * feedforward_gain).astype(jnp.bfloat16)
    pair_count = head_count // 2
    experts_total = seq_count * pair_count
    most_rows = 4 * group_len * TOPK // (3 * experts_total)
    capacity = batch_size * most_rows
    slot_total = seq_count * capacity
    route_flat = routes.reshape(row_count * TOPK)
    gate_flat = gate_weights.reshape(row_count * TOPK)
    onehot = (route_flat[:, None] == jnp.arange(experts_total, dtype=jnp.int32)[None, :]).astype(
        jnp.int32
    )
    earlier = jnp.sum((jnp.cumsum(onehot, axis=0) - onehot) * onehot, axis=1)
    held_here = route_flat % pair_count == head_index // 2
    slot_of = jnp.where(held_here, route_flat // pair_count * capacity + earlier, slot_total)
    token_of = jnp.arange(row_count * TOPK, dtype=jnp.int32) // TOPK
    slot_token = (
        jnp.full((slot_total,), row_count, jnp.int32).at[slot_of].set(token_of, mode="drop")
    )
    slot_gate = jnp.zeros((slot_total,), jnp.float32).at[slot_of].set(gate_flat, mode="drop")
    ffn_padded = jnp.concatenate([ffn_in, jnp.zeros((1, model_width), jnp.bfloat16)], axis=0)
    cot_rows = group_cot.reshape(row_count, model_width)
    cot_padded = jnp.concatenate([cot_rows, jnp.zeros((1, model_width), jnp.bfloat16)], axis=0)
    send_rows = ffn_padded[slot_token].reshape(seq_count, capacity, model_width)
    send_grads = (
        (slot_gate[:, None] * cot_padded[slot_token].astype(jnp.float32))
        .astype(jnp.bfloat16)
        .reshape(seq_count, capacity, model_width)
    )
    got_rows, got_grads = (
        lax.all_to_all(send_rows, "seq", split_axis=0, concat_axis=0, tiled=True),
        lax.all_to_all(send_grads, "seq", split_axis=0, concat_axis=0, tiled=True),
    )
    expert_input_rows = got_rows.reshape(slot_total, model_width)
    egate_mat = expert_gate[0]
    expert_up_matrix = expert_up_weight[0]
    edown_mat = expert_down[0]
    expert_pre = jnp.dot(expert_input_rows, egate_mat, preferred_element_type=jnp.float32)
    expert_up_product = jnp.dot(
        expert_input_rows, expert_up_matrix, preferred_element_type=jnp.float32
    )
    expert_silu, expert_slope = silu_parts(expert_pre)
    expert_act = (expert_silu * expert_up_product).astype(jnp.bfloat16)
    expert_part = jnp.dot(expert_act, edown_mat, preferred_element_type=jnp.float32)
    returned = lax.all_to_all(
        expert_part.reshape(seq_count, capacity, model_width).astype(jnp.bfloat16),
        "seq",
        split_axis=0,
        concat_axis=0,
        tiled=True,
    ).astype(jnp.float32)
    routed = (
        jnp.zeros((row_count + 1, model_width), jnp.float32)
        .at[slot_token]
        .add(slot_gate[:, None] * returned.reshape(slot_total, model_width))[:row_count]
    )
    shared_pre = jnp.dot(ffn_in, sgate_full, preferred_element_type=jnp.float32)
    shared_upp = jnp.dot(ffn_in, sup_full, preferred_element_type=jnp.float32)
    shared_silu, shared_slope = silu_parts(shared_pre)
    shared_act = (shared_silu * shared_upp).astype(jnp.bfloat16)
    ffn_part = jnp.dot(shared_act, sdown_full, preferred_element_type=jnp.float32) + routed
    ffn_own = lax.psum_scatter(
        ffn_part.reshape(batch_size, group_len, model_width).astype(jnp.bfloat16),
        "head",
        scatter_dimension=1,
        tiled=True,
    ).astype(jnp.float32)
    residual_own = lax.dynamic_slice_in_dim(
        residual.reshape(batch_size, group_len, model_width), head_index * local_len, local_len, 1
    )
    output = (residual_own + ffn_own).astype(jnp.bfloat16)
    expert_gin = got_grads.reshape(slot_total, model_width)
    grad_eact = jnp.einsum("rd,fd->rf", expert_gin, edown_mat, preferred_element_type=jnp.float32)
    grad_epre = (grad_eact * expert_up_product * expert_slope).astype(jnp.bfloat16)
    expert_up_product_gradient = (grad_eact * expert_silu).astype(jnp.bfloat16)
    exdown_grad = jnp.einsum(
        "rf,rd->fd", expert_act, expert_gin, preferred_element_type=jnp.float32
    )[None]
    exgate_grad = jnp.einsum(
        "rd,rf->df", expert_input_rows, grad_epre, preferred_element_type=jnp.float32
    )[None]
    exup_grad = jnp.einsum(
        "rd,rf->df",
        expert_input_rows,
        expert_up_product_gradient,
        preferred_element_type=jnp.float32,
    )[None]
    grad_ein = jnp.einsum(
        "bv,mv->bm", grad_epre, egate_mat, preferred_element_type=jnp.float32
    ) + jnp.einsum(
        "bv,mv->bm",
        expert_up_product_gradient,
        expert_up_matrix,
        preferred_element_type=jnp.float32,
    )
    grad_back = lax.all_to_all(
        grad_ein.reshape(seq_count, capacity, model_width).astype(jnp.bfloat16),
        "seq",
        split_axis=0,
        concat_axis=0,
        tiled=True,
    ).astype(jnp.float32)
    grad_sact = jnp.einsum("td,sd->ts", cot_rows, sdown_full, preferred_element_type=jnp.float32)
    grad_spre = (grad_sact * shared_upp * shared_slope).astype(jnp.bfloat16)
    grad_supp = (grad_sact * shared_silu).astype(jnp.bfloat16)
    shdown_term = jnp.einsum("ts,td->sd", shared_act, cot_rows, preferred_element_type=jnp.float32)
    shgate_term = jnp.einsum("td,ts->ds", ffn_in, grad_spre, preferred_element_type=jnp.float32)
    shup_term = jnp.einsum("td,ts->ds", ffn_in, grad_supp, preferred_element_type=jnp.float32)
    grad_ffn_part = (
        jnp.einsum("ts,ds->td", grad_spre, sgate_full, preferred_element_type=jnp.float32)
        + jnp.einsum("ts,ds->td", grad_supp, sup_full, preferred_element_type=jnp.float32)
        + jnp.zeros((row_count + 1, model_width), jnp.float32)
        .at[slot_token]
        .add(grad_back.reshape(slot_total, model_width))[:row_count]
    )
    grad_ffn = lax.psum(grad_ffn_part.astype(jnp.bfloat16), "head").astype(jnp.float32)
    grad_norm_two, ffngain_term = norm_back(grad_ffn, ffn_hat, ffn_inverse, feedforward_gain)
    grad_residual = cot_rows.astype(jnp.float32) + grad_norm_two
    grad_attention = grad_residual.astype(jnp.bfloat16)
    outproj_term = jnp.einsum(
        "tj,td->jd", attended, grad_attention, preferred_element_type=jnp.float32
    )
    grad_attended = (
        jnp.einsum("td,jd->tj", grad_attention, outproj_full, preferred_element_type=jnp.float32)
        .astype(jnp.bfloat16)
        .reshape(batch_size, group_len, heads_here, HDIM)
    )
    row_delta = jnp.transpose(
        jnp.sum(grad_attended.astype(jnp.float32) * attended_full, axis=-1), (0, 2, 1)
    )
    query_zero = jnp.zeros((batch_size, group_len, heads_here, QDIM), jnp.float32)

    def back_piece(grad_query, key_piece, value_piece, offset):
        piece_len = key_piece.shape[1]

        def back_compute(grad_in):
            key_pos = offset + jnp.arange(piece_len, dtype=jnp.int32)
            grad_scores, probs, key_blocks = score_grads(
                query_rows,
                grad_attended,
                log_total,
                row_delta,
                key_piece,
                value_piece,
                positions,
                key_pos,
                score_scale,
            )
            grad_in = (
                grad_in
                + jnp.einsum(
                    "bhqk,bkhd->bqhd", grad_scores, key_blocks, preferred_element_type=jnp.float32
                )
                * score_scale
            )
            grad_keys = (
                jnp.einsum(
                    "bhqk,bqhd->bkhd", grad_scores, query_rows, preferred_element_type=jnp.float32
                )
                * score_scale
            )
            grad_values = jnp.einsum(
                "bhqk,bqhd->bkhd",
                probs.astype(jnp.bfloat16),
                grad_attended,
                preferred_element_type=jnp.float32,
            )
            return (
                grad_in,
                grad_keys.reshape(batch_size, piece_len, heads_here * QDIM),
                grad_values.reshape(batch_size, piece_len, heads_here * HDIM),
            )

        def skip_piece(grad_in):
            return (
                grad_in,
                jnp.zeros((batch_size, piece_len, heads_here * QDIM), jnp.float32),
                jnp.zeros((batch_size, piece_len, heads_here * HDIM), jnp.float32),
            )

        return lax.cond(offset // BLOCK > last_block, skip_piece, back_compute, grad_query)

    def scan_backward(grad_query, piece_index):
        offset = piece_index * group_len
        key_piece = lax.dynamic_slice_in_dim(key_whole, offset, group_len, 1)
        value_piece = lax.dynamic_slice_in_dim(value_whole, offset, group_len, 1)
        grad_query, grad_keys, grad_values = back_piece(grad_query, key_piece, value_piece, offset)
        return (grad_query, (grad_keys, grad_values))

    grad_query, (key_terms, value_terms) = lax.scan(
        scan_backward, query_zero, jnp.arange(seq_count, dtype=jnp.int32)
    )
    key_grad, value_grad = (
        lax.psum_scatter(
            key_terms.astype(jnp.bfloat16), "seq", scatter_dimension=0, tiled=True
        ).astype(jnp.float32),
        lax.psum_scatter(
            value_terms.astype(jnp.bfloat16), "seq", scatter_dimension=0, tiled=True
        ).astype(jnp.float32),
    )
    key_grad = key_grad.reshape(batch_size, group_len, heads_here, QDIM)
    value_grad = value_grad.reshape(batch_size, group_len, heads_here, HDIM)
    grad_expanded = (
        jnp.concatenate([key_grad[..., :HDIM], value_grad], axis=-1)
        .astype(jnp.bfloat16)
        .reshape(row_count, heads_here * 2 * HDIM)
    )
    grad_rope = rope_back(jnp.sum(key_grad[..., HDIM:], axis=2), cosine_table, sine_table).reshape(
        row_count, RDIM
    )
    expand_term = jnp.einsum(
        "tr,tk->rk", comp_normed, grad_expanded, preferred_element_type=jnp.float32
    )
    grad_comp = jnp.einsum(
        "tk,rk->tr", grad_expanded, expand_full, preferred_element_type=jnp.float32
    )
    grad_qlin = (
        jnp.concatenate(
            [
                grad_query[..., :HDIM],
                rope_back(grad_query[..., HDIM:], cosine_table[:, None, :], sine_table[:, None, :]),
            ],
            axis=-1,
        )
        .astype(jnp.bfloat16)
        .reshape(row_count, heads_here * QDIM)
    )
    query_term = jnp.einsum("td,tk->dk", normed, grad_qlin, preferred_element_type=jnp.float32)
    grad_normed_q = jnp.einsum(
        "tk,dk->td", grad_qlin, query_full, preferred_element_type=jnp.float32
    )
    grad_normed_q, grad_comp, grad_rope = (
        lax.psum(grad_normed_q.astype(jnp.bfloat16), "head").astype(jnp.float32),
        lax.psum(grad_comp.astype(jnp.bfloat16), "head").astype(jnp.float32),
        lax.psum(grad_rope.astype(jnp.bfloat16), "head").astype(jnp.float32),
    )
    grad_compressed, latgain_term = norm_back(grad_comp, comp_hat, comp_inverse, latent_norm_gain)
    grad_latent = jnp.concatenate([grad_compressed, grad_rope], axis=-1).astype(jnp.bfloat16)
    latent_term = jnp.einsum("td,tk->dk", normed, grad_latent, preferred_element_type=jnp.float32)
    grad_normed = grad_normed_q + jnp.einsum(
        "tk,dk->td", grad_latent, latent_full, preferred_element_type=jnp.float32
    )
    grad_input, attngain_term = norm_back(
        grad_normed, input_hat, input_inverse, attention_norm_gain
    )
    grad_input = grad_input + grad_residual
    inputs_grad = lax.dynamic_slice_in_dim(
        grad_input.reshape(batch_size, group_len, model_width), head_index * local_len, local_len, 1
    ).astype(jnp.bfloat16)
    summed = (
        lax.psum_scatter(
            query_term.astype(jnp.bfloat16), "seq", scatter_dimension=0, tiled=True
        ).astype(jnp.float32),
        lax.psum_scatter(
            latent_term.astype(jnp.bfloat16), "seq", scatter_dimension=0, tiled=True
        ).astype(jnp.float32),
        lax.psum_scatter(
            expand_term.astype(jnp.bfloat16), "seq", scatter_dimension=0, tiled=True
        ).astype(jnp.float32),
        lax.psum_scatter(
            outproj_term.astype(jnp.bfloat16), "seq", scatter_dimension=1, tiled=True
        ).astype(jnp.float32),
        lax.psum_scatter(
            shgate_term.astype(jnp.bfloat16), "seq", scatter_dimension=0, tiled=True
        ).astype(jnp.float32),
        lax.psum_scatter(
            shup_term.astype(jnp.bfloat16), "seq", scatter_dimension=0, tiled=True
        ).astype(jnp.float32),
        lax.psum_scatter(
            shdown_term.astype(jnp.bfloat16), "seq", scatter_dimension=1, tiled=True
        ).astype(jnp.float32),
        lax.psum_scatter(
            attngain_term.astype(jnp.bfloat16), "seq", scatter_dimension=0, tiled=True
        ).astype(jnp.float32),
        lax.psum_scatter(
            latgain_term.astype(jnp.bfloat16), "seq", scatter_dimension=0, tiled=True
        ).astype(jnp.float32),
        lax.psum_scatter(
            ffngain_term.astype(jnp.bfloat16), "seq", scatter_dimension=0, tiled=True
        ).astype(jnp.float32),
    )
    return (
        output,
        inputs_grad,
        summed[0],
        summed[1],
        summed[2],
        summed[3],
        summed[4],
        summed[5],
        summed[6],
        exgate_grad,
        exup_grad,
        exdown_grad,
        summed[7],
        summed[8],
        summed[9],
    )


def solution(mesh):
    placed = (
        P(None, ("seq", "head"), None),
        P(None, ("seq", "head"), None),
        P(None, "seq", None),
        P(None, "seq", None),
        P("seq"),
        P("seq"),
        P("seq"),
        P("seq", "head"),
        P("seq", None),
        P("seq", "head"),
        P("head", "seq"),
        P("seq", "head"),
        P("seq", "head"),
        P("head", "seq"),
        P(("seq", "head"), None, None),
        P(("seq", "head"), None, None),
        P(("seq", "head"), None, None),
    )
    return jax.shard_map(
        local,
        mesh=mesh,
        in_specs=placed,
        out_specs=(
            P(None, ("seq", "head"), None),
            P(None, ("seq", "head"), None),
            P("seq", "head"),
            P("seq", None),
            P("seq", "head"),
            P("head", "seq"),
            P("seq", "head"),
            P("seq", "head"),
            P("head", "seq"),
            P(("seq", "head"), None, None),
            P(("seq", "head"), None, None),
            P(("seq", "head"), None, None),
            P("seq"),
            P("seq"),
            P("seq"),
        ),
        check_vma=False,
    )
```

profile of v0, /device:TPU:0, one launch (start us, length us, event | category | flops | bytes accessed | tf_op | source)
XLA Modules:
  0.0 2010.0 jit_solution(2596367438499178434)
XLA Ops:
  109.2 35.1 %all-gather.22.cloned.1.call-done = bf16[2048,768]{1,0:T(8,128)(2,1)} async-done(((bf16[256,768]{1,0:T(8,128)(2,1)}), bf16[2048,768]{1,0:T(8,128)(2,1)}) %all-gather.22.cloned.1.call-update) | async-done | bytes 3145744 | tf_op jit(solution)/shard_map/all_gather | solution.py:108
  154.5 38.5 %all-gather.24.cloned.1.call-done = bf16[2,2048,512]{1,2,0:T(8,128)(2,1)} async-done(((bf16[2,256,512]{1,2,0:T(8,128)(2,1)}), bf16[2,2048,512]{1,2,0:T(8,128)(2,1)}) %all-gather.24.cloned.1.call-update) | async-done | bytes 4194320 | tf_op jit(solution)/shard_map/all_gather | solution.py:213
  193.0 65.5 %all-gather.20.cloned.1.call-done = bf16[2,2048,768]{1,2,0:T(8,128)(2,1)} async-done(((bf16[2,256,768]{1,2,0:T(8,128)(2,1)}), bf16[2,2048,768]{1,2,0:T(8,128)(2,1)}) %all-gather.20.cloned.1.call-update) | async-done | bytes 6291472 | tf_op jit(solution)/shard_map/all_gather | solution.py:212
  294.1 50.5 %all-gather.1 = bf16[8,1,256]{2,1,0:T(2,128)(2,1)S(1)} all-gather(bf16[1,1,256]{2,1,0:T(2,128)(2,1)S(1)} %reshape.707), channel_id=1, replica_groups=mesh['head'=4,'seq'=8] {'seq'}, dimensions={0}, use_global_device_ids=true | all-gather | bytes 4608 | tf_op jit(solution)/shard_map/all_gather | solution.py:117
  362.8 41.5 %all-reduce.12.cloned.1.call-done = bf16[512,2048]{1,0:T(8,128)(2,1)} async-done(((bf16[512,2048]{1,0:T(8,128)(2,1)}), bf16[512,2048]{1,0:T(8,128)(2,1)}) %all-reduce.12.cloned.1.call-update) | async-done | bytes 2097168 | tf_op jit(solution)/shard_map/psum | solution.py:228
  448.0 25.7 %all-gather.34.cloned.1.call-done = bf16[2,256,2048]{2,1,0:T(8,128)(2,1)} async-done(((bf16[2,64,2048]{2,1,0:T(8,128)(2,1)}), bf16[2,256,2048]{2,1,0:T(8,128)(2,1)}) %all-gather.34.cloned.1.call-update) | async-done | bytes 2097168 | tf_op jit(solution)/shard_map/all_gather | solution.py:132
  503.2 115.8 %all-to-all-done = bf16[8,256,2048]{2,1,0:T(8,128)(2,1)} async-done(((bf16[8,256,2048]{2,1,0:T(8,128)(2,1)}), bf16[8,256,2048]{2,1,0:T(8,128)(2,1)}, u32[]{:S(2)}, u32[]{:S(2)}) %all-to-all-start) | async-done | bytes 8388640 | tf_op jit(solution)/shard_map/all_to_all | solution.py:261
  645.9 185.1 %all-to-all-done.2 = bf16[8,256,2048]{2,1,0:T(8,128)(2,1)} async-done(((bf16[8,256,2048]{2,1,0:T(8,128)(2,1)}), bf16[8,256,2048]{2,1,0:T(8,128)(2,1)}, u32[]{:S(2)}, u32[]{:S(2)}) %all-to-all-start.2) | async-done | bytes 8388640 | tf_op jit(solution)/shard_map/all_to_all | solution.py:262
  881.0 64.9 %all-gather.30.cloned.1.call-done = bf16[2048,704]{0,1:T(8,128)(2,1)} async-done(((bf16[256,704]{0,1:T(8,128)(2,1)}), bf16[2048,704]{0,1:T(8,128)(2,1)}) %all-gather.30.cloned.1.call-update) | async-done | bytes 2883600 | tf_op jit(solution)/shard_map/all_gather | solution.py:113
  951.1 111.1 %all-gather.32.cloned.1.call-done = bf16[704,2048]{1,0:T(8,128)(2,1)} async-done(((bf16[704,256]{1,0:T(8,128)(2,1)}), bf16[704,2048]{1,0:T(8,128)(2,1)}) %all-gather.32.cloned.1.call-update) | async-done | bytes 2883600 | tf_op jit(solution)/shard_map/all_gather | solution.py:114
  1073.7 30.5 %all-to-all-done.3 = bf16[8,256,2048]{2,1,0:T(8,128)(2,1)} async-done(((bf16[8,256,2048]{2,1,0:T(8,128)(2,1)}), bf16[8,256,2048]{2,1,0:T(8,128)(2,1)}, u32[]{:S(2)}, u32[]{:S(2)}) %all-to-all-start.3) | async-done | bytes 8388640 | tf_op jit(solution)/shard_map/all_to_all | solution.py:326
  1104.2 30.0 %scatter_custom_fusion.3 = f32[513,2048]{1,0:T(8,128)} fusion(s32[2048]{0:T(1024)} %get-tuple-element.753, bf16[2048,2048]{1,0:T(8,128)(2,1)} %bitcast.62, f32[]{:T(128)} %constant.317.clone.1), kind=kCustom, calls=%fused_computation.59 | custom fusion | flops 8388608 | bytes 12591616 | tf_op jit(solution)/shard_map/scatter-add | solution.py:344
  1142.3 67.4 %all-reduce.14.cloned.1.call-done = bf16[512,2048]{1,0:T(8,128)(2,1)} async-done(((bf16[512,2048]{1,0:T(8,128)(2,1)}), bf16[512,2048]{1,0:T(8,128)(2,1)}) %all-reduce.14.cloned.1.call-update) | async-done | bytes 2097168 | tf_op jit(solution)/shard_map/psum | solution.py:346
  1231.4 33.4 %while.38 = (s32[]{:T(128)}, f32[2,256,4,192]{1,3,2,0:T(8,128)}, bf16[8,2,256,768]{2,3,1,0:T(8,128)(2,1)}, bf16[8,2,256,512]{2,3,1,0:T(8,128)(2,1)}, s32[8]{0:T(...) while((s32[]{:T(128)}, f32[2,256,4,192]{1,3,2,0:T(8,128)}, ...), condition=%wide.region_25.26_spmd.clone, body=%wide.region_22.25_spmd.clone.sunk | while | flops 877731840 | bytes 39738964 | solution.py:420
  1281.7 58.7 %all-to-all-start.1 = ((bf16[8,256,2048]{2,1,0:T(8,128)(2,1)}), bf16[8,256,2048]{2,1,0:T(8,128)(2,1)}, u32[]{:S(2)}, u32[]{:S(2)}) async-start(bf16[8,256,2048]{2,1,0:T(8,128)(2,1)} %convolution_convert_fusion), calls=%async_computation.1 | async-start | bytes 16777216 | tf_op jit(solution)/shard_map/all_to_all | solution.py:275
  1359.0 31.8 %reduce-scatter.15.cloned.1.call-done = bf16[1,2,256,512]{2,3,1,0:T(8,128)(2,1)} async-done(((bf16[8,2,256,512]{2,3,1,0:T(8,128)(2,1)}), bf16[1,2,256,512]{2,3,1,0:T(8,128)(2,1)}) %reduce-scatter.15.cloned.1.call-update) | async-done | bytes 524304 | tf_op jit(solution)/shard_map/reduce_scatter | solution.py:427
  1392.9 193.5 %reduce-scatter.13.cloned.1.call-done = bf16[1,2,256,768]{2,3,1,0:T(8,128)(2,1)} async-done(((bf16[8,2,256,768]{2,3,1,0:T(8,128)(2,1)}), bf16[1,2,256,768]{2,3,1,0:T(8,128)(2,1)}) %reduce-scatter.13.cloned.1.call-update) | async-done | bytes 786448 | tf_op jit(solution)/shard_map/reduce_scatter | solution.py:424
  1602.2 30.5 %scatter_custom_fusion.2 = f32[513,2048]{1,0:T(8,128)} fusion(s32[2048]{0:T(1024)} %get-tuple-element.753, bf16[2048,2048]{1,0:T(8,128)(2,1)} %bitcast.60, f32[2048]{0:T(1024)S(1)} %copy-done.37, f32[]{:T(128)} %constant.317.clone.1), kind=kCustom, calls=%fused_computation.64 | custom fusion | flops 12582912 | bytes 12599808 | tf_op jit(solution)/shard_map/scatter-add | solution.py:285
  1652.9 35.1 %reduce-scatter.27.cloned.1.call-done = bf16[256,704]{0,1:T(8,128)(2,1)} async-done(((bf16[2048,704]{0,1:T(8,128)(2,1)}), bf16[256,704]{0,1:T(8,128)(2,1)}) %reduce-scatter.27.cloned.1.call-update) | async-done | bytes 360464 | tf_op jit(solution)/shard_map/reduce_scatter | solution.py:496
  1689.9 38.5 %reduce-scatter.29.cloned.1.call-done = bf16[704,256]{1,0:T(8,128)(2,1)} async-done(((bf16[704,2048]{1,0:T(8,128)(2,1)}), bf16[704,256]{1,0:T(8,128)(2,1)}) %reduce-scatter.29.cloned.1.call-update) | async-done | bytes 360464 | tf_op jit(solution)/shard_map/reduce_scatter | solution.py:499
  1744.7 68.0 %all-reduce.16.cloned.1.call-done = (bf16[512,2048]{1,0:T(8,128)(2,1)}, bf16[512,64]{1,0:T(8,128)(2,1)}, bf16[512,512]{1,0:T(8,128)(2,1)}) async-done(((bf16[512,2048]{1,0:T(8,128)(2,1)}, bf16[512,64]{1,0:T(8,128)(2,1)}, bf16[512,512]{1,0:T(8,128)(2,1)}), (bf16[512,2048]{1,0:T(8,128)(2,1)}, bf16[512,64]{1,0:T(8,128)(2,1)}, bf16[512,512]{1,0:T(8,128)(2,1)})) %all-reduce.16.cloned.1.call-update) | async-done | bytes 2686992 | tf_op jit(solution)/shard_map/psum | solution.py:463
  1853.0 36.0 %reduce-scatter.23.cloned.1.call-done = bf16[512,256]{1,0:T(8,128)(2,1)} async-done(((bf16[512,2048]{1,0:T(8,128)(2,1)}), bf16[512,256]{1,0:T(8,128)(2,1)}) %reduce-scatter.23.cloned.1.call-update) | async-done | bytes 262160 | tf_op jit(solution)/shard_map/reduce_scatter | solution.py:490
  1890.8 39.5 %reduce-scatter.17.cloned.1.call-done = bf16[256,768]{1,0:T(8,128)(2,1)} async-done(((bf16[2048,768]{1,0:T(8,128)(2,1)}), bf16[256,768]{1,0:T(8,128)(2,1)}) %reduce-scatter.17.cloned.1.call-update) | async-done | bytes 393232 | tf_op jit(solution)/shard_map/reduce_scatter | solution.py:481
  1932.2 32.0 %reduce-scatter.21.cloned.1.call-done = bf16[64,1024]{1,0:T(8,128)(2,1)} async-done(((bf16[512,1024]{1,0:T(8,128)(2,1)}), bf16[64,1024]{1,0:T(8,128)(2,1)}) %reduce-scatter.21.cloned.1.call-update) | async-done | bytes 131088 | tf_op jit(solution)/shard_map/reduce_scatter | solution.py:487
  (454 shorter events, 590.5 us)
Async XLA Ops:
  8.7 95.8 %all-gather.14.cloned.1.call-start = ((), (), s32[]{:S(2)}) async-start(), calls=%async_computation.14 | async-start | bytes 2621440 | tf_op jit(solution)/shard_map/all_gather | solution.py:131
  9.4 134.9 %all-gather.22.cloned.1.call-start = ((), (), s32[]{:S(2)}) async-start(), calls=%async_computation.18 | async-start | bytes 3538944 | tf_op jit(solution)/shard_map/all_gather | solution.py:108
  10.0 183.0 %all-gather.24.cloned.1.call-start = ((), (), s32[]{:S(2)}) async-start(), calls=%async_computation.19 | async-start | bytes 4718592 | tf_op jit(solution)/shard_map/all_gather | solution.py:213
  78.2 180.2 %all-gather.20.cloned.1.call-start = ((), (), s32[]{:S(2)}) async-start(), calls=%async_computation.17 | async-start | bytes 7077888 | tf_op jit(solution)/shard_map/all_gather | solution.py:212
  88.7 200.4 %all-gather.26.cloned.1.call-start = ((), (), s32[]{:S(2)}) async-start(), calls=%async_computation.20 | async-start | bytes 2359296 | tf_op jit(solution)/shard_map/all_gather | solution.py:111
  89.5 314.8 %all-reduce.12.cloned.1.call-start = ((), (), s32[]{:S(2)}) async-start(), calls=%async_computation.21 | async-start | bytes 4194304 | tf_op jit(solution)/shard_map/psum | solution.py:228
  430.0 189.0 %all-to-all-start = ((bf16[8,256,2048]{2,1,0:T(8,128)(2,1)}), bf16[8,256,2048]{2,1,0:T(8,128)(2,1)}, u32[]{:S(2)}, u32[]{:S(2)}) async-start(bf16[8,256,2048]{2,1,0:T(8,128)(2,1)} %bitcast.255), calls=%async_computation | async-start | bytes 16777216 | tf_op jit(solution)/shard_map/all_to_all | solution.py:261
  619.0 212.0 %all-to-all-start.2 = ((bf16[8,256,2048]{2,1,0:T(8,128)(2,1)}), bf16[8,256,2048]{2,1,0:T(8,128)(2,1)}, u32[]{:S(2)}, u32[]{:S(2)}) async-start(bf16[8,256,2048]{2,1,0:T(8,128)(2,1)} %fusion.24), calls=%async_computation.3 | async-start | bytes 16777216 | tf_op jit(solution)/shard_map/all_to_all | solution.py:262
  624.0 251.8 %all-gather.28.cloned.1.call-start = ((), (), s32[]{:S(2)}) async-start(), calls=%async_computation.22 | async-start | bytes 3244032 | tf_op jit(solution)/shard_map/all_gather | solution.py:112
  868.9 235.2 %all-to-all-start.3 = ((bf16[8,256,2048]{2,1,0:T(8,128)(2,1)}), bf16[8,256,2048]{2,1,0:T(8,128)(2,1)}, u32[]{:S(2)}, u32[]{:S(2)}) async-start(bf16[8,256,2048]{2,1,0:T(8,128)(2,1)} %bitcast.260), calls=%async_computation.4 | async-start | bytes 16777216 | tf_op jit(solution)/shard_map/all_to_all | solution.py:326
  874.7 187.6 %all-gather.32.cloned.1.call-start = ((), (), s32[]{:S(2)}) async-start(), calls=%async_computation.24 | async-start | bytes 3244032 | tf_op jit(solution)/shard_map/all_gather | solution.py:114
  875.3 334.4 %all-reduce.14.cloned.1.call-start = ((), (), s32[]{:S(2)}) async-start(), calls=%async_computation.27 | async-start | bytes 4194304 | tf_op jit(solution)/shard_map/psum | solution.py:346
  1142.0 248.8 %reduce-scatter.15.cloned.1.call-start = ((), (), s32[]{:S(2)}) async-start(), calls=%async_computation.29 | async-start | bytes 4718592 | tf_op jit(solution)/shard_map/reduce_scatter | solution.py:427
  1264.9 321.5 %reduce-scatter.13.cloned.1.call-start = ((), (), s32[]{:S(2)}) async-start(), calls=%async_computation.28 | async-start | bytes 7077888 | tf_op jit(solution)/shard_map/reduce_scatter | solution.py:424
  1265.4 385.6 %reduce-scatter.25.cloned.1.call-start = ((), (), s32[]{:S(2)}) async-start(), calls=%async_computation.34 | async-start | bytes 3244032 | tf_op jit(solution)/shard_map/reduce_scatter | solution.py:493
  1281.7 320.5 %all-to-all-start.1 = ((bf16[8,256,2048]{2,1,0:T(8,128)(2,1)}), bf16[8,256,2048]{2,1,0:T(8,128)(2,1)}, u32[]{:S(2)}, u32[]{:S(2)}) async-start(bf16[8,256,2048]{2,1,0:T(8,128)(2,1)} %convolution_convert_fusion), calls=%async_computation.1 | async-start | bytes 16777216 | tf_op jit(solution)/shard_map/all_to_all | solution.py:275
  1340.4 347.6 %reduce-scatter.27.cloned.1.call-start = ((), (), s32[]{:S(2)}) async-start(), calls=%async_computation.35 | async-start | bytes 3244032 | tf_op jit(solution)/shard_map/reduce_scatter | solution.py:496
  1345.5 382.8 %reduce-scatter.29.cloned.1.call-start = ((), (), s32[]{:S(2)}) async-start(), calls=%async_computation.36 | async-start | bytes 3244032 | tf_op jit(solution)/shard_map/reduce_scatter | solution.py:499
  1350.7 462.0 %all-reduce.16.cloned.1.call-start = ((), (), s32[]{:S(2)}) async-start(), calls=%async_computation.37 | async-start | bytes 5505024 | tf_op jit(solution)/shard_map/psum | solution.py:463
  1596.4 254.3 %reduce-scatter.11.cloned.1.call-start = ((), (), s32[]{:S(2)}) async-start(), calls=%async_computation.25 | async-start | bytes 2621440 | tf_op jit(solution)/shard_map/reduce_scatter | solution.py:292
  1639.3 249.7 %reduce-scatter.23.cloned.1.call-start = ((), (), s32[]{:S(2)}) async-start(), calls=%async_computation.33 | async-start | bytes 2359296 | tf_op jit(solution)/shard_map/reduce_scatter | solution.py:490
  1644.3 286.0 %reduce-scatter.17.cloned.1.call-start = ((), (), s32[]{:S(2)}) async-start(), calls=%async_computation.30 | async-start | bytes 3538944 | tf_op jit(solution)/shard_map/reduce_scatter | solution.py:481
  1649.6 314.6 %reduce-scatter.21.cloned.1.call-start = ((), (), s32[]{:S(2)}) async-start(), calls=%async_computation.32 | async-start | bytes 1179648 | tf_op jit(solution)/shard_map/reduce_scatter | solution.py:487
  1733.6 267.5 %reduce-scatter.19.cloned.1.call-start = ((), (), s32[]{:S(2)}) async-start(), calls=%async_computation.31 | async-start | bytes 2654208 | tf_op jit(solution)/shard_map/reduce_scatter | solution.py:484
  (61 other events, 2014.8 us)
Sparse Core Ops, SparseCore 0:
  9.6 35.7 all-gather.15
  47.0 20.6 all-gather.17
  69.5 34.9 all-gather.13
  106.0 38.2 all-gather.21
  146.3 46.6 all-gather.23
  195.0 63.3 all-gather.19
  260.1 29.0 all-gather.25
  293.5 110.7 all-reduce.11
  438.0 35.6 all-gather.33
  626.2 69.6 all-gather.27
  876.5 69.3 all-gather.29
  947.4 114.7 all-gather.31
  1142.1 67.5 all-reduce.13
  1265.0 125.7 reduce-scatter.14
  1392.9 193.3 reduce-scatter.12
  1589.1 57.7 reduce-scatter.24
  1649.7 38.2 reduce-scatter.26
  1690.1 38.1 reduce-scatter.28
  1732.3 80.3 all-reduce.15
  1815.5 35.1 reduce-scatter.10
  1853.1 35.8 reduce-scatter.22
  1891.4 38.8 reduce-scatter.16
  1932.7 31.5 reduce-scatter.20
  1966.6 34.5 reduce-scatter.18
where the time goes:
time: 2020 us; the launch traced here: 2010 us
  waiting for transfers between devices  1320 us (65%)
  matrix products  205 us (10%)
  local copies, waits for them, and re-layouts  142 us (7%)
  other arithmetic  135 us (7%)
  blocking collectives  104 us (5%)
  starting transfers between devices  76.8 us (4%)
    reduce_scatter x1, waiting for transfers between devices, local(): lax.psum_scatter(key_terms.astype(jnp.bfloat16), 'seq', scatter_dimension...  193 us
    all_to_all x1, waiting for transfers between devices, local(): lax.all_to_all(send_grads, 'seq', split_axis=0, concat_axis=0, tiled=True)  185 us
    all_to_all x1, waiting for transfers between devices, local(): lax.all_to_all(send_rows, 'seq', split_axis=0, concat_axis=0, tiled=True)  116 us
    all_gather x1, waiting for transfers between devices, local(): lax.all_gather(shared_down, 'seq', axis=1, tiled=True)  111 us
    psum x1, waiting for transfers between devices, local(): lax.psum(grad_normed_q.astype(jnp.bfloat16), 'head').astype(jnp.float32)  68 us
    psum x1, waiting for transfers between devices, local(): lax.psum(grad_ffn_part.astype(jnp.bfloat16), 'head').astype(jnp.float32)  67.4 us
    all_gather x1, waiting for transfers between devices, local(): lax.all_gather(key_flat, 'seq', axis=1, tiled=True)  65.5 us
    all_gather x1, waiting for transfers between devices, local(): lax.all_gather(shared_up, 'seq', axis=0, tiled=True)  64.9 us
  transfers between devices with their start and end apart: 28, of which 26 were waited for; matrix products, arithmetic and copies ran while one was open for 18% of the time, Pallas kernels for 0%

commit v1 on v0

v1 whole, which is shorter than its diff:
```python
import functools

import jax
import jax.numpy as jnp
from jax import lax
from jax.experimental import pallas as pl
from jax.experimental.pallas import tpu as pltpu
from jax.sharding import PartitionSpec as P

HDIM = 128
RDIM = 64
RANK = 512
TOPK = 6
BLOCK = 256
QDIM = 192
HALF = RDIM // 2
EPSILON = 1e-06
ROPE_BASE = 10000.0
NEG_LARGE = -1e30
LOG2E = 1.4426950408889634
SCALE = QDIM ** (-0.5)
F32 = jnp.float32
BF16 = jnp.bfloat16
MIB = 1024 * 1024


def dot(a, b):
    return lax.dot_general(a, b, (((1,), (0,)), ((), ())), preferred_element_type=F32)


def dot_nt(a, b):
    return lax.dot_general(a, b, (((1,), (1,)), ((), ())), preferred_element_type=F32)


def dot_tn(a, b):
    return lax.dot_general(a, b, (((0,), (0,)), ((), ())), preferred_element_type=F32)


def rms_inverse(values):
    return lax.rsqrt(jnp.mean(values * values, axis=-1, keepdims=True) + EPSILON)


def rope_tables(positions):
    frequency = ROPE_BASE ** (-jnp.arange(HALF, dtype=F32) / HALF)
    angles = positions.astype(F32)[:, None] * frequency[None, :]
    return (jnp.cos(angles), jnp.sin(angles))


def norm_back(grad_normed, hat_rows, inverse, gain_vec):
    scaled = grad_normed * gain_vec
    gain_term = jnp.sum(grad_normed * hat_rows, axis=(0, 1))
    grad_rows = inverse * (scaled - hat_rows * jnp.mean(scaled * hat_rows, axis=-1, keepdims=True))
    return (grad_rows, gain_term)


def swap(value, axis, mask):
    size = lax.axis_size(axis)
    return lax.ppermute(value, axis, [(i, i ^ mask) for i in range(size)])


def after(value, *others):
    seen = sum(other[(0,) * other.ndim].astype(F32) for other in others)
    return jnp.where(seen == seen, value, jnp.zeros((), value.dtype))


def bits_of(size):
    return [1 << i for i in range(size.bit_length() - 1)]


def depth():
    return lax.axis_size("seq") // 2


def plane_order(flip):
    bits = bits_of(lax.axis_size("head"))
    order = [0]
    for bit in bits[::-1] if flip else bits:
        order = order + [i | bit for i in order]
    return order


def spread_line(value):
    held = [value[None]]
    for bit in bits_of(depth())[::-1]:
        last = held[-1]
        got = swap(last, "seq", 2 * bit)
        held.append(jnp.stack([last, got], axis=1).reshape((-1,) + value.shape))
    return held


def collect_line(value):
    for bit in bits_of(depth()):
        pairs = value.reshape((-1, 2) + value.shape[1:])
        value = pairs[:, 0].astype(F32) + swap(pairs[:, 1], "seq", 2 * bit).astype(F32)
        if value.shape[0] > 1:
            value = value.astype(BF16)
    return value[0]


def spread_plane(value, flip):
    bits = bits_of(lax.axis_size("head"))
    value = value[None]
    for bit in bits[::-1] if flip else bits:
        value = jnp.concatenate([value, swap(value, "head", bit)], axis=0)
    return value


def collect_plane(value, flip):
    bits = bits_of(lax.axis_size("head"))
    for bit in bits if flip else bits[::-1]:
        half = value.shape[0] // 2
        value = (
            value[:half].astype(F32) + swap(value[half:], "head", bit).astype(F32)
        ).astype(BF16)
    return value[0]


def spread_all(value, flip):
    own = spread_plane(value, flip)
    return (own, swap(own, "seq", 1))


def collect_all(own, other, flip):
    both = (own.astype(F32) + swap(other, "seq", 1).astype(F32)).astype(BF16)
    return collect_plane(both, flip)


def pick(value, index, axis=0):
    return lax.dynamic_index_in_dim(value, index, axis, keepdims=False)


def gather_seq(steps):
    return (steps[-1], swap(steps[-1], "seq", 1))


def scatter_seq(own, other):
    both = (own.astype(F32) + swap(other, "seq", 1).astype(F32)).astype(BF16)
    return collect_line(both)


def load_block(ref, line):
    block = ref[:, line]
    return block.reshape(block.shape[0] * block.shape[1], block.shape[2])


def parts_of(here, own, other, size):
    out = []
    for core, ref in enumerate((own, other)):
        for line in range(own.shape[0]):
            place = pl.multiple_of((here ^ (2 * line + core)) * size, size)
            out.append((ref, line, place))
    return out


def latent_kernel(
    s_ref, x_ref, cos, sin, own, other, keys_out, lat_out, gattn_out, gffn_out, wide_out
):
    here = s_ref[0]
    rows = RANK + RDIM
    size = own.shape[2]
    x = x_ref[...].astype(F32)
    inverse = rms_inverse(x)
    acc = jnp.zeros((x.shape[0], rows), F32)
    glat = jnp.zeros((RANK // size, size), F32)
    for ref, line, place in parts_of(here, own, other, size):
        gains = ref[line, rows:, :].astype(F32)
        block = x_ref[:, pl.ds(place, size)].astype(F32)
        normed = (block * inverse * gains[0:1]).astype(BF16)
        acc = acc + dot_nt(normed, ref[line, :rows, :])
        gattn_out[:, pl.ds(place, size)] = gains[0:1]
        gffn_out[:, pl.ds(place, size)] = gains[1:2]
        glat = glat + gains[2 : 2 + RANK // size]
        wide_out[:, pl.ds(place, size)] = ref[line, :rows, :]
    low = acc.astype(BF16)
    lat_out[...] = low
    low = low.astype(F32)
    comp = low[:, :RANK]
    glat = jnp.concatenate([glat[i : i + 1] for i in range(RANK // size)], axis=1)
    normed = comp * rms_inverse(comp) * glat
    first, second = low[:, RANK : RANK + HALF], low[:, RANK + HALF :]
    keys_out[...] = jnp.concatenate(
        [normed, first * cos[...] - second * sin[...], first * sin[...] + second * cos[...]],
        axis=1,
    ).astype(BF16)


def block_scores(query, keys, masks):
    scores = dot_nt(query, keys)
    if masks is not None:
        scores = jnp.where(masks, scores, NEG_LARGE)
    return scores


def fill_expand(here, own, other, wexp, rank_each):
    for ref, line, place in parts_of(here, own, other, rank_each):
        wexp[pl.ds(place, rank_each), :] = ref[line, :rank_each, :]


def attend_kernel(heads, masked, *refs):
    if masked:
        s_ref, qblk_ref, kblk_ref, *refs = refs
    else:
        s_ref, *refs = refs
    (
        x, gain, cos, sin, own, other, q_own, q_other, e_own, e_other, o_own, o_other,
        normed_out, q_out, att_out, lse_out, part_out, acc, mx, sm, wexp,
    ) = refs
    group = x.shape[0]
    lines = own.shape[1]
    nope = heads * HDIM
    wide = heads * HALF
    here = s_ref[0]
    fill_expand(here, e_own, e_other, wexp, RANK // (2 * lines))
    rows = x[...].astype(F32)
    normed_out[...] = (rows * rms_inverse(rows) * gain[...]).astype(BF16)
    qlin = jnp.zeros((group, heads * QDIM), F32)
    size = q_own.shape[1]
    for ref, line, place in parts_of(here, q_own, q_other, size):
        qlin = qlin + dot(normed_out[:, pl.ds(place, size)], ref[line])
    first = qlin[:, nope : nope + wide]
    second = qlin[:, nope + wide :]
    turned_a = first * cos[...] - second * sin[...]
    turned_b = first * sin[...] + second * cos[...]
    for h in range(heads):
        q_out[h] = jnp.concatenate(
            [
                qlin[:, h * HDIM : (h + 1) * HDIM],
                turned_a[:, h * HALF : (h + 1) * HALF],
                turned_b[:, h * HALF : (h + 1) * HALF],
            ],
            axis=1,
        ).astype(BF16)
    acc[...] = jnp.zeros_like(acc)
    mx[...] = jnp.full_like(mx, NEG_LARGE)
    sm[...] = jnp.zeros_like(sm)

    for core, ref in enumerate((own, other)):

        def step(line, carry, core=core, ref=ref):
            @pl.when((here ^ (2 * line + core)) <= here)
            def _():
                latent = load_block(ref, line)
                expanded = dot(latent[:, :RANK], wexp[...]).astype(BF16)
                rope_key = latent[:, RANK:]
                allowed = None
                if masked:
                    allowed = kblk_ref[pl.ds(2 * line + core, 1), :] <= qblk_ref[...]
                for h in range(heads):
                    keys = jnp.concatenate(
                        [expanded[:, 2 * h * HDIM : (2 * h + 1) * HDIM], rope_key], axis=1
                    )
                    vals = expanded[:, (2 * h + 1) * HDIM : (2 * h + 2) * HDIM]
                    scores = block_scores(q_out[h], keys, allowed)
                    old = mx[h][:, :1]
                    new = jnp.maximum(old, jnp.max(scores, axis=1, keepdims=True))
                    weights = jnp.exp2((scores - new) * (SCALE * LOG2E))
                    if masked:
                        weights = jnp.where(allowed, weights, 0.0)
                    rescale = jnp.exp2((old - new) * (SCALE * LOG2E))
                    sm[h] = sm[h] * rescale + jnp.sum(weights, axis=1, keepdims=True)
                    acc[h] = acc[h] * rescale + dot(weights.astype(BF16), vals)
                    mx[h] = jnp.broadcast_to(new, (group, HDIM))

            return carry

        lax.fori_loop(0, lines, step, 0)
    for h in range(heads):
        att_out[:, h * HDIM : (h + 1) * HDIM] = (acc[h] / sm[h]).astype(BF16)
        lse_out[h] = mx[h] * (SCALE * LOG2E) + jnp.log2(sm[h])
    size = o_own.shape[2]
    for ref, line, place in parts_of(here, o_own, o_other, size):
        part_out[:, pl.ds(place, size)] = dot(att_out[...], ref[line]).astype(BF16)


def attend_back_kernel(heads, masked, batches, *refs):
    s_ref, *refs = refs
    take = lambda count: [refs.pop(0) for _ in range(count)]
    marks = [take(2) if masked else None for _ in range(batches)]
    per_batch = [take(9) for _ in range(batches)]
    q_own, q_other, e_own, e_other, o_own, o_other = take(6)
    outs = [take(3) for _ in range(batches)]
    dq_own, dq_other, de_own, de_other, do_own, do_other = take(6)
    gq_acc, gqlin, gatt, wexp, dwexp, dwq, dwo = refs
    group = per_batch[0][0].shape[0]
    lines = q_own.shape[0]
    nope = heads * HDIM
    wide = heads * HALF
    here = s_ref[0]
    fill_expand(here, e_own, e_other, wexp, RANK // (2 * lines))
    dwexp[...] = jnp.zeros_like(dwexp)
    out_parts = parts_of(here, o_own, o_other, o_own.shape[2])
    query_parts = parts_of(here, q_own, q_other, q_own.shape[1])
    for b in range(batches):
        gres, normed, q_ref, att, lse, cos, sin, own, other = per_batch[b]
        gpart_out, own_out, other_out = outs[b]
        plane, each = own.shape[0], own.shape[2]
        total = jnp.zeros((group, heads * HDIM), F32)
        for i, (ref, line, place) in enumerate(out_parts):
            block = gres[:, pl.ds(place, ref.shape[2])]
            total = total + dot_nt(block, ref[line])
            term = dot_tn(att[...], block)
            dwo[i] = term if b == 0 else dwo[i] + term
        gatt[...] = total.astype(BF16)
        gq_acc[...] = jnp.zeros_like(gq_acc)
        deltas = [
            jnp.sum(
                gatt[:, h * HDIM : (h + 1) * HDIM].astype(F32)
                * att[:, h * HDIM : (h + 1) * HDIM].astype(F32),
                axis=1,
                keepdims=True,
            )
            for h in range(heads)
        ]
        for core, (ref, out) in enumerate(((own, own_out), (other, other_out))):

            def step(line, carry, core=core, ref=ref, out=out, b=b, q_ref=q_ref, lse=lse):
                live = (here ^ (2 * line + core)) <= here

                @pl.when(jnp.logical_not(live))
                def _():
                    out[:, line] = jnp.zeros((plane, each, RANK + RDIM), BF16)

                @pl.when(live)
                def _():
                    latent = load_block(ref, line)
                    expanded = dot(latent[:, :RANK], wexp[...]).astype(BF16)
                    rope_key = latent[:, RANK:]
                    allowed = None
                    if masked:
                        qblk_ref, kblk_ref = marks[b]
                        allowed = kblk_ref[pl.ds(2 * line + core, 1), :] <= qblk_ref[...]
                    grads = []
                    grad_rope = jnp.zeros((group, RDIM), F32)
                    for h in range(heads):
                        keys = jnp.concatenate(
                            [expanded[:, 2 * h * HDIM : (2 * h + 1) * HDIM], rope_key], axis=1
                        )
                        vals = expanded[:, (2 * h + 1) * HDIM : (2 * h + 2) * HDIM]
                        query = q_ref[h]
                        gout = gatt[:, h * HDIM : (h + 1) * HDIM]
                        scores = block_scores(query, keys, allowed)
                        probs = jnp.exp2(scores * (SCALE * LOG2E) - lse[h][:, :1])
                        if masked:
                            probs = jnp.where(allowed, probs, 0.0)
                        gprobs = dot_nt(gout, vals)
                        gscores = (probs * (gprobs - deltas[h])).astype(BF16)
                        gq_acc[h] = gq_acc[h] + dot(gscores, keys)
                        gkeys = dot_tn(gscores, query) * SCALE
                        gvals = dot_tn(probs.astype(BF16), gout)
                        grads.append(gkeys[:, :HDIM].astype(BF16))
                        grads.append(gvals.astype(BF16))
                        grad_rope = grad_rope + gkeys[:, HDIM:]
                    gexp = jnp.concatenate(grads, axis=1)
                    dwexp[...] = dwexp[...] + dot_tn(latent[:, :RANK], gexp)
                    gcomp = dot_nt(gexp, wexp[...])
                    packed = jnp.concatenate([gcomp, grad_rope], axis=1).astype(BF16)
                    out[:, line] = packed.reshape(plane, each, RANK + RDIM)

                return carry

            lax.fori_loop(0, lines, step, 0)
        firsts, seconds = [], []
        for h in range(heads):
            value = gq_acc[h] * SCALE
            gqlin[:, h * HDIM : (h + 1) * HDIM] = value[:, :HDIM].astype(BF16)
            firsts.append(value[:, HDIM : HDIM + HALF])
            seconds.append(value[:, HDIM + HALF :])
        first = jnp.concatenate(firsts, axis=1)
        second = jnp.concatenate(seconds, axis=1)
        gqlin[:, nope : nope + wide] = (first * cos[...] + second * sin[...]).astype(BF16)
        gqlin[:, nope + wide :] = (second * cos[...] - first * sin[...]).astype(BF16)
        for i, (ref, line, place) in enumerate(query_parts):
            size = ref.shape[1]
            gpart_out[:, pl.ds(place, size)] = dot_nt(gqlin[...], ref[line]).astype(BF16)
            term = dot_tn(normed[:, pl.ds(place, size)], gqlin[...])
            dwq[i] = term if b == 0 else dwq[i] + term
    for line in range(lines):
        dq_own[line] = dwq[line].astype(BF16)
        dq_other[line] = dwq[lines + line].astype(BF16)
        do_own[line] = dwo[line].astype(BF16)
        do_other[line] = dwo[lines + line].astype(BF16)
    each = RANK // (2 * lines)
    for core, out in enumerate((de_own, de_other)):
        for line in range(lines):
            place = pl.multiple_of((here ^ (2 * line + core)) * each, each)
            out[line] = dwexp[pl.ds(place, each), :].astype(BF16)


def vmem_specs(count):
    return [pl.BlockSpec(memory_space=pltpu.VMEM)] * count


def smem_spec():
    return [pl.BlockSpec(memory_space=pltpu.SMEM)]


def own_latents(here, x, cos, sin, parts):
    rows, width = x.shape
    return pl.pallas_call(
        latent_kernel,
        out_shape=(
            jax.ShapeDtypeStruct((rows, RANK + RDIM), BF16),
            jax.ShapeDtypeStruct((rows, RANK + RDIM), BF16),
            jax.ShapeDtypeStruct((1, width), F32),
            jax.ShapeDtypeStruct((1, width), F32),
            jax.ShapeDtypeStruct((RANK + RDIM, width), BF16),
        ),
        in_specs=smem_spec() + vmem_specs(5),
        out_specs=tuple(vmem_specs(5)),
        compiler_params=pltpu.CompilerParams(vmem_limit_bytes=40 * MIB),
        cost_estimate=pl.CostEstimate(
            flops=1_000_000_000, bytes_accessed=6_000_000, transcendentals=1_000
        ),
        name="own_latents",
    )(here, x, cos, sin, *parts)


def attend(here, marks, x, gain, cos, sin, keys, weights, heads):
    group, width = x.shape
    return pl.pallas_call(
        functools.partial(attend_kernel, heads, bool(marks)),
        out_shape=(
            jax.ShapeDtypeStruct((group, width), BF16),
            jax.ShapeDtypeStruct((heads, group, QDIM), BF16),
            jax.ShapeDtypeStruct((group, heads * HDIM), BF16),
            jax.ShapeDtypeStruct((heads, group, HDIM), F32),
            jax.ShapeDtypeStruct((group, width), BF16),
        ),
        in_specs=smem_spec() + vmem_specs(len(marks) + 12),
        out_specs=tuple(vmem_specs(5)),
        scratch_shapes=[pltpu.VMEM((heads, group, HDIM), F32)] * 3
        + [pltpu.VMEM((RANK, 2 * heads * HDIM), BF16)],
        compiler_params=pltpu.CompilerParams(vmem_limit_bytes=56 * MIB),
        cost_estimate=pl.CostEstimate(
            flops=8_000_000_000, bytes_accessed=12_000_000, transcendentals=4_000_000
        ),
        name="attend",
    )(here, *marks, x, gain, cos, sin, *keys, *weights)


def attend_back(here, marks, per_batch, weights):
    batches = len(per_batch)
    heads, group = per_batch[0][2].shape[:2]
    width = per_batch[0][0].shape[1]
    q_own, _, e_own, _, o_own, _ = weights
    lines = q_own.shape[0]
    rank_each = RANK // (2 * lines)
    outs = []
    for args in per_batch:
        outs.append(jax.ShapeDtypeStruct((group, width), BF16))
        outs += [jax.ShapeDtypeStruct(args[7].shape, BF16)] * 2
    outs += [jax.ShapeDtypeStruct(q_own.shape, BF16)] * 2
    outs += [jax.ShapeDtypeStruct((lines, rank_each, e_own.shape[2]), BF16)] * 2
    outs += [jax.ShapeDtypeStruct(o_own.shape, BF16)] * 2
    inputs = [m for mark in marks for m in mark] + [v for args in per_batch for v in args]
    inputs += list(weights)
    return pl.pallas_call(
        functools.partial(attend_back_kernel, heads, bool(marks[0]), batches),
        out_shape=tuple(outs),
        in_specs=smem_spec() + vmem_specs(len(inputs)),
        out_specs=tuple(vmem_specs(len(outs))),
        scratch_shapes=[
            pltpu.VMEM((heads, group, QDIM), F32),
            pltpu.VMEM((group, heads * QDIM), BF16),
            pltpu.VMEM((group, heads * HDIM), BF16),
            pltpu.VMEM((RANK, 2 * heads * HDIM), BF16),
            pltpu.VMEM((RANK, 2 * heads * HDIM), F32),
            pltpu.VMEM((2 * lines,) + q_own.shape[1:], F32),
            pltpu.VMEM((2 * lines,) + o_own.shape[1:], F32),
        ],
        compiler_params=pltpu.CompilerParams(vmem_limit_bytes=62 * MIB),
        cost_estimate=pl.CostEstimate(
            flops=24_000_000_000, bytes_accessed=30_000_000, transcendentals=8_000_000
        ),
        name="attend_back",
    )(here, *inputs)


def feed_kernel(batch, order, aliased, *refs):
    slot, gate, xa, xb, c, wg, wu, wd, sgu, sgut, sd = refs[:11]
    refs = refs[11 + aliased :]
    o, ga, gb, rows_out, grows_out, act_out, gpre_out, gup_out, dsgut, dsd = refs
    plane, per, half, width = xa.shape
    group = 2 * plane * half
    cap = rows_out.shape[2]
    pad = sd.shape[0]

    @pl.when(pl.program_id(0) == 0)
    def _():
        dsgut[...] = jnp.zeros_like(dsgut)
        dsd[...] = jnp.zeros_like(dsd)

    xs, cs, picks, gates = [], [], [], []
    for i in range(per):
        xs += [xa[:, i].reshape(group // 2, width), xb[:, i].reshape(group // 2, width)]
        for side in range(2):
            for j in range(plane):
                place = order[j] if (side != batch) else j
                cs.append(c[place, i, side * half : (side + 1) * half])
        chosen = lax.broadcasted_iota(jnp.int32, (cap, group), 0) == slot[i]
        gates.append(jnp.sum(jnp.where(chosen, gate[i], 0.0), axis=1, keepdims=True))
        picks.append(chosen.astype(F32))
    x = jnp.concatenate(xs, axis=0)
    cot = jnp.concatenate(cs, axis=0)
    gates = jnp.concatenate(gates, axis=0)
    rows = jnp.concatenate(
        [
            dot(picks[i].astype(BF16), x[i * group : (i + 1) * group]).astype(BF16)
            for i in range(per)
        ],
        axis=0,
    )
    grows = jnp.concatenate(
        [dot(picks[i].astype(BF16), cot[i * group : (i + 1) * group]) for i in range(per)],
        axis=0,
    )
    grows = (grows * gates).astype(BF16)
    pre = dot_nt(rows, wg[...])
    upp = dot_nt(rows, wu[...])
    sig = 1.0 / (1.0 + jnp.exp(-pre))
    silu = pre * sig
    act = (silu * upp).astype(BF16)
    geact = dot_nt(grows, wd[...])
    gpre = (geact * upp * (sig * (1.0 + pre * (1.0 - sig)))).astype(BF16)
    gup = (geact * silu).astype(BF16)
    for i in range(per):
        part = slice(i * cap, (i + 1) * cap)
        rows_out[0, i] = rows[part]
        grows_out[0, i] = grows[part]
        act_out[0, i] = act[part]
        gpre_out[0, i] = gpre[part]
        gup_out[0, i] = gup[part]
    made = (dot(act, wd[...]) * gates).astype(BF16)
    gmade = (dot(gpre, wg[...]) + dot(gup, wu[...])).astype(BF16)
    both = dot(x, sgu[...])
    spre, supp = both[:, :pad], both[:, pad:]
    ssig = 1.0 / (1.0 + jnp.exp(-spre))
    ssilu = spre * ssig
    sact = (ssilu * supp).astype(BF16)
    gsact = dot_nt(cot, sd[...])
    gspre = (gsact * supp * (ssig * (1.0 + spre * (1.0 - ssig)))).astype(BF16)
    gsupp = (gsact * ssilu).astype(BF16)
    gsboth = jnp.concatenate([gspre, gsupp], axis=1)
    dsgut[...] = dsgut[...] + dot_tn(gsboth, x)
    dsd[...] = dsd[...] + dot_tn(sact, cot)
    for i in range(per):
        back = picks[i].T.astype(BF16)
        toks = slice(i * group, (i + 1) * group)
        part = slice(i * cap, (i + 1) * cap)
        out = dot(
            jnp.concatenate([back, sact[toks]], axis=1),
            jnp.concatenate([made[part], sd[...]], axis=0),
        ).astype(BF16)
        for side in range(2):
            for j in range(plane):
                place = order[j] if (side != batch) else j
                at = (side * plane + j) * half
                o[place, i, side * half : (side + 1) * half] = out[at : at + half]
        gx = dot(
            jnp.concatenate([back, gsboth[toks]], axis=1),
            jnp.concatenate([gmade[part], sgut[...]], axis=0),
        ).astype(BF16)
        ga[:, i] = gx[: group // 2].reshape(plane, half, width)
        gb[:, i] = gx[group // 2 :].reshape(plane, half, width)


def feed(batch, core, batches, cap, slot, gate, xa, xb, cot, weights, earlier):
    plane, lines, half, width = xa.shape
    group = 2 * plane * half
    per = 2 if group <= 256 and lines % 2 == 0 else 1
    steps = lines // per
    hidden = weights[0].shape[0]
    pad = weights[-1].shape[0]

    def block(size):
        return pl.BlockSpec((plane, per, size, width), lambda i: (0, i, 0, 0))

    def fixed(shape):
        return pl.BlockSpec(shape, lambda i: (0,) * len(shape), pipeline_mode=pl.Buffered(1))

    def saved(size):
        return pl.BlockSpec((1, per, cap, size), lambda i: (batch, core * steps + i, 0, 0))

    mark = pl.BlockSpec((per, 1, group), lambda i: (i, 0, 0))
    full = jax.ShapeDtypeStruct(xa.shape, BF16)
    keep = [width, width, hidden, hidden, hidden]
    kept_shapes = [jax.ShapeDtypeStruct((batches, 2 * lines, cap, size), BF16) for size in keep]
    aliased = len(earlier)
    return pl.pallas_call(
        functools.partial(feed_kernel, batch, plane_order(True), aliased),
        grid=(steps,),
        out_shape=tuple(
            [jax.ShapeDtypeStruct(cot.shape, BF16), full, full]
            + kept_shapes
            + [
                jax.ShapeDtypeStruct((2 * pad, width), F32),
                jax.ShapeDtypeStruct((pad, width), F32),
            ]
        ),
        in_specs=[mark, mark, block(half), block(half), block(2 * half)]
        + [fixed(w.shape) for w in weights]
        + [pl.BlockSpec(memory_space=pl.ANY)] * aliased,
        out_specs=tuple(
            [block(2 * half), block(half), block(half)]
            + [saved(size) for size in keep]
            + [fixed((2 * pad, width)), fixed((pad, width))]
        ),
        input_output_aliases={11 + i: 3 + i for i in range(aliased)},
        compiler_params=pltpu.CompilerParams(vmem_limit_bytes=62 * MIB),
        cost_estimate=pl.CostEstimate(
            flops=16_000_000_000, bytes_accessed=30_000_000, transcendentals=1_000_000
        ),
        name="feed",
    )(slot, gate, xa, xb, cot, *weights, *earlier)


def local(
    inputs,
    cotangent,
    routes,
    gate_weights,
    attn_gain,
    latent_gain,
    ffn_gain,
    query_proj,
    latent_proj,
    expand_proj,
    out_proj,
    shared_gate,
    shared_up,
    shared_down,
    expert_gate,
    expert_up_weight,
    expert_down,
):
    seq_count = lax.axis_size("seq")
    head_count = lax.axis_size("head")
    seq_index = lax.axis_index("seq")
    head_index = lax.axis_index("head")
    lines = depth()
    line, core = seq_index // 2, seq_index % 2
    batches, each, width = inputs.shape
    group = each * head_count
    heads = out_proj.shape[0] // HDIM
    half = each // 2
    orders = [plane_order(False), plane_order(True)]
    serial = group > BLOCK

    here = seq_index.reshape(1)
    positions = seq_index * group + jnp.arange(group, dtype=jnp.int32)

    shard = latent_proj.shape[0]
    n_lat = latent_gain.shape[0]
    lat_gain = lax.dynamic_update_slice_in_dim(
        jnp.zeros((RANK,), BF16), latent_gain, seq_index * n_lat, 0
    )
    gain_rows = 16
    gain_part = jnp.concatenate(
        [attn_gain[None], ffn_gain[None], lat_gain.reshape(RANK // shard, shard)], axis=0
    )
    gain_part = jnp.pad(gain_part, ((0, gain_rows - gain_part.shape[0]), (0, 0)))
    lat_mine = jnp.concatenate([jnp.transpose(latent_proj), gain_part], axis=0)
    with jax.named_scope("latent_weights"):
        lat_steps = spread_line(lat_mine)
        lat_parts = gather_seq(lat_steps)
    with jax.named_scope("inputs"):
        group_rows = [
            spread_plane(inputs[b], bool(b)).reshape(group, width) for b in range(batches)
        ]

    pair = head_count // 2
    expert_ids = jnp.arange(seq_count, dtype=jnp.int32) * pair + head_index // 2
    hits = routes[None] == expert_ids[:, None, None, None]
    gate_of = jnp.sum(jnp.where(hits, gate_weights[None], 0.0), axis=-1)
    named = jnp.any(hits, axis=-1)

    def block_order(value):
        value = value.reshape(value.shape[:-1] + (head_count, 2, half))
        sides = []
        for side in range(2):
            ids = jnp.array(orders[side], jnp.int32) ^ head_index
            sides.append(jnp.take(value[..., side, :], ids, axis=-2))
        value = jnp.stack(sides, axis=-3)
        return value.reshape(value.shape[:-3] + (group,))

    gate_of, named = block_order(gate_of), block_order(named)
    ahead = jnp.arange(group)[:, None] < jnp.arange(group)[None, :]
    rank = lax.dot_general(
        named.astype(BF16), ahead.astype(BF16), (((2,), (0,)), ((), ())), preferred_element_type=F32
    )
    gate_high = gate_of.astype(BF16)
    mark_mine = jnp.stack(
        [
            jnp.where(named, jnp.minimum(rank, 255.0), -1.0).astype(BF16),
            gate_high,
            (gate_of - gate_high.astype(F32)).astype(BF16),
        ],
        axis=1,
    )
    expand_rows, expand_cols = expand_proj.shape
    mark_rows = -(-mark_mine.size // expand_cols)
    mark_pad = -(-mark_rows // 16) * 16
    mark_mine = jnp.pad(
        mark_mine.reshape(-1), (0, mark_pad * expand_cols - mark_mine.size)
    ).reshape(mark_pad, expand_cols)
    with jax.named_scope("expand_weights"):
        expand_mine = after(jnp.concatenate([expand_proj, mark_mine], axis=0), lat_steps[1])
        expand_steps = spread_line(expand_mine)
        expand_parts = gather_seq(expand_steps)
    mark_size = seq_count * 3 * batches * group

    def marks_from(parts):
        flat = parts[:, expand_rows:].reshape(lines, -1)[:, :mark_size]
        return pick(flat.reshape(lines, seq_count, 3, batches, 1, group), seq_index, 1).astype(F32)

    marks_mine = [marks_from(parts) for parts in expand_parts]
    slots = [m[:, 0].astype(jnp.int32) for m in marks_mine]
    gates = [m[:, 1] + m[:, 2] for m in marks_mine]

    cos_all, sin_all = rope_tables(positions)
    own_cos, own_sin = [
        lax.dynamic_slice_in_dim(t, head_index * each, each, 0) for t in (cos_all, sin_all)
    ]
    own_keys, own_latent, gain_attn, gain_ffn, latent_t = own_latents(
        here,
        inputs.reshape(batches * each, width),
        jnp.tile(own_cos, (batches, 1)),
        jnp.tile(own_sin, (batches, 1)),
        lat_parts,
    )
    own_keys = own_keys.reshape(batches, each, RANK + RDIM)
    with jax.named_scope("keys"):
        key_steps = spread_line(own_keys)
        keys = [spread_all(key_steps[-1][:, b], bool(b)) for b in range(batches)]

    cols = query_proj.reshape(query_proj.shape[0], heads, QDIM)
    query_mine = jnp.concatenate(
        [
            cols[..., :HDIM].reshape(-1, heads * HDIM),
            cols[..., HDIM : HDIM + HALF].reshape(-1, heads * HALF),
            cols[..., HDIM + HALF :].reshape(-1, heads * HALF),
        ],
        axis=1,
    )
    with jax.named_scope("query_weights"):
        query_mine = after(query_mine, expand_steps[1])
        query_steps = spread_line(query_mine)
        query_parts = gather_seq(query_steps)
    with jax.named_scope("output_weights"):
        out_mine = after(out_proj, query_steps[1], key_steps[1])
        out_steps = spread_line(out_mine)
        out_parts = gather_seq(out_steps)
    attn_weights = (*query_parts, *expand_parts, *out_parts)

    hidden_each = shared_gate.shape[1] // seq_count
    hidden_pad = -(-hidden_each // 128) * 128
    dshard = shared_gate.shape[0]
    shared_mine = jnp.stack(
        [
            jnp.transpose(shared_gate).reshape(seq_count, hidden_each, dshard),
            jnp.transpose(shared_up).reshape(seq_count, hidden_each, dshard),
            shared_down.reshape(seq_count, hidden_each, dshard),
        ],
        axis=1,
    ).reshape(lines, 2, 3, hidden_each, dshard)
    with jax.named_scope("shared_weights"):
        kept = pick(shared_mine, core, 1)
        came = swap(pick(shared_mine, core ^ 1, 1), "seq", 1)
        paired = jnp.where(core == 0, jnp.stack([kept, came], 1), jnp.stack([came, kept], 1))
        paired = after(paired, out_steps[1])
        shared_pieces = [pick(paired, line)]
        shared_pieces += [swap(pick(paired, line ^ k), "seq", 2 * k) for k in range(1, lines)]
    shared_t = jnp.zeros((lines, 2, 3, hidden_each, dshard), BF16)
    for k in range(lines):
        shared_t = lax.dynamic_update_slice_in_dim(
            shared_t, shared_pieces[k][None], line ^ k, 0
        )
    shared_t = jnp.transpose(shared_t, (2, 3, 0, 1, 4)).reshape(3, hidden_each, width)
    shared_t = jnp.pad(shared_t, ((0, 0), (0, hidden_pad - hidden_each), (0, 0)))
    sgut = shared_t[:2].reshape(2 * hidden_pad, width)
    weights = (
        jnp.transpose(expert_gate[0]),
        jnp.transpose(expert_up_weight[0]),
        expert_down[0],
        jnp.transpose(sgut),
        sgut,
        shared_t[2],
    )

    with jax.named_scope("cotangents"):
        cot_steps = spread_line(after(cotangent, out_steps[1]))
        cot_line = after(cot_steps[-1], keys[0][0], keys[1][0])

    own_rows = inputs.astype(F32)
    own_inverse = rms_inverse(own_rows)
    own_hat = own_rows * own_inverse
    normed, queries, attended, lses, tables, marks = [], [], [], [], [], []
    residual, ffn_hat, ffn_inverse, ffn_rows = [], [], [], []
    for b in range(batches):
        away = jnp.array(orders[b], jnp.int32) ^ head_index
        place = (away[:, None] * each + jnp.arange(each, dtype=jnp.int32)[None, :]).reshape(group)
        cos_b, sin_b = [
            jnp.tile(
                jnp.take(t.reshape(head_count, each, HALF), away, axis=0).reshape(group, HALF),
                (1, heads),
            )
            for t in (cos_all, sin_all)
        ]
        tables.append((cos_b, sin_b))
        marks_b = ()
        if group > BLOCK:
            own_block = (seq_index * group + place) // BLOCK
            offsets = jnp.arange(seq_count, dtype=jnp.int32) ^ seq_index
            key_block = (offsets[:, None] * group + place[None, :]) // BLOCK
            marks_b = (jnp.broadcast_to(own_block[:, None], (group, group)), key_block)
        marks.append(marks_b)
        normed_b, q_b, att_b, lse_b, part = attend(
            here, marks_b, group_rows[b], gain_attn, cos_b, sin_b, keys[b], attn_weights, heads
        )
        normed.append(normed_b)
        queries.append(q_b)
        attended.append(att_b)
        lses.append(lse_b)
        part = part.reshape(head_count, each, width)
        total = part[0].astype(F32)
        with jax.named_scope("attention_sum"):
            for j in range(1, head_count):
                total = total + swap(part[j], "head", orders[b][j]).astype(F32)
        residual_b = own_rows[b] + total
        inverse_b = rms_inverse(residual_b)
        hat_b = residual_b * inverse_b
        ffn_b = (hat_b * gain_ffn).astype(BF16)
        residual.append(residual_b)
        ffn_inverse.append(inverse_b)
        ffn_hat.append(hat_b)
        ffn_rows.append(ffn_b)

    most_rows = 4 * group * TOPK // (3 * seq_count * pair)
    kept_rows, outs, grad_ffn, dsgut, dsd = (), [], [], 0.0, 0.0
    spread_ffn, cots = [], []
    for b in range(batches):
        with jax.named_scope("ffn_rows"):
            if serial and b:
                ffn_rows[b] = after(ffn_rows[b], grad_ffn[b - 1], outs[b - 1])
                cot_line = after(cot_line, grad_ffn[b - 1], outs[b - 1])
            rows_b = spread_line(ffn_rows[b])[-1]
            spread_ffn.append(
                (spread_all(rows_b[:, :half], False), spread_all(rows_b[:, half:], True))
            )
        with jax.named_scope("cotangents"):
            cots.append(spread_all(cot_line[:, b], bool(b)))
        made = [None, None]
        for side in (1, 0):
            res = feed(
                b, side, batches, most_rows, slots[side][:, b], gates[side][:, b],
                spread_ffn[b][0][side], spread_ffn[b][1][side], cots[b][side], weights, kept_rows,
            )
            made[side] = res[:3]
            kept_rows = tuple(res[3:8])
            dsgut = dsgut + res[8]
            dsd = dsd + res[9]
        with jax.named_scope("ffn_grads"):
            first = collect_all(made[0][1], made[1][1], False)
            second = collect_all(made[0][2], made[1][2], True)
            grad_ffn.append(collect_line(jnp.concatenate([first, second], axis=1)))
        with jax.named_scope("outputs"):
            outs.append(collect_all(made[0][0], made[1][0], bool(b)))

    ffn_hat, ffn_inverse = jnp.stack(ffn_hat), jnp.stack(ffn_inverse)
    grad_two, ffngain_term = norm_back(jnp.stack(grad_ffn), ffn_hat, ffn_inverse, gain_ffn)
    grad_residual = cotangent.astype(F32) + grad_two
    grad_attention = grad_residual.astype(BF16)
    with jax.named_scope("attention_grads"):
        gatt_rows = [
            spread_plane(grad_attention[b], bool(b)).reshape(group, width)
            for b in range(batches)
        ]
    per_batch = [
        (gatt_rows[b], normed[b], queries[b], attended[b], lses[b], *tables[b], *keys[b])
        for b in range(batches)
    ]
    if serial:
        calls = [
            attend_back(here, marks[b : b + 1], per_batch[b : b + 1], attn_weights)
            for b in range(batches)
        ]
        sums = [sum(v.astype(F32) for v in t).astype(BF16) for t in zip(*[c[3:] for c in calls])]
        res = [v for c in calls for v in c[:3]] + sums
    else:
        res = attend_back(here, marks, per_batch, attn_weights)
    gparts = [res[3 * b] for b in range(batches)]
    gkeys = [res[3 * b + 1 : 3 * b + 3] for b in range(batches)]
    dq_own, dq_other, de_own, de_other, do_own, do_other = res[3 * batches :]
    with jax.named_scope("key_grads"):
        grad_key = [collect_all(*gkeys[b], bool(b)) for b in range(batches)]
        grad_key = collect_line(jnp.stack(grad_key, axis=1))
    latent_rows = own_latent.astype(F32).reshape(batches, each, RANK + RDIM)
    compressed = latent_rows[..., :RANK]
    comp_inverse = rms_inverse(compressed)
    comp_hat = compressed * comp_inverse
    lat_gains = sum(
        part[:, RANK + RDIM + 2 : RANK + RDIM + 2 + RANK // shard].astype(F32).sum(axis=0)
        for part in lat_parts
    ).reshape(RANK)
    grad_comp = grad_key[..., :RANK]
    grad_a, grad_b = grad_key[..., RANK : RANK + HALF], grad_key[..., RANK + HALF :]
    grad_rope = jnp.concatenate(
        [grad_a * own_cos + grad_b * own_sin, grad_b * own_cos - grad_a * own_sin], axis=-1
    )
    grad_compressed, latgain_term = norm_back(grad_comp, comp_hat, comp_inverse, lat_gains)
    grad_latent = jnp.concatenate([grad_compressed, grad_rope], axis=-1).astype(BF16)

    grad_normed = []
    for b in range(batches):
        part = gparts[b].reshape(head_count, each, width)
        total = part[0].astype(F32)
        with jax.named_scope("normed_grads"):
            for j in range(1, head_count):
                total = total + swap(part[j], "head", orders[b][j]).astype(F32)
        grad_normed.append(total)
    grad_normed = jnp.stack(grad_normed) + dot(
        grad_latent.reshape(batches * each, RANK + RDIM), latent_t
    ).reshape(batches, each, width)
    grad_input, attngain_term = norm_back(grad_normed, own_hat, own_inverse, gain_attn)
    inputs_grad = (grad_input + grad_residual).astype(BF16)

    with jax.named_scope("query_grads"):
        query_grad = scatter_seq(dq_own, dq_other)
    nope = heads * HDIM
    query_grad = jnp.concatenate(
        [
            query_grad[:, :nope].reshape(-1, heads, HDIM),
            query_grad[:, nope : nope + heads * HALF].reshape(-1, heads, HALF),
            query_grad[:, nope + heads * HALF :].reshape(-1, heads, HALF),
        ],
        axis=-1,
    ).reshape(-1, heads * QDIM)
    with jax.named_scope("expand_grads"):
        expand_grad = scatter_seq(de_own, de_other)
    with jax.named_scope("output_grads"):
        outproj_grad = scatter_seq(do_own, do_other)
    share = (RANK + RDIM) // head_count
    with jax.named_scope("latent_grads"):
        latent_rows = [
            spread_plane(grad_latent[b], bool(b)).reshape(group, -1) for b in range(batches)
        ]
    latent_term = 0.0
    for b in range(batches):
        mine = lax.dynamic_slice_in_dim(latent_rows[b], head_index * share, share, 1)
        latent_term = latent_term + dot_tn(mine, normed[b])
    latent_term = latent_term.astype(BF16)
    gain_term = jnp.concatenate(
        [
            attngain_term.reshape(seq_count, 1, shard),
            ffngain_term.reshape(seq_count, 1, shard),
            jnp.pad(
                latgain_term.reshape(seq_count, 1, n_lat), ((0, 0), (0, 0), (0, shard - n_lat))
            ),
            jnp.zeros((seq_count, gain_rows - 3, shard), F32),
        ],
        axis=1,
    ).astype(BF16)
    latent_term = jnp.concatenate(
        [
            jnp.stack([latent_term[:, i * shard : (i + 1) * shard] for i in range(seq_count)]),
            gain_term,
        ],
        axis=1,
    )
    latent_own, latent_other = [
        jnp.stack([pick(latent_term, seq_index ^ (2 * k + c)) for k in range(lines)])
        for c in range(2)
    ]
    with jax.named_scope("latent_grads"):
        latent_mine = scatter_seq(latent_own, latent_other).astype(BF16)
        latent_parts = [latent_mine]
        latent_parts += [swap(latent_mine, "head", k) for k in range(1, head_count)]
    latent_grad = jnp.zeros((head_count, share, shard), BF16)
    gain_grad = 0.0
    for k in range(head_count):
        latent_grad = lax.dynamic_update_slice_in_dim(
            latent_grad, latent_parts[k][None, :share], head_index ^ k, 0
        )
        gain_grad = gain_grad + latent_parts[k][share:].astype(F32)
    latent_grad = jnp.transpose(latent_grad.reshape(RANK + RDIM, shard)).astype(F32)
    attngain_grad = gain_grad[0]
    ffngain_grad = gain_grad[1]
    latgain_grad = gain_grad[2, :n_lat]

    shared_term = jnp.concatenate(
        [dsgut.reshape(2, hidden_pad, width), dsd[None]], axis=0
    )[:, :hidden_each].astype(BF16)
    shared_term = jnp.transpose(
        shared_term.reshape(3, hidden_each, lines, 2, dshard), (2, 3, 0, 1, 4)
    )
    with jax.named_scope("shared_grads"):
        held = [pick(shared_term, line)]
        held += [swap(pick(shared_term, line ^ k), "seq", 2 * k) for k in range(1, lines)]
        held = jnp.stack(held)
        kept = pick(held, core, 1)
        came = swap(pick(held, core ^ 1, 1), "seq", 1)
    paired = jnp.where(core == 0, jnp.stack([kept, came], 1), jnp.stack([came, kept], 1))
    shared_grad = jnp.zeros(paired.shape, BF16)
    for k in range(lines):
        shared_grad = lax.dynamic_update_slice_in_dim(shared_grad, paired[k : k + 1], line ^ k, 0)
    shared_grad = jnp.transpose(shared_grad, (2, 0, 1, 3, 4)).reshape(3, -1, dshard).astype(F32)
    shgate_grad = jnp.transpose(shared_grad[0])
    shup_grad = jnp.transpose(shared_grad[1])
    shdown_grad = shared_grad[2]

    rows, grows, act, gpre, gup = [v.reshape(-1, v.shape[-1]) for v in kept_rows]
    exgate_grad = jnp.transpose(dot_tn(gpre, rows))[None]
    exup_grad = jnp.transpose(dot_tn(gup, rows))[None]
    exdown_grad = dot_tn(act, grows)[None]

    with jax.named_scope("outputs"):
        ffn_own = collect_line(jnp.stack(outs, axis=1))
    output = (jnp.stack(residual) + ffn_own).astype(BF16)

    return (
        output,
        inputs_grad,
        query_grad,
        latent_grad,
        expand_grad,
        outproj_grad,
        shgate_grad,
        shup_grad,
        shdown_grad,
        exgate_grad,
        exup_grad,
        exdown_grad,
        attngain_grad,
        latgain_grad,
        ffngain_grad,
    )


def solution(mesh):
    own = P(None, ("seq", "head"), None)
    stack = P(("seq", "head"), None, None)
    return jax.shard_map(
        local,
        mesh=mesh,
        in_specs=(
            own,
            own,
            P(None, "seq", None),
            P(None, "seq", None),
            P("seq"),
            P("seq"),
            P("seq"),
            P("seq", "head"),
            P("seq", None),
            P("seq", "head"),
            P("head", "seq"),
            P("seq", "head"),
            P("seq", "head"),
            P("head", "seq"),
            stack,
            stack,
            stack,
        ),
        out_specs=(
            own,
            own,
            P("seq", "head"),
            P("seq", None),
            P("seq", "head"),
            P("head", "seq"),
            P("seq", "head"),
            P("seq", "head"),
            P("head", "seq"),
            stack,
            stack,
            stack,
            P("seq"),
            P("seq"),
            P("seq"),
        ),
        check_vma=False,
    )
```

time: 2020 us -> 1030 us (0.51)
  waiting for transfers between devices: 1320 us -> 408 us
  matrix products: 205 us -> 30.1 us
  Pallas kernels: 0 us -> 164 us
  starting transfers between devices: 76.8 us -> 240 us
  blocking collectives: 104 us -> 0 us
  local copies, waits for them, and re-layouts: 142 us -> 74.2 us
  other arithmetic: 135 us -> 90.4 us
    reduce_scatter x10 -> x0, waiting for transfers between devices: 423 us -> none  [the longest x1 193 us: local(): lax.psum_scatter(key_terms.astype(jnp.bfloat16), 'seq', scatter_dimension...]
    ppermute x0 -> x123, waiting for transfers between devices: none -> 408 us  [swap(): return lax.ppermute(value, axis, [(i, i ^ mask) for i in range(size)])]
    all_gather x11 -> x0, waiting for transfers between devices: 374 us -> none  [the longest x1 111 us: local(): lax.all_gather(shared_down, 'seq', axis=1, tiled=True)]
    all_to_all x4 -> x0, waiting for transfers between devices: 337 us -> none  [the longest x1 185 us: local(): lax.all_to_all(send_grads, 'seq', split_axis=0, concat_axis=0, tiled=True)]
    ppermute x0 -> x123, starting transfers between devices: none -> 240 us  [swap(): return lax.ppermute(value, axis, [(i, i ^ mask) for i in range(size)])]
    psum x3 -> x0, waiting for transfers between devices: 177 us -> none  [the longest x1 68 us: local(): lax.psum(grad_normed_q.astype(jnp.bfloat16), 'head').astype(jnp.float32)]
    dot_general x37 -> x7, matrix products: 205 us -> 30.1 us  [the longest x5 29.1 us: dot_tn(): lax.dot_general(a, b, (((0,), (0,)), ((), ())), preferred_element_type=F32)]
    pallas_call x0 -> x8, Pallas kernels: none -> 164 us  [the longest x4 118 us: feed(): pl.pallas_call(functools.partial(feed_kernel, batch, plane_order(True), a...]
  transfers between devices with their start and end apart: 28 -> 123, of which waited for: 26 -> 50; matrix products, arithmetic and copies ran while one was open for 18% -> 17% of each run, Pallas kernels for 0% -> 16%
where the time goes in v1:
time: 1030 us; the launch traced here: 1020 us
  waiting for transfers between devices  408 us (40%)
  starting transfers between devices  240 us (23%)
  Pallas kernels  164 us (16%)
  other arithmetic  90.4 us (9%)
  local copies, waits for them, and re-layouts  74.2 us (7%)
  matrix products  30.1 us (3%)
  between operations  10.5 us (1%)
    ppermute x123, waiting for transfers between devices, swap(): return lax.ppermute(value, axis, [(i, i ^ mask) for i in range(size)])  408 us
    ppermute x123, starting transfers between devices, swap(): return lax.ppermute(value, axis, [(i, i ^ mask) for i in range(size)])  240 us
    pallas_call x4, Pallas kernels, feed(): pl.pallas_call(functools.partial(feed_kernel, batch, plane_order(True), a...  118 us
    dot_general x5, matrix products, dot_tn(): lax.dot_general(a, b, (((0,), (0,)), ((), ())), preferred_element_type=F32)  29.1 us
    concatenate x28, other arithmetic, spread_plane(): value = jnp.concatenate([value, swap(value, 'head', bit)], axis=0)  25.3 us
    unnamed x223, local copies, waits for them, and re-layouts  23.9 us
    pallas_call x1, Pallas kernels, attend_back(): pl.pallas_call(functools.partial(attend_back_kernel, heads, bool(marks[0]...  23 us
    pallas_call x2, Pallas kernels, attend(): pl.pallas_call(functools.partial(attend_kernel, heads, bool(marks)), out_...  21.8 us
  transfers between devices with their start and end apart: 123, of which 50 were waited for; matrix products, arithmetic and copies ran while one was open for 17% of the time, Pallas kernels for 16%

profile of v1, /device:TPU:0, one launch (start us, length us, event | category | flops | bytes accessed | tf_op | source)
XLA Modules:
  0.0 1016.9 jit_solution(12149844685062857293)
XLA Ops:
  52.5 12.5 %collective-permute-done.3 = bf16[2,592,256]{2,1,0:T(8,128)(2,1)S(1)} collective-permute-done((bf16[2,592,256]{2,1,0:T(8,128)(2,1)S(1)}, bf16[2,592,256]{2,1,0:T(8,128)(2,1)S(1)}, u32[]{:S(2)}, u32[]{:S(2)}) %collective-permute-start.3) | collective-permute-done | bytes 606240 | tf_op jit(solution)/shard_map/latent_weights/ppermute | solution.py:58
  97.1 18.7 %collective-permute-done.16 = bf16[1,512,256]{2,1,0:T(8,128)(2,1)S(1)} collective-permute-done((bf16[1,512,256]{2,1,0:T(8,128)(2,1)}, bf16[1,512,256]{2,1,0:T(8,128)(2,1)S(1)}, u32[]{:S(2)}, u32[]{:S(2)}) %collective-permute-start.16) | collective-permute-done | bytes 262176 | tf_op jit(solution)/shard_map/output_weights/ppermute | solution.py:58
  132.8 13.1 %collective-permute-done.36 = bf16[1,2,64,2048]{3,2,1,0:T(8,128)(2,1)S(1)} collective-permute-done((bf16[1,2,64,2048]{3,2,1,0:T(8,128)(2,1)S(1)}, bf16[1,2,64,2048]{3,2,1,0:T(8,128)(2,1)S(1)}, u32[]{:S(2)}, u32[]{:S(2)}) %collective-permute-start.36) | collective-permute-done | bytes 524320 | tf_op jit(solution)/shard_map/cotangents/ppermute | solution.py:58
  152.4 18.6 %collective-permute-done.37 = bf16[2,2,64,2048]{3,2,1,0:T(8,128)(2,1)S(1)} collective-permute-done((bf16[2,2,64,2048]{3,2,1,0:T(8,128)(2,1)S(1)}, bf16[2,2,64,2048]{3,2,1,0:T(8,128)(2,1)S(1)}, u32[]{:S(2)}, u32[]{:S(2)}) %collective-permute-start.37) | collective-permute-done | bytes 1048608 | tf_op jit(solution)/shard_map/cotangents/ppermute | solution.py:58
  217.2 22.8 %collective-permute-start.30 = (bf16[1,64,2048]{2,1,0:T(8,128)(2,1)S(1)}, bf16[1,64,2048]{2,1,0:T(8,128)(2,1)S(1)}, u32[]{:S(2)}, u32[]{:S(2)}) collective-permute-start(bf16[1,64,2048]{2,1,0:T(8,128)(2,1)S(1)} %get-tuple-element.330), channel_id=1, source_target_pairs={{0,4},{1,5},{2,6},{3,7},{4,0},{5,1},{6,2},{7,3},{8,12},{9,13},{10,... | collective-permute-start | bytes 786440 | tf_op jit(solution)/shard_map/ffn_rows/ppermute | solution.py:58
  244.5 12.6 %collective-permute-start.31 = (bf16[2,64,2048]{2,1,0:T(8,128)(2,1)S(1)}, bf16[2,64,2048]{2,1,0:T(8,128)(2,1)S(1)}, u32[]{:S(2)}, u32[]{:S(2)}) collective-permute-start(bf16[2,64,2048]{2,1,0:T(8,128)(2,1)S(1)} %get-tuple-element.294), channel_id=1, source_target_pairs={{0,2},{1,3},{2,0},{3,1},{4,6},{5,7},{6,4},{7,5},{8,10},{9,11},{10,... | collective-permute-start | bytes 1572872 | tf_op jit(solution)/shard_map/ffn_rows/ppermute | solution.py:58
  257.4 16.3 %collective-permute-start.50 = (bf16[1,64,2048]{2,1,0:T(8,128)(2,1)S(1)}, bf16[1,64,2048]{2,1,0:T(8,128)(2,1)S(1)}, u32[]{:S(2)}, u32[]{:S(2)}) collective-permute-start(bf16[1,64,2048]{2,1,0:T(8,128)(2,1)S(1)} %get-tuple-element.288), channel_id=1, source_target_pairs={{0,4},{1,5},{2,6},{3,7},{4,0},{5,1},{6,2},{7,3},{8,12},{9,13},{10,... | collective-permute-start | bytes 786440 | tf_op jit(solution)/shard_map/ffn_rows/ppermute | solution.py:58
  280.1 15.6 %collective-permute-start.51 = (bf16[2,64,2048]{2,1,0:T(8,128)(2,1)S(1)}, bf16[2,64,2048]{2,1,0:T(8,128)(2,1)S(1)}, u32[]{:S(2)}, u32[]{:S(2)}) collective-permute-start(bf16[2,64,2048]{2,1,0:T(8,128)(2,1)S(1)} %get-tuple-element.298), channel_id=1, source_target_pairs={{0,2},{1,3},{2,0},{3,1},{4,6},{5,7},{6,4},{7,5},{8,10},{9,11},{10,... | collective-permute-start | bytes 1572872 | tf_op jit(solution)/shard_map/ffn_rows/ppermute | solution.py:58
  313.3 19.4 %collective-permute-done.32 = bf16[1,4,32,2048]{3,2,1,0:T(8,128)(2,1)S(1)} collective-permute-done((bf16[1,4,32,2048]{3,2,1,0:T(8,128)(2,1)S(1)}, bf16[1,4,32,2048]{3,2,1,0:T(8,128)(2,1)S(1)}, u32[]{:S(2)}, u32[]{:S(2)}) %collective-permute-start.32) | collective-permute-done | bytes 524320 | tf_op jit(solution)/shard_map/ffn_rows/ppermute | solution.py:58
  336.7 21.9 %collective-permute-done.35 = bf16[2,4,32,2048]{3,2,1,0:T(8,128)(2,1)S(1)} collective-permute-done((bf16[2,4,32,2048]{3,2,1,0:T(8,128)(2,1)S(1)}, bf16[2,4,32,2048]{3,2,1,0:T(8,128)(2,1)S(1)}, u32[]{:S(2)}, u32[]{:S(2)}) %collective-permute-start.35) | collective-permute-done | bytes 1048608 | tf_op jit(solution)/shard_map/ffn_rows/ppermute | solution.py:58
  413.5 29.4 %feed.4 = (bf16[4,4,64,2048]{3,2,1,0:T(8,128)(2,1)}, bf16[4,4,32,2048]{3,2,1,0:T(8,128)(2,1)}, bf16[4,4,32,2048]{3,2,1,0:T(8,128)(2,1)}, bf16[2,8,128,2048]{3,2,...) custom-call(s32[4,1,256]{2,1,0:T(1,128)} %get-tuple-element.338.refs, ...), custom_call_target="tpu_custom_call" | custom-call | flops 16000000000 | bytes 30000000 | tf_op jit(solution)/shard_map/feed/pallas_call | solution.py:589
  443.5 29.4 %feed.5 = (bf16[4,4,64,2048]{3,2,1,0:T(8,128)(2,1)}, bf16[4,4,32,2048]{3,2,1,0:T(8,128)(2,1)}, bf16[4,4,32,2048]{3,2,1,0:T(8,128)(2,1)}, bf16[2,8,128,2048]{3,2,...) custom-call(s32[4,1,256]{2,1,0:T(1,128)} %get-tuple-element.335.refs, ...), custom_call_target="tpu_custom_call", output_to_operand_aliasing={{3}: (11, {}), {4}: (12, {}), {5}: (13, {}), {6}: (14, {}),... | custom-call | flops 16000000000 | bytes 30000000 | tf_op jit(solution)/shard_map/feed/pallas_call | solution.py:589
  472.9 29.6 %feed.6 = (bf16[4,4,64,2048]{3,2,1,0:T(8,128)(2,1)}, bf16[4,4,32,2048]{3,2,1,0:T(8,128)(2,1)}, bf16[4,4,32,2048]{3,2,1,0:T(8,128)(2,1)}, bf16[2,8,128,2048]{3,2,...) custom-call(s32[4,1,256]{2,1,0:T(1,128)} %get-tuple-element.339.refs, ...), custom_call_target="tpu_custom_call", output_to_operand_aliasing={{3}: (11, {}), {4}: (12, {}), {5}: (13, {}), {6}: (14, {}),... | custom-call | flops 16000000000 | bytes 30000000 | tf_op jit(solution)/shard_map/feed/pallas_call | solution.py:589
  502.5 29.5 %feed.7 = (bf16[4,4,64,2048]{3,2,1,0:T(8,128)(2,1)}, bf16[4,4,32,2048]{3,2,1,0:T(8,128)(2,1)}, bf16[4,4,32,2048]{3,2,1,0:T(8,128)(2,1)}, bf16[2,8,128,2048]{3,2,...) custom-call(s32[4,1,256]{2,1,0:T(1,128)} %get-tuple-element.334.refs, ...), custom_call_target="tpu_custom_call", output_to_operand_aliasing={{3}: (11, {}), {4}: (12, {}), {5}: (13, {}), {6}: (14, {}),... | custom-call | flops 16000000000 | bytes 30000000 | tf_op jit(solution)/shard_map/feed/pallas_call | solution.py:589
  592.2 17.1 %collective-permute-done.67 = bf16[2,4,32,2048]{3,2,1,0:T(8,128)(2,1)S(1)} collective-permute-done((bf16[2,4,32,2048]{3,2,1,0:T(8,128)(2,1)S(1)}, bf16[2,4,32,2048]{3,2,1,0:T(8,128)(2,1)S(1)}, u32[]{:S(2)}, u32[]{:S(2)}) %collective-permute-start.67) | collective-permute-done | bytes 1048608 | tf_op jit(solution)/shard_map/ffn_grads/ppermute | solution.py:58
  615.1 15.7 %collective-permute-done.75 = bf16[2,4,32,2048]{3,2,1,0:T(8,128)(2,1)S(1)} collective-permute-done((bf16[2,4,32,2048]{3,2,1,0:T(8,128)(2,1)S(1)}, bf16[2,4,32,2048]{3,2,1,0:T(8,128)(2,1)S(1)}, u32[]{:S(2)}, u32[]{:S(2)}) %collective-permute-start.75) | collective-permute-done | bytes 1048608 | tf_op jit(solution)/shard_map/ffn_grads/ppermute | solution.py:58
  666.2 15.0 %collective-permute-done.80 = bf16[2,64,2048]{2,1,0:T(8,128)(2,1)S(1)} collective-permute-done((bf16[2,64,2048]{2,1,0:T(8,128)(2,1)S(1)}, bf16[2,64,2048]{2,1,0:T(8,128)(2,1)S(1)}, u32[]{:S(2)}, u32[]{:S(2)}) %collective-permute-start.80) | collective-permute-done | bytes 524320 | tf_op jit(solution)/shard_map/ffn_grads/ppermute | solution.py:58
  681.5 12.0 %collective-permute-done.81 = bf16[1,64,2048]{2,1,0:T(8,128)(2,1)S(1)} collective-permute-done((bf16[1,64,2048]{2,1,0:T(8,128)(2,1)S(1)}, bf16[1,64,2048]{2,1,0:T(8,128)(2,1)S(1)}, u32[]{:S(2)}, u32[]{:S(2)}) %collective-permute-start.81) | collective-permute-done | bytes 262176 | tf_op jit(solution)/shard_map/ffn_grads/ppermute | solution.py:58
  712.9 47.7 %collective-permute-done.85 = bf16[2,64,2048]{2,1,0:T(8,128)(2,1)} collective-permute-done((bf16[2,64,2048]{2,1,0:T(8,128)(2,1)}, bf16[2,64,2048]{2,1,0:T(8,128)(2,1)}, u32[]{:S(2)}, u32[]{:S(2)}) %collective-permute-start.85) | collective-permute-done | bytes 524320 | tf_op jit(solution)/shard_map/attention_grads/ppermute | solution.py:58
  764.9 23.0 %attend_back.1 = (bf16[256,2048]{1,0:T(8,128)(2,1)}, bf16[4,4,64,576]{3,2,1,0:T(8,128)(2,1)}, bf16[4,4,64,576]{3,2,1,0:T(8,128)(2,1)}, bf16[256,2048]{1,0:T(8,12...) custom-call(s32[1]{0:T(128)} %bitcast.1.s_ref.refs_0_, ...), custom_call_target="tpu_custom_call" | custom-call | flops 24000000000 | bytes 30000000 | tf_op jit(solution)/shard_map/attend_back/pallas_call | solution.py:457
  828.9 21.7 %collective-permute-start.115 = (bf16[1,64,1024]{2,1,0:T(8,128)(2,1)S(1)}, bf16[1,64,1024]{2,1,0:T(8,128)(2,1)S(1)}, u32[]{:S(2)}, u32[]{:S(2)}) collective-permute-start(bf16[1,64,1024]{2,1,0:T(8,128)(2,1)S(1)} %slice_bitcast_fusion.28), channel_id=1, source_target_pairs={{0,4},{1,5},{2,6},{3,7},{4,0},{5,1},{6,2},{7,3},{8,12},{9,13},{10,... | collective-permute-start | bytes 393224 | tf_op jit(solution)/shard_map/expand_grads/ppermute | solution.py:58
  890.2 12.5 %collective-permute-done.96 = bf16[2,4,64,576]{3,2,1,0:T(8,128)(2,1)} collective-permute-done((bf16[2,4,64,576]{3,2,1,0:T(8,128)(2,1)}, bf16[2,4,64,576]{3,2,1,0:T(8,128)(2,1)}, u32[]{:S(2)}, u32[]{:S(2)}) %collective-permute-start.96) | collective-permute-done | bytes 589856 | tf_op jit(solution)/shard_map/key_grads/ppermute | solution.py:58
  935.6 20.8 %collective-permute-done.99 = bf16[1,2,64,576]{3,2,1,0:T(8,128)(2,1)S(1)} collective-permute-done((bf16[1,2,64,576]{3,2,1,0:T(8,128)(2,1)S(1)}, bf16[1,2,64,576]{3,2,1,0:T(8,128)(2,1)S(1)}, u32[]{:S(2)}, u32[]{:S(2)}) %collective-permute-start.99) | collective-permute-done | bytes 147488 | tf_op jit(solution)/shard_map/key_grads/ppermute | solution.py:58
  989.0 16.1 %collective-permute-done.109 = bf16[1,160,256]{2,1,0:T(8,128)(2,1)S(1)} collective-permute-done((bf16[1,160,256]{2,1,0:T(8,128)(2,1)S(1)}, bf16[1,160,256]{2,1,0:T(8,128)(2,1)S(1)}, u32[]{:S(2)}, u32[]{:S(2)}) %collective-permute-start.109) | collective-permute-done | bytes 81952 | tf_op jit(solution)/shard_map/latent_grads/ppermute | solution.py:58
  (778 shorter events, 515.5 us)
Async XLA Ops:
  83.1 47.1 %collective-permute-start.12 = (bf16[2,256,768]{2,1,0:T(8,128)(2,1)}, bf16[2,256,768]{2,1,0:T(8,128)(2,1)}, u32[]{:S(2)}, u32[]{:S(2)}) collective-permute-start(bf16[2,256,768]{2,1,0:T(8,128)(2,1)} %get-tuple-element.270), channel_id=1, source_target_pairs={{0,2},{1,3},{2,0},{3,1},{4,6},{5,7},{6,4},{7,5},{8,10},{9,11},{10,... | collective-permute-start | bytes 2359304 | tf_op jit(solution)/shard_map/query_weights/ppermute | solution.py:58
  210.4 63.2 %collective-permute-start.56 = (bf16[1,4,64,2048]{3,2,1,0:T(8,128)(2,1)S(1)}, bf16[1,4,64,2048]{3,2,1,0:T(8,128)(2,1)S(1)}, u32[]{:S(2)}, u32[]{:S(2)}) collective-permute-start(bf16[1,4,64,2048]{3,2,1,0:T(8,128)(2,1)S(1)} %get-tuple-element.232), channel_id=1, source_target_pairs={{0,16},{8,24},{16,0},{24,8},{1,17},{9,25},{17,1},{25,9},{2,18},{10... | collective-permute-start | bytes 3145736 | tf_op jit(solution)/shard_map/cotangents/ppermute | solution.py:58
  240.2 69.0 %collective-permute-start.39 = (bf16[2,4,64,2048]{3,2,1,0:T(8,128)(2,1)S(1)}, bf16[2,4,64,2048]{3,2,1,0:T(8,128)(2,1)S(1)}, u32[]{:S(2)}, u32[]{:S(2)}) collective-permute-start(bf16[2,4,64,2048]{3,2,1,0:T(8,128)(2,1)S(1)} %pad_maximum_fusion.4), channel_id=1, source_target_pairs={{0,16},{8,24},{16,0},{24,8},{1,17},{9,25},{17,1},{25,9},{2,18},{10... | collective-permute-start | bytes 6291464 | tf_op jit(solution)/shard_map/cotangents/ppermute | solution.py:58
  244.5 51.3 %collective-permute-start.31 = (bf16[2,64,2048]{2,1,0:T(8,128)(2,1)S(1)}, bf16[2,64,2048]{2,1,0:T(8,128)(2,1)S(1)}, u32[]{:S(2)}, u32[]{:S(2)}) collective-permute-start(bf16[2,64,2048]{2,1,0:T(8,128)(2,1)S(1)} %get-tuple-element.294), channel_id=1, source_target_pairs={{0,2},{1,3},{2,0},{3,1},{4,6},{5,7},{6,4},{7,5},{8,10},{9,11},{10,... | collective-permute-start | bytes 1572872 | tf_op jit(solution)/shard_map/ffn_rows/ppermute | solution.py:58
  257.3 77.2 %collective-permute-start.41 = (bf16[2,3,88,256]{3,2,0,1:T(8,128)(2,1)S(1)}, bf16[2,3,88,256]{3,2,0,1:T(8,128)(2,1)S(1)}, u32[]{:S(2)}, u32[]{:S(2)}) collective-permute-start(bf16[2,3,88,256]{3,2,0,1:T(8,128)(2,1)S(1)} %get-tuple-element.243), channel_id=1, source_target_pairs={{0,2},{1,3},{2,0},{3,1},{4,6},{5,7},{6,4},{7,5},{8,10},{9,11},{10,... | collective-permute-start | bytes 811016 | tf_op jit(solution)/shard_map/shared_weights/ppermute | solution.py:58
  273.8 100.6 %collective-permute-start.57 = (bf16[2,4,64,2048]{3,2,1,0:T(8,128)(2,1)S(1)}, bf16[2,4,64,2048]{3,2,1,0:T(8,128)(2,1)S(1)}, u32[]{:S(2)}, u32[]{:S(2)}) collective-permute-start(bf16[2,4,64,2048]{3,2,1,0:T(8,128)(2,1)S(1)} %pad_maximum_fusion.7), channel_id=1, source_target_pairs={{0,8},{8,0},{16,24},{24,16},{1,9},{9,1},{17,25},{25,17},{2,10},{10... | collective-permute-start | bytes 6291464 | tf_op jit(solution)/shard_map/cotangents/ppermute | solution.py:58
  311.5 102.0 %collective-permute-start.46 = (bf16[4,4,64,2048]{3,2,1,0:T(8,128)(2,1)}, bf16[4,4,64,2048]{3,2,1,0:T(8,128)(2,1)}, u32[]{:S(2)}, u32[]{:S(2)}) collective-permute-start(bf16[4,4,64,2048]{3,2,1,0:T(8,128)(2,1)} %pad_maximum_fusion.refs_4_), channel_id=1, source_target_pairs={{0,1},{1,0},{2,3},{3,2},{4,5},{5,4},{6,7},{7,6},{8,9},{9,8},{10,11... | collective-permute-start | bytes 12582920 | tf_op jit(solution)/shard_map/cotangents/ppermute | solution.py:58
  363.7 49.3 %collective-permute-start.45 = (bf16[4,4,32,2048]{3,2,1,0:T(8,128)(2,1)}, bf16[4,4,32,2048]{3,2,1,0:T(8,128)(2,1)}, u32[]{:S(2)}, u32[]{:S(2)}) collective-permute-start(bf16[4,4,32,2048]{3,2,1,0:T(8,128)(2,1)} %pad_maximum_fusion.3.refs_3_), channel_id=1, source_target_pairs={{0,1},{1,0},{2,3},{3,2},{4,5},{5,4},{6,7},{7,6},{8,9},{9,8},{10,11... | collective-permute-start | bytes 6291464 | tf_op jit(solution)/shard_map/ffn_rows/ppermute | solution.py:58
  394.7 78.2 %collective-permute-start.60 = (bf16[4,4,64,2048]{3,2,1,0:T(8,128)(2,1)}, bf16[4,4,64,2048]{3,2,1,0:T(8,128)(2,1)}, u32[]{:S(2)}, u32[]{:S(2)}) collective-permute-start(bf16[4,4,64,2048]{3,2,1,0:T(8,128)(2,1)} %pad_maximum_fusion.1.refs_4_), channel_id=1, source_target_pairs={{0,1},{1,0},{2,3},{3,2},{4,5},{5,4},{6,7},{7,6},{8,9},{9,8},{10,11... | collective-permute-start | bytes 12582920 | tf_op jit(solution)/shard_map/cotangents/ppermute | solution.py:58
  410.2 62.7 %collective-permute-start.59 = (bf16[4,4,32,2048]{3,2,1,0:T(8,128)(2,1)}, bf16[4,4,32,2048]{3,2,1,0:T(8,128)(2,1)}, u32[]{:S(2)}, u32[]{:S(2)}) collective-permute-start(bf16[4,4,32,2048]{3,2,1,0:T(8,128)(2,1)} %pad_maximum_fusion.6.refs_3_), channel_id=1, source_target_pairs={{0,1},{1,0},{2,3},{3,2},{4,5},{5,4},{6,7},{7,6},{8,9},{9,8},{10,11... | collective-permute-start | bytes 6291464 | tf_op jit(solution)/shard_map/ffn_rows/ppermute | solution.py:58
  413.0 59.9 %collective-permute-start.58 = (bf16[4,4,32,2048]{3,2,1,0:T(8,128)(2,1)}, bf16[4,4,32,2048]{3,2,1,0:T(8,128)(2,1)}, u32[]{:S(2)}, u32[]{:S(2)}) collective-permute-start(bf16[4,4,32,2048]{3,2,1,0:T(8,128)(2,1)} %pad_maximum_fusion.5.refs_2_), channel_id=1, source_target_pairs={{0,1},{1,0},{2,3},{3,2},{4,5},{5,4},{6,7},{7,6},{8,9},{9,8},{10,11... | collective-permute-start | bytes 6291464 | tf_op jit(solution)/shard_map/ffn_rows/ppermute | solution.py:58
  442.9 136.9 %collective-permute-start.66 = (bf16[4,4,32,2048]{3,2,1,0:T(8,128)(2,1)}, bf16[4,4,32,2048]{3,2,1,0:T(8,128)(2,1)}, u32[]{:S(2)}, u32[]{:S(2)}) collective-permute-start(bf16[4,4,32,2048]{3,2,1,0:T(8,128)(2,1)} %get-tuple-element.110), channel_id=1, source_target_pairs={{0,1},{1,0},{2,3},{3,2},{4,5},{5,4},{6,7},{7,6},{8,9},{9,8},{10,11... | collective-permute-start | bytes 6291464 | tf_op jit(solution)/shard_map/ffn_grads/ppermute | solution.py:58
  443.0 140.2 %collective-permute-start.69 = (bf16[4,4,32,2048]{3,2,1,0:T(8,128)(2,1)}, bf16[4,4,32,2048]{3,2,1,0:T(8,128)(2,1)}, u32[]{:S(2)}, u32[]{:S(2)}) collective-permute-start(bf16[4,4,32,2048]{3,2,1,0:T(8,128)(2,1)} %get-tuple-element.112), channel_id=1, source_target_pairs={{0,1},{1,0},{2,3},{3,2},{4,5},{5,4},{6,7},{7,6},{8,9},{9,8},{10,11... | collective-permute-start | bytes 6291464 | tf_op jit(solution)/shard_map/ffn_grads/ppermute | solution.py:58
  577.1 119.5 %collective-permute-start.61 = (bf16[4,4,64,2048]{3,2,1,0:T(8,128)(2,1)}, bf16[4,4,64,2048]{3,2,1,0:T(8,128)(2,1)S(1)}, u32[]{:S(2)}, u32[]{:S(2)}) collective-permute-start(bf16[4,4,64,2048]{3,2,1,0:T(8,128)(2,1)} %get-tuple-element.108), channel_id=1, source_target_pairs={{0,1},{1,0},{2,3},{3,2},{4,5},{5,4},{6,7},{7,6},{8,9},{9,8},{10,11... | collective-permute-start | bytes 12582920 | tf_op jit(solution)/shard_map/outputs/ppermute | solution.py:58
  579.7 127.1 %collective-permute-start.47 = (bf16[4,4,64,2048]{3,2,1,0:T(8,128)(2,1)}, bf16[4,4,64,2048]{3,2,1,0:T(8,128)(2,1)S(1)}, u32[]{:S(2)}, u32[]{:S(2)}) collective-permute-start(bf16[4,4,64,2048]{3,2,1,0:T(8,128)(2,1)} %get-tuple-element.96), channel_id=1, source_target_pairs={{0,1},{1,0},{2,3},{3,2},{4,5},{5,4},{6,7},{7,6},{8,9},{9,8},{10,11... | collective-permute-start | bytes 12582920 | tf_op jit(solution)/shard_map/outputs/ppermute | solution.py:58
  702.0 152.2 %collective-permute-start.62 = (bf16[2,4,64,2048]{3,2,1,0:T(8,128)(2,1)}, bf16[2,4,64,2048]{3,2,1,0:T(8,128)(2,1)}, u32[]{:S(2)}, u32[]{:S(2)}) collective-permute-start(bf16[2,4,64,2048]{3,2,1,0:T(8,128)(2,1)} %slice.754), channel_id=1, source_target_pairs={{0,8},{8,0},{16,24},{24,16},{1,9},{9,1},{17,25},{25,17},{2,10},{10... | collective-permute-start | bytes 6291464 | tf_op jit(solution)/shard_map/outputs/ppermute | solution.py:58
  703.8 56.8 %collective-permute-start.85 = (bf16[2,64,2048]{2,1,0:T(8,128)(2,1)}, bf16[2,64,2048]{2,1,0:T(8,128)(2,1)}, u32[]{:S(2)}, u32[]{:S(2)}) collective-permute-start(bf16[2,64,2048]{2,1,0:T(8,128)(2,1)} %pad_maximum_fusion.45), channel_id=1, source_target_pairs={{0,8},{8,0},{16,24},{24,16},{1,9},{9,1},{17,25},{25,17},{2,10},{10... | collective-permute-start | bytes 1572872 | tf_op jit(solution)/shard_map/attention_grads/ppermute | solution.py:58
  705.8 56.9 %collective-permute-start.83 = (bf16[2,64,2048]{2,1,0:T(8,128)(2,1)}, bf16[2,64,2048]{2,1,0:T(8,128)(2,1)}, u32[]{:S(2)}, u32[]{:S(2)}) collective-permute-start(bf16[2,64,2048]{2,1,0:T(8,128)(2,1)} %pad_maximum_fusion.44), channel_id=1, source_target_pairs={{0,16},{8,24},{16,0},{24,8},{1,17},{9,25},{17,1},{25,9},{2,18},{10... | collective-permute-start | bytes 1572872 | tf_op jit(solution)/shard_map/attention_grads/ppermute | solution.py:58
  711.9 146.6 %collective-permute-start.48 = (bf16[2,4,64,2048]{3,2,1,0:T(8,128)(2,1)}, bf16[2,4,64,2048]{3,2,1,0:T(8,128)(2,1)}, u32[]{:S(2)}, u32[]{:S(2)}) collective-permute-start(bf16[2,4,64,2048]{3,2,1,0:T(8,128)(2,1)} %slice.743), channel_id=1, source_target_pairs={{0,16},{8,24},{16,0},{24,8},{1,17},{9,25},{17,1},{25,9},{2,18},{10... | collective-permute-start | bytes 6291464 | tf_op jit(solution)/shard_map/outputs/ppermute | solution.py:58
  824.5 41.2 %collective-permute-start.95 = (bf16[4,4,64,576]{3,2,1,0:T(8,128)(2,1)S(1)}, bf16[4,4,64,576]{3,2,1,0:T(8,128)(2,1)S(1)}, u32[]{:S(2)}, u32[]{:S(2)}) collective-permute-start(bf16[4,4,64,576]{3,2,1,0:T(8,128)(2,1)S(1)} %copy-done.90), channel_id=1, source_target_pairs={{0,1},{1,0},{2,3},{3,2},{4,5},{5,4},{6,7},{7,6},{8,9},{9,8},{10,11... | collective-permute-start | bytes 3538952 | tf_op jit(solution)/shard_map/key_grads/ppermute | solution.py:58
  824.6 44.9 %collective-permute-start.92 = (bf16[4,4,64,576]{3,2,1,0:T(8,128)(2,1)S(1)}, bf16[4,4,64,576]{3,2,1,0:T(8,128)(2,1)S(1)}, u32[]{:S(2)}, u32[]{:S(2)}) collective-permute-start(bf16[4,4,64,576]{3,2,1,0:T(8,128)(2,1)S(1)} %copy-done.89), channel_id=1, source_target_pairs={{0,1},{1,0},{2,3},{3,2},{4,5},{5,4},{6,7},{7,6},{8,9},{9,8},{10,11... | collective-permute-start | bytes 3538952 | tf_op jit(solution)/shard_map/key_grads/ppermute | solution.py:58
  858.5 58.8 %collective-permute-start.63 = (bf16[1,4,64,2048]{3,2,1,0:T(8,128)(2,1)}, bf16[1,4,64,2048]{3,2,1,0:T(8,128)(2,1)}, u32[]{:S(2)}, u32[]{:S(2)}) collective-permute-start(bf16[1,4,64,2048]{3,2,1,0:T(8,128)(2,1)} %slice.756), channel_id=1, source_target_pairs={{0,16},{8,24},{16,0},{24,8},{1,17},{9,25},{17,1},{25,9},{2,18},{10... | collective-permute-start | bytes 3145736 | tf_op jit(solution)/shard_map/outputs/ppermute | solution.py:58
  863.4 55.7 %collective-permute-start.49 = (bf16[1,4,64,2048]{3,2,1,0:T(8,128)(2,1)}, bf16[1,4,64,2048]{3,2,1,0:T(8,128)(2,1)}, u32[]{:S(2)}, u32[]{:S(2)}) collective-permute-start(bf16[1,4,64,2048]{3,2,1,0:T(8,128)(2,1)} %slice.745), channel_id=1, source_target_pairs={{0,8},{8,0},{16,24},{24,16},{1,9},{9,1},{17,25},{25,17},{2,10},{10... | collective-permute-start | bytes 3145736 | tf_op jit(solution)/shard_map/outputs/ppermute | solution.py:58
  922.0 59.1 %collective-permute-start.64 = (bf16[2,2,64,2048]{3,2,1,0:T(8,128)(2,1)}, bf16[2,2,64,2048]{3,2,1,0:T(8,128)(2,1)}, u32[]{:S(2)}, u32[]{:S(2)}) collective-permute-start(bf16[2,2,64,2048]{3,2,1,0:T(8,128)(2,1)} %bitcast.588), channel_id=1, source_target_pairs={{0,2},{1,3},{2,0},{3,1},{4,6},{5,7},{6,4},{7,5},{8,10},{9,11},{10,... | collective-permute-start | bytes 3145736 | tf_op jit(solution)/shard_map/outputs/ppermute | solution.py:58
  (198 other events, 3586.5 us)

commit v2 on v1

v2 whole, which is shorter than its diff:
```python
import functools

import jax
import jax.numpy as jnp
from jax import lax
from jax.experimental import pallas as pl
from jax.experimental.pallas import tpu as pltpu
from jax.sharding import PartitionSpec as P

HDIM = 128
RDIM = 64
RANK = 512
TOPK = 6
BLOCK = 256
QDIM = 192
HALF = RDIM // 2
EPSILON = 1e-06
ROPE_BASE = 10000.0
NEG_LARGE = -1e30
LOG2E = 1.4426950408889634
SCALE = QDIM ** (-0.5)
WIDE = -(-(RANK + RDIM) // 128) * 128
F32 = jnp.float32
BF16 = jnp.bfloat16
MIB = 1024 * 1024


def dot(a, b):
    return lax.dot_general(a, b, (((1,), (0,)), ((), ())), preferred_element_type=F32)


def dot_nt(a, b):
    return lax.dot_general(a, b, (((1,), (1,)), ((), ())), preferred_element_type=F32)


def dot_tn(a, b):
    return lax.dot_general(a, b, (((0,), (0,)), ((), ())), preferred_element_type=F32)


def rms_inverse(values):
    return lax.rsqrt(jnp.mean(values * values, axis=-1, keepdims=True) + EPSILON)


def rope_tables(positions):
    frequency = ROPE_BASE ** (-jnp.arange(HALF, dtype=F32) / HALF)
    angles = positions.astype(F32)[:, None] * frequency[None, :]
    return (jnp.cos(angles), jnp.sin(angles))


def norm_back(grad_normed, hat_rows, inverse, gain_vec):
    scaled = grad_normed * gain_vec
    gain_term = jnp.sum(grad_normed * hat_rows, axis=(0, 1))
    grad_rows = inverse * (scaled - hat_rows * jnp.mean(scaled * hat_rows, axis=-1, keepdims=True))
    return (grad_rows, gain_term)


def swap(value, axis, mask):
    size = lax.axis_size(axis)
    return lax.ppermute(value, axis, [(i, i ^ mask) for i in range(size)])


def depth():
    return lax.axis_size("seq") // 2


def line_pieces(value):
    return [value] + [swap(value, "seq", 2 * k) for k in range(1, depth())]


def plane_pieces(value):
    return [value] + [swap(value, "head", r) for r in range(1, lax.axis_size("head"))]


def core_pieces(values):
    return values, [swap(v, "seq", 1) for v in values]


def line_sum(values):
    total = values[0].astype(F32)
    for k in range(1, depth()):
        total = total + swap(values[k], "seq", 2 * k).astype(F32)
    return total


def plane_sum(values):
    total = values[0].astype(F32)
    for r in range(1, lax.axis_size("head")):
        total = total + swap(values[r], "head", r).astype(F32)
    return total


def pick(value, index, axis=0):
    return lax.dynamic_index_in_dim(value, index, axis, keepdims=False)


def any_spec():
    return [pl.BlockSpec(memory_space=pl.ANY)]


def after(value, *others):
    return pl.pallas_call(
        lambda *refs: None,
        out_shape=jax.ShapeDtypeStruct(value.shape, value.dtype),
        in_specs=any_spec() * (1 + len(others)),
        out_specs=any_spec()[0],
        input_output_aliases={0: 0},
        name="after",
    )(value, *others)


def sync(*values):
    return pl.pallas_call(
        lambda *refs: None,
        out_shape=tuple(jax.ShapeDtypeStruct(v.shape, v.dtype) for v in values),
        in_specs=any_spec() * len(values),
        out_specs=tuple(any_spec() * len(values)),
        input_output_aliases={i: i for i in range(len(values))},
        name="sync",
    )(*values)


def bits_of(size):
    return [1 << i for i in range(size.bit_length() - 1)]


def plane_order(flip):
    bits = bits_of(lax.axis_size("head"))
    order = [0]
    for bit in bits[::-1] if flip else bits:
        order = order + [i | bit for i in order]
    return order


class Spread:
    def __init__(self, name, value):
        self.name, self.held, self.rest = name, value[None], self.plan()

    def send(self):
        with jax.named_scope(self.name):
            self.got = swap(self.held, self.axis, self.rest[0])
        return [self.got]

    def take(self, got):
        self.rest = self.rest[1:]
        with jax.named_scope(self.name):
            self.held = self.join(self.held, got[0])
        return self

    @property
    def more(self):
        return bool(self.rest)


class Line(Spread):
    axis = "seq"

    def plan(self):
        return [2 * bit for bit in bits_of(depth())[::-1]]

    def join(self, held, got):
        return jnp.stack([held, got], axis=1).reshape((-1,) + held.shape[1:])


class Plane:
    def __init__(self, name, first, second):
        self.name, self.held = name, [first[None], second[None]]
        self.rest = bits_of(lax.axis_size("head"))

    def send(self):
        count = len(self.rest)
        with jax.named_scope(self.name):
            masks = (self.rest[0], bits_of(lax.axis_size("head"))[count - 1])
            return [swap(v, "head", m) for v, m in zip(self.held, masks)]

    def take(self, got):
        self.rest = self.rest[1:]
        if not self.rest:
            self.held = [v for pair in zip(self.held, got) for v in pair]
            return self
        with jax.named_scope(self.name):
            self.held = [jnp.concatenate([v, g], axis=0) for v, g in zip(self.held, got)]
        return self

    @property
    def more(self):
        return bool(self.rest)


def add_halves(first, second):
    half = first.shape[0] // 2
    return [
        (first[i].astype(F32) + second[i].astype(F32)).astype(BF16)
        for i in (slice(0, half), slice(half, None))
    ]


class PlaneSum:
    def __init__(self, name, *halves):
        self.name, self.held, self.left = name, halves, len(bits_of(lax.axis_size("head")))

    def send(self):
        bits = bits_of(lax.axis_size("head"))
        masks = (bits[self.left - 1], bits[len(bits) - self.left])
        with jax.named_scope(self.name):
            return [swap(sent, "head", m) for (_, sent), m in zip(self.held, masks)]

    def take(self, got):
        self.left -= 1
        with jax.named_scope(self.name):
            if self.left:
                self.held = [add_halves(kept, g) for (kept, _), g in zip(self.held, got)]
            else:
                self.held = [
                    (kept.astype(F32) + g.astype(F32)).astype(BF16)[0]
                    for (kept, _), g in zip(self.held, got)
                ]
        return self

    @property
    def more(self):
        return self.left > 0


class LineSum:
    def __init__(self, name, value):
        self.name, self.held, self.rest = name, value, bits_of(depth())

    def send(self):
        pairs = self.held.reshape((-1, 2) + self.held.shape[1:])
        self.kept = pairs[:, 0]
        with jax.named_scope(self.name):
            return [swap(pairs[:, 1], "seq", 2 * self.rest[0])]

    def take(self, got):
        self.rest = self.rest[1:]
        with jax.named_scope(self.name):
            self.held = self.kept.astype(F32) + got[0].astype(F32)
            if self.rest:
                self.held = self.held.astype(BF16)
            else:
                self.held = self.held[0]
        return self

    @property
    def more(self):
        return bool(self.rest)


class Sends:
    def __init__(self, name, values, axis, masks):
        self.name, self.values, self.axis, self.masks = name, values, axis, masks
        self.more = True

    def send(self):
        with jax.named_scope(self.name):
            return [swap(v, self.axis, m) for v, m in zip(self.values, self.masks)]

    def take(self, got):
        self.more = False
        self.held = list(got)
        return self


def core_send(name, values):
    return Sends(name, values, "seq", [1] * len(values))


def head_send(name, values):
    return Sends(name, values, "head", list(range(1, lax.axis_size("head"))))


class Phase:
    def __init__(self, *flows):
        self.flows = [flow for flow in flows if flow is not None and flow.more]
        self.sent = [flow.send() for flow in self.flows]

    def end(self, *others):
        flat = [v for got in self.sent for v in got] + list(others)
        flat = list(sync(*flat))
        for flow, got in zip(self.flows, self.sent):
            flow.take([flat.pop(0) for _ in got])
        return flat


def run(*flows):
    while any(flow.more for flow in flows):
        Phase(*flows).end()
    return [flow.held for flow in flows]


def take(refs, count):
    return [refs.pop(0) for _ in range(count)]


def part_places(here, own, other, size):
    return [
        ((ref, line), pl.multiple_of((here ^ (2 * line + core)) * size, size))
        for core, ref in enumerate((own, other))
        for line in range(ref.shape[0])
    ]


class Pack:
    def __init__(self, size, heads, seq_count):
        self.size, self.rank = size, RANK // seq_count
        self.query_parts = heads * QDIM // size
        self.expand_parts = 2 * heads * HDIM // size
        self.expand_at = self.query_parts * size
        self.out_at = self.expand_at + self.expand_parts * self.rank
        self.out_rows = heads * HDIM
        self.rows = self.out_at + self.out_rows

    def query(self, ref, part):
        array, line = ref
        return array[line, part * self.size : (part + 1) * self.size, :]

    def expand(self, ref, part):
        array, line = ref
        at = part * self.rank
        return array[line, at : at + self.rank, :]

    def out(self, ref):
        array, line = ref
        return array[line, : self.out_rows, :]


def latent_kernel(plane, s_ref, x_ref, cos, sin, *refs):
    refs = list(refs)
    own, other = take(refs, plane), take(refs, plane)
    keys_out, lat_out, gattn_out, gffn_out, glat_out, wide_out, full = refs
    here, column = s_ref[0], s_ref[1]
    rows = RANK + RDIM
    lines, each, size = own[0].shape
    for core, group in enumerate((own, other)):
        for line in range(lines):
            place = pl.multiple_of((here ^ (2 * line + core)) * size, size)
            for r, ref in enumerate(group):
                top = pl.multiple_of((column ^ r) * each, 16)
                full[pl.ds(top, each), pl.ds(place, size)] = ref[line]
    x = x_ref[...].astype(F32)
    gains = full[rows : rows + 16, :].astype(F32)
    gattn_out[...] = gains[0:1]
    gffn_out[...] = gains[1:2]
    spread = gains[2 : 2 + RANK // size]
    glat = spread[:, :size]
    for i in range(1, 2 * lines):
        glat = glat + spread[:, i * size : (i + 1) * size]
    glat = jnp.concatenate([glat[i : i + 1] for i in range(RANK // size)], axis=1)
    glat_out[...] = glat
    normed = (x * rms_inverse(x) * gains[0:1]).astype(BF16)
    wide_out[...] = full[:rows, :]
    low = dot_nt(normed, wide_out[...]).astype(BF16)
    lat_out[...] = low
    low = low.astype(F32)
    comp = low[:, :RANK]
    comp = comp * rms_inverse(comp) * glat
    first, second = low[:, RANK : RANK + HALF], low[:, RANK + HALF :]
    keys_out[...] = jnp.concatenate(
        [
            comp,
            first * cos[...] - second * sin[...],
            first * sin[...] + second * cos[...],
            jnp.zeros((x.shape[0], WIDE - RANK - RDIM), F32),
        ],
        axis=1,
    ).astype(BF16)


def block_scores(query, keys, masks):
    scores = dot_nt(query, keys)
    if masks is not None:
        scores = jnp.where(masks, scores, NEG_LARGE)
    return scores


def entry(pair, order, r):
    half, j = divmod(order.index(r), len(order) // 2)
    return pair[half], j


def load_keys(pair, order, line):
    found = [entry(pair, order, r) for r in range(len(order))]
    return jnp.concatenate([ref[j, line] for ref, j in found], axis=0)


def fill_expand(here, own, other, wexp, pack):
    for ref, place in part_places(here, own, other, pack.rank):
        for part in range(pack.expand_parts):
            columns = slice(part * pack.size, (part + 1) * pack.size)
            wexp[pl.ds(place, pack.rank), columns] = pack.expand(ref, part)


def attend_masked(here, heads, order, lines, key_refs, wexp, q_out, state, qblk_ref, kblk_ref):
    acc, mx, sm = state
    group = q_out.shape[1]
    for core, ref in enumerate(key_refs):

        def step(line, carry, core=core, ref=ref):
            @pl.when((here ^ (2 * line + core)) <= here)
            def _():
                latent = load_keys(ref, order, line)
                expanded = dot(latent[:, :RANK], wexp[...]).astype(BF16)
                rope_key = latent[:, RANK : RANK + RDIM]
                allowed = kblk_ref[pl.ds(2 * line + core, 1), :] <= qblk_ref[...]
                for h in range(heads):
                    keys = jnp.concatenate(
                        [expanded[:, 2 * h * HDIM : (2 * h + 1) * HDIM], rope_key], axis=1
                    )
                    vals = expanded[:, (2 * h + 1) * HDIM : (2 * h + 2) * HDIM]
                    scores = block_scores(q_out[h], keys, allowed)
                    old = mx[h][:, :1]
                    new = jnp.maximum(old, jnp.max(scores, axis=1, keepdims=True))
                    weights = jnp.exp2((scores - new) * (SCALE * LOG2E))
                    weights = jnp.where(allowed, weights, 0.0)
                    rescale = jnp.exp2((old - new) * (SCALE * LOG2E))
                    sm[h] = sm[h] * rescale + jnp.sum(weights, axis=1, keepdims=True)
                    acc[h] = acc[h] * rescale + dot(weights.astype(BF16), vals)
                    mx[h] = jnp.broadcast_to(new, (group, HDIM))

            return carry

        lax.fori_loop(0, lines, step, 0)


def attend_whole(here, heads, order, lines, key_refs, wexp, q_out, state, all_scores, all_vals):
    acc, mx, sm = state
    wide = mx.shape[2]

    def each_block(body):
        for core, ref in enumerate(key_refs):

            def step(line, carry, core=core, ref=ref):
                @pl.when((here ^ (2 * line + core)) <= here)
                def _():
                    body(2 * line + core, ref, line)

                return carry

            lax.fori_loop(0, lines, step, 0)

    def score(place, ref, line):
        latent = load_keys(ref, order, line)
        expanded = dot(latent[:, :RANK], wexp[...]).astype(BF16)
        rope_key = latent[:, RANK : RANK + RDIM]
        for h in range(heads):
            keys = jnp.concatenate(
                [expanded[:, 2 * h * HDIM : (2 * h + 1) * HDIM], rope_key], axis=1
            )
            all_vals[place, :, h * HDIM : (h + 1) * HDIM] = expanded[
                :, (2 * h + 1) * HDIM : (2 * h + 2) * HDIM
            ]
            scores = dot_nt(q_out[h], keys)
            all_scores[h, place] = scores
            top = mx[h]
            for i in range(scores.shape[1] // wide):
                top = jnp.maximum(top, scores[:, i * wide : (i + 1) * wide])
            mx[h] = top

    each_block(score)
    for h in range(heads):
        mx[h] = jnp.broadcast_to(jnp.max(mx[h], axis=1, keepdims=True), mx.shape[1:])

    def weigh(place, ref, line):
        for h in range(heads):
            weights = jnp.exp2((all_scores[h, place] - mx[h][:, :1]) * (SCALE * LOG2E))
            total = sm[h]
            for i in range(weights.shape[1] // wide):
                total = total + weights[:, i * wide : (i + 1) * wide]
            sm[h] = total
            vals = all_vals[place, :, h * HDIM : (h + 1) * HDIM]
            acc[h] = acc[h] + dot(weights.astype(BF16), vals)

    each_block(weigh)
    for h in range(heads):
        sm[h] = jnp.broadcast_to(jnp.sum(sm[h], axis=1, keepdims=True), sm.shape[1:])


def attend_kernel(pack, heads, masked, order, tokens, *refs):
    refs = list(refs)
    (s_ref,) = take(refs, 1)
    qblk_ref, kblk_ref = take(refs, 2) if masked else (None, None)
    x, own, other = take(refs, 2), take(refs, 2), take(refs, 2)
    gain, cos, sin, w_own, w_other, e_own, e_other = take(refs, 7)
    take(refs, tokens)
    lines = own[0].shape[1]
    normed_out, q_out, att_out, lse_out = take(refs, 4)
    acc, mx, sm, wexp, *kept = refs
    group = normed_out.shape[0]
    nope = heads * HDIM
    wide = heads * HALF
    size = pack.size
    here = s_ref[0]
    fill_expand(here, e_own, e_other, wexp, pack)
    found = [entry(x, order, r) for r in range(len(order))]
    rows = jnp.concatenate([ref[j] for ref, j in found], axis=0).astype(F32)
    normed_out[...] = (rows * rms_inverse(rows) * gain[...]).astype(BF16)
    qlin = [jnp.zeros((group, size), F32) for _ in range(pack.query_parts)]
    for ref, place in part_places(here, w_own, w_other, size):
        block = normed_out[:, pl.ds(place, size)]
        qlin = [q + dot(block, pack.query(ref, part)) for part, q in enumerate(qlin)]
    qlin = jnp.concatenate(qlin, axis=1)
    first = qlin[:, nope : nope + wide]
    second = qlin[:, nope + wide :]
    turned_a = first * cos[...] - second * sin[...]
    turned_b = first * sin[...] + second * cos[...]
    for h in range(heads):
        q_out[h] = jnp.concatenate(
            [
                qlin[:, h * HDIM : (h + 1) * HDIM],
                turned_a[:, h * HALF : (h + 1) * HALF],
                turned_b[:, h * HALF : (h + 1) * HALF],
            ],
            axis=1,
        ).astype(BF16)
    acc[...] = jnp.zeros_like(acc)
    mx[...] = jnp.full_like(mx, NEG_LARGE)
    sm[...] = jnp.zeros_like(sm)
    if masked:
        attend_masked(
            here, heads, order, lines, (own, other), wexp, q_out, (acc, mx, sm), qblk_ref, kblk_ref
        )
    else:
        attend_whole(here, heads, order, lines, (own, other), wexp, q_out, (acc, mx, sm), *kept)
    for h in range(heads):
        att_out[:, h * HDIM : (h + 1) * HDIM] = (acc[h] / sm[h]).astype(BF16)
        lse_out[h] = mx[h] * (SCALE * LOG2E) + jnp.log2(sm[h])


def out_kernel(pack, tokens, *refs):
    refs = list(refs)
    s_ref, att, w_own, w_other = take(refs, 4)
    take(refs, tokens)
    each = refs[0].shape[0]
    for ref, place in part_places(s_ref[0], w_own, w_other, pack.size):
        block = dot(att[...], pack.out(ref)).astype(BF16)
        for r, out in enumerate(refs):
            out[:, pl.ds(place, pack.size)] = block[r * each : (r + 1) * each]


def project(pack, here, att, weights, plane, tokens):
    width = 2 * weights[0].shape[0] * pack.size
    return pl.pallas_call(
        functools.partial(out_kernel, pack, len(tokens)),
        out_shape=tuple(
            [jax.ShapeDtypeStruct((att.shape[0] // plane, width), BF16)] * plane
        ),
        in_specs=smem_spec() + vmem_specs(3) + any_spec() * len(tokens),
        out_specs=tuple(vmem_specs(plane)),
        compiler_params=pltpu.CompilerParams(vmem_limit_bytes=40 * MIB),
        cost_estimate=pl.CostEstimate(
            flops=1_000_000_000, bytes_accessed=5_000_000, transcendentals=0
        ),
        name="project",
    )(here, att, *weights, *tokens)


def attend_back_kernel(pack, heads, masked, orders, *refs):
    refs = list(refs)
    (s_ref,) = take(refs, 1)
    qblk_ref, kblk_ref = take(refs, 2) if masked else (None, None)
    cos, sin, w_own, w_other, e_own, e_other, o_own, o_other = take(refs, 8)
    per_batch = [
        (take(refs, 2), take(refs, 2), take(refs, 2), *take(refs, 4)) for _ in orders
    ]
    take(refs, 1)
    batches, plane = len(orders), len(orders[0])
    lines = w_own.shape[0]
    gpart_outs = [take(refs, 2) for _ in orders]
    own_out, other_out, dw_own, dw_other = take(refs, 4)
    gq_acc, gqlin, gatt, wexp, dwexp, dwq, dwo = refs
    group = gqlin.shape[0]
    each = group // plane
    nope = heads * HDIM
    wide = heads * HALF
    size = pack.size
    here = s_ref[0]
    fill_expand(here, e_own, e_other, wexp, pack)
    dwexp[...] = jnp.zeros_like(dwexp)
    places = part_places(here, w_own, w_other, size)
    for b, order in enumerate(orders):
        gres, own, other, normed, q_ref, att, lse = per_batch[b]
        total = jnp.zeros((group, nope), F32)
        for i, (ref, place) in enumerate(part_places(here, o_own, o_other, size)):
            found = [entry(gres, order, r) for r in range(plane)]
            block = jnp.concatenate([g[j, :, pl.ds(place, size)] for g, j in found], axis=0)
            total = total + dot_nt(block, pack.out(ref))
            term = dot_tn(att[...], block)
            dwo[i] = term if b == 0 else dwo[i] + term
        gatt[...] = total.astype(BF16)
        gq_acc[...] = jnp.zeros_like(gq_acc)
        deltas = [
            jnp.sum(
                gatt[:, h * HDIM : (h + 1) * HDIM].astype(F32)
                * att[:, h * HDIM : (h + 1) * HDIM].astype(F32),
                axis=1,
                keepdims=True,
            )
            for h in range(heads)
        ]
        for core, (ref, out) in enumerate(((own, own_out), (other, other_out))):

            def step(
                line, carry, core=core, key_ref=ref, out=out, b=b, q_ref=q_ref, lse=lse,
                deltas=deltas, order=order,
            ):
                live = (here ^ (2 * line + core)) <= here

                @pl.when(jnp.logical_not(live))
                def _():
                    out[line, b] = jnp.zeros((group, WIDE), BF16)

                @pl.when(live)
                def _():
                    latent = load_keys(key_ref, order, line)
                    expanded = dot(latent[:, :RANK], wexp[...]).astype(BF16)
                    rope_key = latent[:, RANK : RANK + RDIM]
                    allowed = None
                    if masked:
                        allowed = kblk_ref[pl.ds(2 * line + core, 1), :] <= qblk_ref[...]
                    grads = []
                    grad_rope = jnp.zeros((group, RDIM), F32)
                    for h in range(heads):
                        keys = jnp.concatenate(
                            [expanded[:, 2 * h * HDIM : (2 * h + 1) * HDIM], rope_key], axis=1
                        )
                        vals = expanded[:, (2 * h + 1) * HDIM : (2 * h + 2) * HDIM]
                        query = q_ref[h]
                        gout = gatt[:, h * HDIM : (h + 1) * HDIM]
                        scores = block_scores(query, keys, allowed)
                        probs = jnp.exp2(scores * (SCALE * LOG2E) - lse[h][:, :1])
                        if masked:
                            probs = jnp.where(allowed, probs, 0.0)
                        gprobs = dot_nt(gout, vals)
                        gscores = (probs * (gprobs - deltas[h])).astype(BF16)
                        gq_acc[h] = gq_acc[h] + dot(gscores, keys)
                        gkeys = dot_tn(gscores, query) * SCALE
                        gvals = dot_tn(probs.astype(BF16), gout)
                        grads.append(gkeys[:, :HDIM].astype(BF16))
                        grads.append(gvals.astype(BF16))
                        grad_rope = grad_rope + gkeys[:, HDIM:]
                    gexp = jnp.concatenate(grads, axis=1)
                    dwexp[...] = dwexp[...] + dot_tn(latent[:, :RANK], gexp)
                    gcomp = dot_nt(gexp, wexp[...])
                    blank = jnp.zeros((group, WIDE - RANK - RDIM), F32)
                    out[line, b] = jnp.concatenate([gcomp, grad_rope, blank], axis=1).astype(BF16)

                return carry

            lax.fori_loop(0, lines, step, 0)
        firsts, seconds = [], []
        for h in range(heads):
            value = gq_acc[h] * SCALE
            gqlin[:, h * HDIM : (h + 1) * HDIM] = value[:, :HDIM].astype(BF16)
            firsts.append(value[:, HDIM : HDIM + HALF])
            seconds.append(value[:, HDIM + HALF :])
        first = jnp.concatenate(firsts, axis=1)
        second = jnp.concatenate(seconds, axis=1)
        gqlin[:, nope : nope + wide] = (first * cos[...] + second * sin[...]).astype(BF16)
        gqlin[:, nope + wide :] = (second * cos[...] - first * sin[...]).astype(BF16)
        for i, (ref, place) in enumerate(places):
            weight = jnp.concatenate(
                [pack.query(ref, part) for part in range(pack.query_parts)], axis=1
            )
            block = dot_nt(gqlin[...], weight).astype(BF16)
            for r in range(plane):
                half, j = divmod(order.index(r), plane // 2)
                gpart_outs[b][half][j, :, pl.ds(place, size)] = block[r * each : (r + 1) * each]
            term = dot_tn(normed[:, pl.ds(place, size)], gqlin[...])
            dwq[i] = term if b == 0 else dwq[i] + term
    for core, out in enumerate((dw_own, dw_other)):
        for line in range(lines):
            i = core * lines + line
            term = dwq[i].astype(BF16)
            for part in range(pack.query_parts):
                out[line, part * size : (part + 1) * size] = term[
                    :, part * size : (part + 1) * size
                ]
            place = pl.multiple_of((here ^ (2 * line + core)) * pack.rank, pack.rank)
            term = dwexp[pl.ds(place, pack.rank), :].astype(BF16)
            for part in range(pack.expand_parts):
                at = pack.expand_at + part * pack.rank
                out[line, at : at + pack.rank] = term[:, part * size : (part + 1) * size]
            out[line, pack.out_at : pack.rows] = dwo[i].astype(BF16)


def vmem_specs(count):
    return [pl.BlockSpec(memory_space=pltpu.VMEM)] * count


def smem_spec():
    return [pl.BlockSpec(memory_space=pltpu.SMEM)]


def own_latents(place, x, cos, sin, own, other):
    rows, width = x.shape
    total = len(own) * own[0].shape[1]
    return pl.pallas_call(
        functools.partial(latent_kernel, len(own)),
        out_shape=(
            jax.ShapeDtypeStruct((rows, WIDE), BF16),
            jax.ShapeDtypeStruct((rows, RANK + RDIM), BF16),
            jax.ShapeDtypeStruct((1, width), F32),
            jax.ShapeDtypeStruct((1, width), F32),
            jax.ShapeDtypeStruct((1, RANK), F32),
            jax.ShapeDtypeStruct((RANK + RDIM, width), BF16),
        ),
        in_specs=smem_spec() + vmem_specs(3 + len(own) + len(other)),
        out_specs=tuple(vmem_specs(6)),
        scratch_shapes=[pltpu.VMEM((total, width), BF16)],
        compiler_params=pltpu.CompilerParams(vmem_limit_bytes=40 * MIB),
        cost_estimate=pl.CostEstimate(
            flops=1_000_000_000, bytes_accessed=6_000_000, transcendentals=1_000
        ),
        name="own_latents",
    )(place, x, cos, sin, *own, *other)


def whole(value):
    rank = len(value.shape)
    return pl.BlockSpec(value.shape, lambda i: (0,) * rank)


def attend(pack, here, marks, order, x, gain, cos, sin, keys, weights, heads, tokens):
    plane, each, width = x[0].shape
    group = 2 * plane * each
    lines = keys[0].shape[1]
    inputs = [*marks, *x, *keys, gain, cos, sin, *weights]
    return pl.pallas_call(
        functools.partial(attend_kernel, pack, heads, bool(marks), order, len(tokens)),
        out_shape=(
            jax.ShapeDtypeStruct((group, width), BF16),
            jax.ShapeDtypeStruct((heads, group, QDIM), BF16),
            jax.ShapeDtypeStruct((group, heads * HDIM), BF16),
            jax.ShapeDtypeStruct((heads, group, HDIM), F32),
        ),
        in_specs=smem_spec() + vmem_specs(len(inputs)) + any_spec() * len(tokens),
        out_specs=tuple(vmem_specs(4)),
        scratch_shapes=[pltpu.VMEM((heads, group, HDIM), F32)] * 3
        + [pltpu.VMEM((RANK, 2 * heads * HDIM), BF16)]
        + (
            []
            if marks
            else [
                pltpu.VMEM((heads, 2 * lines, group, group), F32),
                pltpu.VMEM((2 * lines, group, heads * HDIM), BF16),
            ]
        ),
        compiler_params=pltpu.CompilerParams(vmem_limit_bytes=60 * MIB),
        cost_estimate=pl.CostEstimate(
            flops=16_000_000_000, bytes_accessed=16_000_000, transcendentals=4_000_000
        ),
        name="attend",
    )(here, *inputs, *tokens)


def attend_back(pack, here, marks, orders, cos, sin, weights, out_weights, per_batch, token):
    batches, plane = len(orders), len(orders[0])
    lines = weights[0].shape[0]
    heads, group = per_batch[0][7].shape[:2]
    each, width = per_batch[0][0].shape[1:]
    size = pack.size
    outs = [jax.ShapeDtypeStruct((plane // 2, each, width), BF16)] * (2 * batches)
    outs += [jax.ShapeDtypeStruct((lines, batches, group, WIDE), BF16)] * 2
    outs += [jax.ShapeDtypeStruct((lines, pack.rows, size), BF16)] * 2
    inputs = [*marks, cos, sin, *weights, *out_weights]
    inputs += [v for args in per_batch for v in args]
    res = pl.pallas_call(
        functools.partial(attend_back_kernel, pack, heads, bool(marks), orders),
        out_shape=tuple(outs),
        in_specs=smem_spec() + vmem_specs(len(inputs)) + any_spec(),
        out_specs=tuple(vmem_specs(len(outs))),
        scratch_shapes=[
            pltpu.VMEM((heads, group, QDIM), F32),
            pltpu.VMEM((group, heads * QDIM), BF16),
            pltpu.VMEM((group, heads * HDIM), BF16),
            pltpu.VMEM((RANK, 2 * heads * HDIM), BF16),
            pltpu.VMEM((RANK, 2 * heads * HDIM), F32),
            pltpu.VMEM((2 * lines, size, heads * QDIM), F32),
            pltpu.VMEM((2 * lines, heads * HDIM, size), F32),
        ],
        compiler_params=pltpu.CompilerParams(vmem_limit_bytes=63 * MIB),
        cost_estimate=pl.CostEstimate(
            flops=32_000_000_000, bytes_accessed=30_000_000, transcendentals=8_000_000
        ),
        name="attend_back",
    )(here, *inputs, token)
    return res[: 2 * batches], res[2 * batches : 2 * batches + 2], res[2 * batches + 2 :]


def shared_kernel(s_ref, *refs):
    *pieces, gates_out, down_out = refs
    here = s_ref[0]
    _, kinds, rows, size = pieces[0].shape
    pad = down_out.shape[0]
    gates_out[...] = jnp.zeros_like(gates_out)
    down_out[...] = jnp.zeros_like(down_out)
    for k, ref in enumerate(pieces):
        for core in range(2):
            place = pl.multiple_of(((here // 2) ^ k) * (2 * size) + core * size, size)
            for kind in range(2):
                gates_out[kind * pad : kind * pad + rows, pl.ds(place, size)] = ref[core, kind]
            down_out[:rows, pl.ds(place, size)] = ref[core, 2]


def shared_whole(here, pieces, pad):
    width = 2 * len(pieces) * pieces[0].shape[-1]
    return pl.pallas_call(
        shared_kernel,
        out_shape=(
            jax.ShapeDtypeStruct((2 * pad, width), BF16),
            jax.ShapeDtypeStruct((pad, width), BF16),
        ),
        in_specs=smem_spec() + vmem_specs(len(pieces)),
        out_specs=tuple(vmem_specs(2)),
        cost_estimate=pl.CostEstimate(flops=0, bytes_accessed=4_000_000, transcendentals=0),
        name="shared_whole",
    )(here, *pieces)


def key_back_kernel(got, low_ref, gain, cos, sin, grad_out, gain_out):
    value = got[...]
    comp = low_ref[:, :RANK].astype(F32)
    inverse = rms_inverse(comp)
    hat = comp * inverse
    grad = value[:, :RANK]
    gain_out[...] = jnp.sum(grad * hat, axis=0, keepdims=True)
    scaled = grad * gain[...]
    grad = inverse * (scaled - hat * jnp.mean(scaled * hat, axis=-1, keepdims=True))
    first, second = value[:, RANK : RANK + HALF], value[:, RANK + HALF : RANK + RDIM]
    grad_out[...] = jnp.concatenate(
        [
            grad,
            first * cos[...] + second * sin[...],
            second * cos[...] - first * sin[...],
            jnp.zeros((value.shape[0], WIDE - RANK - RDIM), F32),
        ],
        axis=1,
    ).astype(BF16)


def key_back(got, low, gain, cos, sin):
    return pl.pallas_call(
        key_back_kernel,
        out_shape=(
            jax.ShapeDtypeStruct(got.shape, BF16),
            jax.ShapeDtypeStruct((1, RANK), F32),
        ),
        in_specs=vmem_specs(5),
        out_specs=tuple(vmem_specs(2)),
        name="key_back",
    )(got, low, gain, cos, sin)


def inputs_back_kernel(first, second, grad_latent, latent_t, x_ref, gain, residual, out, gain_out):
    grad = jnp.concatenate([first[...], second[...]], axis=0).astype(F32)
    grad = grad + dot(grad_latent[:, : RANK + RDIM], latent_t[...])
    x = x_ref[...].astype(F32)
    inverse = rms_inverse(x)
    hat = x * inverse
    gain_out[...] = jnp.sum(grad * hat, axis=0, keepdims=True)
    scaled = grad * gain[...]
    grad = inverse * (scaled - hat * jnp.mean(scaled * hat, axis=-1, keepdims=True))
    out[...] = (grad + residual[...]).astype(BF16)


def inputs_back(first, second, grad_latent, latent_t, x, gain, residual):
    return pl.pallas_call(
        inputs_back_kernel,
        out_shape=(
            jax.ShapeDtypeStruct(x.shape, BF16),
            jax.ShapeDtypeStruct(gain.shape, F32),
        ),
        in_specs=vmem_specs(7),
        out_specs=tuple(vmem_specs(2)),
        compiler_params=pltpu.CompilerParams(vmem_limit_bytes=40 * MIB),
        name="inputs_back",
    )(first, second, grad_latent, latent_t, x, gain, residual)


def latent_back_kernel(batches, plane, share, s_ref, *refs):
    refs = list(refs)
    grads, normed = take(refs, plane), take(refs, batches)
    gattn, gffn, glat, own_out, other_out, full = refs
    here, column = s_ref[0], s_ref[1]
    lines, rows, size = own_out.shape
    for b in range(batches):
        mine = jnp.concatenate([g[b, :, : RANK + RDIM] for g in grads], axis=0)
        term = dot_tn(mine, normed[b][...])
        full[...] = term if b == 0 else full[...] + term
    top = pl.multiple_of(column * share, 8)
    parts = RANK // size
    lat = [glat[:, i * size : (i + 1) * size] for i in range(parts)]
    blank = jnp.zeros((rows - share - 2 - parts, size), F32)
    for core, out in enumerate((own_out, other_out)):
        for line in range(lines):
            place = pl.multiple_of((here ^ (2 * line + core)) * size, size)
            columns = pl.ds(place, size)
            out[line] = jnp.concatenate(
                [full[pl.ds(top, share), columns], gattn[:, columns], gffn[:, columns], *lat, blank],
                axis=0,
            ).astype(BF16)


def latent_back(here, grads, normed, gains, lines, share):
    width = normed[0].shape[1]
    out = jax.ShapeDtypeStruct((lines, share + 16, width // (2 * lines)), BF16)
    return pl.pallas_call(
        functools.partial(latent_back_kernel, len(normed), len(grads), share),
        out_shape=(out, out),
        in_specs=smem_spec() + vmem_specs(len(grads) + len(normed) + 3),
        out_specs=tuple(vmem_specs(2)),
        scratch_shapes=[pltpu.VMEM((RANK + RDIM, width), F32)],
        compiler_params=pltpu.CompilerParams(vmem_limit_bytes=40 * MIB),
        cost_estimate=pl.CostEstimate(
            flops=2_000_000_000, bytes_accessed=5_000_000, transcendentals=0
        ),
        name="latent_back",
    )(here, *grads, *normed, *gains)


def feed_kernel(orders, per, side, aliased, *refs):
    refs = list(refs)
    slot, gate = take(refs, 2)
    xa, xb, ca, cb = [take(refs, 2) for _ in range(4)]
    wg, wu, wd, sgut, sd = take(refs, 5)
    came = take(refs, 2) if side == 0 else None
    take(refs, aliased + 1)
    rows_out, grows_out, act_out, gpre_out, gup_out, dsgut, dsd = take(refs, 7)
    pieces = refs
    plane, _, half, width = xa[0].shape
    plane = 2 * plane
    each = 2 * half
    group = plane * each
    cap = rows_out.shape[2]
    pad = sd.shape[0]

    @pl.when(pl.program_id(0) == 0)
    def _():
        dsgut[...] = jnp.zeros_like(dsgut)
        dsd[...] = jnp.zeros_like(dsd)

    picks, gates = [], []
    for i in range(per):
        chosen = lax.broadcasted_iota(jnp.int32, (cap, group), 0) == slot[i]
        gates.append(jnp.sum(jnp.where(chosen, gate[i], 0.0), axis=1, keepdims=True))
        picks.append(chosen.astype(F32))
    at_a, at_b = [[order.index(r) for r in range(plane)] for order in orders]

    def tokens_of(*pairs):
        found = [
            (i, *entry(pair, order, r))
            for i in range(per)
            for r in range(plane)
            for pair, order in zip(pairs, orders)
        ]
        return jnp.concatenate([ref[j, i] for i, ref, j in found], axis=0)

    x, cot = tokens_of(xa, xb), tokens_of(ca, cb)
    gates = jnp.concatenate(gates, axis=0)
    rows = jnp.concatenate(
        [
            dot(picks[i].astype(BF16), x[i * group : (i + 1) * group]).astype(BF16)
            for i in range(per)
        ],
        axis=0,
    )
    grows = jnp.concatenate(
        [dot(picks[i].astype(BF16), cot[i * group : (i + 1) * group]) for i in range(per)],
        axis=0,
    )
    grows = (grows * gates).astype(BF16)
    pre = dot_nt(rows, wg[...])
    upp = dot_nt(rows, wu[...])
    sig = 1.0 / (1.0 + jnp.exp(-pre))
    silu = pre * sig
    act = (silu * upp).astype(BF16)
    geact = dot_nt(grows, wd[...])
    gpre = (geact * upp * (sig * (1.0 + pre * (1.0 - sig)))).astype(BF16)
    gup = (geact * silu).astype(BF16)
    for i in range(per):
        part = slice(i * cap, (i + 1) * cap)
        rows_out[0, i] = rows[part]
        grows_out[0, i] = grows[part]
        act_out[0, i] = act[part]
        gpre_out[0, i] = gpre[part]
        gup_out[0, i] = gup[part]
    made = (dot(act, wd[...]) * gates).astype(BF16)
    gmade = (dot(gpre, wg[...]) + dot(gup, wu[...])).astype(BF16)
    both = dot_nt(x, sgut[...])
    spre, supp = both[:, :pad], both[:, pad:]
    ssig = 1.0 / (1.0 + jnp.exp(-spre))
    ssilu = spre * ssig
    sact = (ssilu * supp).astype(BF16)
    gsact = dot_nt(cot, sd[...])
    gspre = (gsact * supp * (ssig * (1.0 + spre * (1.0 - ssig)))).astype(BF16)
    gsupp = (gsact * ssilu).astype(BF16)
    gsboth = jnp.concatenate([gspre, gsupp], axis=1)
    dsgut[...] = dsgut[...] + dot_tn(gsboth, x)
    dsd[...] = dsd[...] + dot_tn(sact, cot)
    for i in range(per):
        back = picks[i].T.astype(BF16)
        toks = slice(i * group, (i + 1) * group)
        part = slice(i * cap, (i + 1) * cap)
        out = dot(
            jnp.concatenate([back, sact[toks]], axis=1),
            jnp.concatenate([made[part], sd[...]], axis=0),
        )
        gx = dot(
            jnp.concatenate([back, gsboth[toks]], axis=1),
            jnp.concatenate([gmade[part], sgut[...]], axis=0),
        )
        if side == 1:
            pieces[0][i] = out.astype(BF16)
            pieces[1][i] = gx.astype(BF16)
            continue
        out = (out + came[0][i].astype(F32)).astype(BF16)
        gx = (gx + came[1][i].astype(F32)).astype(BF16)
        for value, (keep_a, send_a, keep_b, send_b) in ((out, pieces[:4]), (gx, pieces[4:])):
            for r in range(plane):
                for part_of, at, both in ((0, at_a, (keep_a, send_a)), (1, at_b, (keep_b, send_b))):
                    top = r * each + part_of * half
                    ref = both[at[r] // (plane // 2)]
                    ref[at[r] % (plane // 2), i] = value[top : top + half]


def feed(
    here, orders, b, side, batches, cap, slot, gate, rows, cots, weights, came, earlier, token
):
    plane, lines, half, width = rows[0].shape
    plane = 2 * plane
    group = 2 * plane * half
    per = 2 if group <= 256 and lines % 2 == 0 else 1
    steps = lines // per
    hidden = weights[0].shape[0]
    pad = weights[-1].shape[0]

    def fixed(shape):
        return pl.BlockSpec(shape, lambda i: (0,) * len(shape), pipeline_mode=pl.Buffered(1))

    def block(count, size):
        return pl.BlockSpec((count, per, size, width), lambda i: (0, i, 0, 0))

    def saved(size):
        return pl.BlockSpec((1, per, cap, size), lambda i: (b, side * steps + i, 0, 0))

    mark = pl.BlockSpec((per, 1, group), lambda i: (i, 0, 0))
    flat = pl.BlockSpec((per, group, width), lambda i: (i, 0, 0))
    keep = [width, width, hidden, hidden, hidden]
    shapes = [jax.ShapeDtypeStruct((batches, 2 * lines, cap, size), BF16) for size in keep]
    shapes += [
        jax.ShapeDtypeStruct((2 * pad, width), F32),
        jax.ShapeDtypeStruct((pad, width), F32),
    ]
    out_specs = [saved(size) for size in keep] + [fixed((2 * pad, width)), fixed((pad, width))]
    if side == 1:
        shapes += [jax.ShapeDtypeStruct((lines, group, width), BF16)] * 2
        out_specs += [flat] * 2
    else:
        shapes += [jax.ShapeDtypeStruct((plane // 2, lines, half, width), BF16)] * 8
        out_specs += [block(plane // 2, half)] * 8
    in_specs = [mark, mark] + [block(plane // 2, half)] * 8
    in_specs += [fixed(w.shape) for w in weights]
    inputs = [slot, gate, *rows, *cots, *weights]
    if side == 0:
        in_specs += [flat] * 2
        inputs += list(came)
    aliases = {}
    for value, place in earlier:
        aliases[len(inputs)] = place
        inputs.append(value)
        in_specs += any_spec()
    inputs.append(token)
    in_specs += any_spec()
    return pl.pallas_call(
        functools.partial(feed_kernel, orders, per, side, len(earlier)),
        grid=(steps,),
        out_shape=tuple(shapes),
        in_specs=in_specs,
        out_specs=tuple(out_specs),
        input_output_aliases=aliases,
        compiler_params=pltpu.CompilerParams(vmem_limit_bytes=63 * MIB),
        cost_estimate=pl.CostEstimate(
            flops=24_000_000_000, bytes_accessed=40_000_000, transcendentals=1_000_000
        ),
        name="feed",
    )(*inputs)


def local(
    inputs,
    cotangent,
    routes,
    gate_weights,
    attn_gain,
    latent_gain,
    ffn_gain,
    query_proj,
    latent_proj,
    expand_proj,
    out_proj,
    shared_gate,
    shared_up,
    shared_down,
    expert_gate,
    expert_up_weight,
    expert_down,
):
    seq_count = lax.axis_size("seq")
    head_count = lax.axis_size("head")
    seq_index = lax.axis_index("seq")
    head_index = lax.axis_index("head")
    lines = depth()
    line, core = seq_index // 2, seq_index % 2
    batches, each, width = inputs.shape
    group = each * head_count
    heads = out_proj.shape[0] // HDIM
    serial = group > BLOCK
    here = jnp.stack([seq_index, head_index])
    positions = seq_index * group + jnp.arange(group, dtype=jnp.int32)
    away = jnp.arange(head_count, dtype=jnp.int32) ^ head_index

    shard = latent_proj.shape[0]
    pack = Pack(shard, heads, seq_count)
    n_lat = latent_gain.shape[0]
    lat_gain = lax.dynamic_update_slice_in_dim(
        jnp.zeros((RANK,), BF16), latent_gain, seq_index * n_lat, 0
    )
    unit = 16 * head_count
    lat_rows = -(-(RANK + RDIM + 16) // unit) * unit
    gain_part = jnp.concatenate(
        [attn_gain[None], ffn_gain[None], lat_gain.reshape(RANK // shard, shard)], axis=0
    )
    gain_part = jnp.pad(gain_part, ((0, lat_rows - RANK - RDIM - gain_part.shape[0]), (0, 0)))
    lat_mine = jnp.concatenate([jnp.transpose(latent_proj), gain_part], axis=0)
    lat_each = lat_rows // head_count
    lat_mine = lax.dynamic_slice_in_dim(lat_mine, head_index * lat_each, lat_each, 0)
    orders = [plane_order(False), plane_order(True)]
    lat_line = Sends("latent_weights", [lat_mine] * (lines - 1), "seq", [2 * k for k in range(1, lines)])
    xs_flow = Plane("inputs", inputs[0], inputs[1])
    phase = Phase(lat_line, xs_flow)

    pair = head_count // 2
    expert_ids = jnp.arange(seq_count, dtype=jnp.int32) * pair + head_index // 2
    hits = routes[None] == expert_ids[:, None, None, None]
    gate_of = jnp.sum(jnp.where(hits, gate_weights[None], 0.0), axis=-1)
    named = jnp.any(hits, axis=-1).astype(F32)
    both = jnp.stack([gate_of, named]).reshape(2, seq_count, batches, head_count, each)
    gate_of, named = jnp.take(both, away, axis=3).reshape(2, seq_count, batches, group)
    ahead = jnp.arange(group)[:, None] < jnp.arange(group)[None, :]
    rank = lax.dot_general(
        named.astype(BF16), ahead.astype(BF16), (((2,), (0,)), ((), ())), preferred_element_type=F32
    )
    gate_high = gate_of.astype(BF16)
    mark_mine = jnp.stack(
        [
            jnp.where(named > 0.0, jnp.minimum(rank, 255.0), -1.0).astype(BF16),
            gate_high,
            (gate_of - gate_high.astype(F32)).astype(BF16),
        ],
        axis=1,
    )
    mark_size = mark_mine.size
    mark_rows = -(-mark_size // (16 * shard)) * 16
    mark_mine = jnp.pad(mark_mine.reshape(-1), (0, mark_rows * shard - mark_size)).reshape(
        mark_rows, shard
    )

    cols = query_proj.reshape(query_proj.shape[0], heads, QDIM)
    query_mine = jnp.concatenate(
        [
            cols[..., :HDIM].reshape(-1, heads * HDIM),
            cols[..., HDIM : HDIM + HALF].reshape(-1, heads * HALF),
            cols[..., HDIM + HALF :].reshape(-1, heads * HALF),
        ],
        axis=1,
    )
    blocks = [query_mine[:, i * shard : (i + 1) * shard] for i in range(pack.query_parts)]
    blocks += [expand_proj[:, i * shard : (i + 1) * shard] for i in range(pack.expand_parts)]
    query_mine = jnp.concatenate(blocks[: pack.query_parts], axis=0)
    expand_mine = jnp.concatenate(blocks[pack.query_parts :], axis=0)
    out_mine = jnp.concatenate([out_proj, mark_mine], axis=0)

    lat_mine, query_mine = phase.end(lat_mine, query_mine)
    lat_stack = jnp.stack([lat_mine] + lat_line.held)
    lat_plane = head_send("latent_weights", [lat_stack] * (head_count - 1))
    query_flow = Line("query_weights", query_mine)
    lat_stack, out_mine = Phase(lat_plane, query_flow).end(lat_stack, out_mine)
    lat_own = [lat_stack] + lat_plane.held
    lat_core = core_send("latent_weights", lat_own)
    cot_lines = [None, None]
    if not serial:
        (cot_mine,) = sync(after(cotangent, lat_stack))
        cot_lines = [Line("cotangents", cot_mine[b]) for b in range(batches)]
    cot_phase = Phase(cot_lines[0])
    Phase(lat_core).end()
    lat_other = lat_core.held

    cos_all, sin_all = rope_tables(positions)
    own_cos, own_sin = [
        lax.dynamic_slice_in_dim(t, head_index * each, each, 0) for t in (cos_all, sin_all)
    ]
    own_keys, own_latent, gain_attn, gain_ffn, gain_lat, latent_t = own_latents(
        here,
        inputs.reshape(batches * each, width),
        jnp.tile(own_cos, (batches, 1)),
        jnp.tile(own_sin, (batches, 1)),
        lat_own,
        lat_other,
    )
    own_keys = own_keys.reshape(batches, each, WIDE)
    key_flow = Line("keys", own_keys)
    (own_keys,) = cot_phase.end(own_keys)
    key_flow = Line("keys", own_keys)
    (expand_mine,) = Phase(key_flow, query_flow, xs_flow).end(expand_mine)
    expand_flow = Line("expand_weights", expand_mine)
    run(query_flow)
    query_core = core_send("query_weights", [query_flow.held])
    Phase(key_flow, expand_flow, query_core).end()
    run(key_flow)
    run(query_flow)
    key_plane = Plane("keys", key_flow.held[:, 0], key_flow.held[:, 1])
    shared_mine = jnp.stack(
        [
            jnp.transpose(shared_gate).reshape(seq_count, -1, shard),
            jnp.transpose(shared_up).reshape(seq_count, -1, shard),
            shared_down.reshape(seq_count, -1, shard),
        ],
        axis=1,
    ).reshape(lines, 2, 3, -1, shard)
    out_mine, shared_mine = Phase(key_plane, expand_flow, cot_lines[0]).end(out_mine, shared_mine)
    out_flow = Line("output_weights", out_mine)
    run(expand_flow)
    expand_core = core_send("expand_weights", [expand_flow.held])
    shared_kept = pick(shared_mine, core, 1)
    shared_core = core_send("shared_weights", [pick(shared_mine, core ^ 1, 1)])
    Phase(key_plane, out_flow, expand_core, shared_core).end()
    while key_plane.more:
        Phase(key_plane).end()
    key_core = core_send("keys", key_plane.held)
    first_weights = (query_flow.held, query_core.held[0], expand_flow.held, expand_core.held[0])
    Phase(key_core).end()
    keys = [(*key_plane.held[2 * b : 2 * b + 2], *key_core.held[2 * b : 2 * b + 2]) for b in range(2)]
    xs = run(xs_flow)[0]
    xs = [xs[:2], xs[2:]]

    own_rows = inputs.astype(F32)
    own_inverse = rms_inverse(own_rows)
    own_hat = own_rows * own_inverse
    cos_b, sin_b = [
        jnp.tile(
            jnp.take(t.reshape(head_count, each, HALF), away, axis=0).reshape(group, HALF),
            (1, heads),
        )
        for t in (cos_all, sin_all)
    ]
    marks = ()
    if group > BLOCK:
        place = (away[:, None] * each + jnp.arange(each, dtype=jnp.int32)[None, :]).reshape(group)
        own_block = (seq_index * group + place) // BLOCK
        offsets = jnp.arange(seq_count, dtype=jnp.int32) ^ seq_index
        key_block = (offsets[:, None] * group + place[None, :]) // BLOCK
        marks = (jnp.broadcast_to(own_block[:, None], (group, group)), key_block)
    half = each // 2
    saved, residual, ffn_hat, ffn_inverse = [], [], [], []

    def attend_batch(b, tokens):
        saved.append(
            attend(
                pack, here, marks, orders[b], xs[b], gain_attn, cos_b, sin_b, keys[b],
                first_weights, heads, tokens,
            )
        )
        return saved[-1][2]

    def ffn_rows(b, parts, got):
        total = parts[0].astype(F32)
        for value in got:
            total = total + value.astype(F32)
        residual_b = own_rows[b] + total
        inverse_b = rms_inverse(residual_b)
        hat_b = residual_b * inverse_b
        residual.append(residual_b)
        ffn_inverse.append(inverse_b)
        ffn_hat.append(hat_b)
        return Line("ffn_rows", (hat_b * gain_ffn).astype(BF16))

    def halves_of(name, value):
        return Plane(name, value[:, :half], value[:, half:])

    def keep(b, att):
        saved[b] = (*saved[b][:2], att, saved[b][3])
        return att

    cots = [None, None]
    if not serial:
        cots[0] = halves_of("cotangents", run(cot_lines[0])[0])
    window = Phase(out_flow, cots[0], cot_lines[1])
    att0 = attend_batch(0, [key_core.held[0]])
    att0 = keep(0, window.end(att0)[0])
    run(out_flow)
    out_core = core_send("output_weights", [out_flow.held])
    att0 = keep(0, Phase(out_core).end(att0)[0])
    out_weights = (out_flow.held, out_core.held[0])
    parts0 = project(pack, here, att0, out_weights, head_count, [])
    sum0 = head_send("attention_sum", parts0[1:])
    window = Phase(sum0, cots[0])
    att1 = attend_batch(1, [parts0[0]])
    att1, own0 = window.end(att1, parts0[0])
    keep(1, att1)
    parts1 = project(pack, here, att1, out_weights, head_count, [])
    rows = [ffn_rows(0, [own0], sum0.held)]
    sum1 = head_send("attention_sum", parts1[1:])
    came = shared_core.held[0]
    paired = jnp.where(
        core == 0, jnp.stack([shared_kept, came], 1), jnp.stack([came, shared_kept], 1)
    )
    cot_held = [] if serial else run(cots[0])[0]
    own1, paired, *cot_held = Phase(sum1, rows[0], cot_lines[1]).end(parts1[0], paired, *cot_held)
    rows.append(ffn_rows(1, [own1], sum1.held))

    def moves_of(paired):
        return Sends(
            "shared_weights",
            [pick(paired, line ^ k) for k in range(1, lines)],
            "seq",
            [2 * k for k in range(1, lines)],
        )

    if serial:
        run(rows[0])
        shared_moves = moves_of(paired)
        run(shared_moves)
    else:
        cots[0].held = cot_held
        cot_core = [core_send("cotangents", cots[0].held), None]
        cot_late = run(cot_lines[1])[0]
        cot_late, paired = Phase(rows[0], rows[1], cot_core[0]).end(cot_late, paired)
        row_planes = [halves_of("ffn_rows", run(rows[0])[0]), None]
        cot_late, paired = Phase(row_planes[0], rows[1]).end(cot_late, paired)
        row_late = run(rows[1])[0]
        shared_moves = moves_of(paired)
        cot_late, row_late = Phase(row_planes[0], shared_moves).end(cot_late, row_late)
        run(row_planes[0])
        row_core = [core_send("ffn_rows", row_planes[0].held), None]
        cot_late, row_late = Phase(row_core[0]).end(cot_late, row_late)
        cots[1] = halves_of("cotangents", cot_late)
        row_planes[1] = halves_of("ffn_rows", row_late)
    hidden_each = shared_gate.shape[1] // seq_count
    hidden_pad = -(-hidden_each // 128) * 128
    sgut, sdown = shared_whole(here, [pick(paired, line)] + shared_moves.held, hidden_pad)
    weights = (
        jnp.transpose(expert_gate[0]),
        jnp.transpose(expert_up_weight[0]),
        expert_down[0],
        sgut,
        sdown,
    )

    def marks_from(parts):
        flat = parts[:, pack.out_rows :].reshape(lines, -1)
        flat = flat[:, :mark_size]
        return pick(flat.reshape(lines, seq_count, 3, batches, 1, group), seq_index, 1).astype(F32)

    marks_mine = [marks_from(parts) for parts in out_weights]
    slots = [m[:, 0].astype(jnp.int32) for m in marks_mine]
    gates = [m[:, 1] + m[:, 2] for m in marks_mine]
    most_rows = 4 * group * TOPK // (3 * seq_count * pair)
    state = {"kept": [], "dsgut": 0.0, "dsd": 0.0}

    def run_feed(b, side, rows_b, cots_b, came, token):
        earlier = [(v, i) for i, v in enumerate(state["kept"])]
        res = feed(
            here, orders, b, side, batches, most_rows, slots[side][:, b], gates[side][:, b],
            rows_b, cots_b, weights, came, earlier, token,
        )
        state["kept"] = res[:5]
        state["dsgut"] = state["dsgut"] + res[5]
        state["dsd"] = state["dsd"] + res[6]
        return res[7:]

    def collect(name, values):
        return PlaneSum(name, values[:2], values[2:])

    def lines_of(name, flow):
        return LineSum(name, jnp.concatenate(flow.held, axis=1))

    def whole_sum(name, values):
        flow = collect(name, values)
        run(flow)
        return run(lines_of(name, flow))[0]

    if serial:
        grad_ffn, outs = [], []
        for b in range(batches):
            tokens = [grad_ffn[b - 1], outs[b - 1]] if b else []
            row_line = run(rows[b])[0]
            line_b = cotangent[b]
            if b:
                row_line, line_b = after(row_line, *tokens), after(line_b, *tokens)
            line_b = run(Line("cotangents", line_b))[0]
            row_plane, cot_plane = halves_of("ffn_rows", row_line), halves_of("cotangents", line_b)
            row_own, cot_own = run(row_plane, cot_plane)
            row_other = run(core_send("ffn_rows", row_own))[0]
            cot_other = run(core_send("cotangents", cot_own))[0]
            made = run_feed(b, 1, row_other, cot_other, None, row_own[0])
            came = run(core_send("feed_other", made))[0]
            made = run_feed(b, 0, row_own, cot_own, came, row_own[0])
            grad_ffn.append(whole_sum("ffn_grads", made[4:]))
            outs.append(whole_sum("outputs", made[:4]))
        kept = state["kept"]
        rows, grows, act, gpre, gup = [v.reshape(-1, v.shape[-1]) for v in kept]
        exgate_grad = dot_tn(gpre, rows)
        exup_grad = dot_tn(gup, rows)
        exdown_grad = dot_tn(act, grows)
    else:
        phase = Phase(cots[1], row_planes[1])
        made = run_feed(0, 1, row_core[0].held, cot_core[0].held, None, row_core[0].held[0])
        made = phase.end(*made)
        other = core_send("feed_other", made)
        phase = Phase(cots[1])
        Phase(other).end()
        late = Phase(row_planes[1])
        made0 = run_feed(0, 0, row_planes[0].held, cots[0].held, other.held, other.held[0])
        made0 = phase.end(*made0)
        made0 = late.end(*made0)
        run(cots[1], row_planes[1])
        cot_core[1] = core_send("cotangents", cots[1].held)
        row_core[1] = core_send("ffn_rows", row_planes[1].held)
        grads = [collect("ffn_grads", made0[4:]), None]
        phase = Phase(grads[0])
        Phase(cot_core[1], row_core[1]).end()
        made = run_feed(1, 1, row_core[1].held, cot_core[1].held, None, row_core[1].held[0])
        made = phase.end(*made)
        other = core_send("feed_other", made)
        outs = [collect("outputs", made0[:4]), None]
        phase = Phase(grads[0])
        Phase(other).end()
        out_phase = Phase(outs[0])
        made1 = run_feed(1, 0, row_planes[1].held, cots[1].held, other.held, other.held[0])
        made1 = phase.end(*made1)
        run(grads[0])
        grad_line = [lines_of("ffn_grads", grads[0]), None]
        grads[1] = collect("ffn_grads", made1[4:])
        phase = Phase(grad_line[0], grads[1])
        kept = state["kept"]
        rows, grows, act, gpre, gup = [v.reshape(-1, v.shape[-1]) for v in kept]
        exgate_grad = dot_tn(after(gpre, made1[0]), rows)
        exgate_grad, gup = phase.end(exgate_grad, gup)
        phase = Phase(grad_line[0], grads[1])
        exup_grad = dot_tn(gup, rows)
        exup_grad, act = phase.end(exup_grad, act)
        run(grads[1], grad_line[0])
        grad_line[1] = lines_of("ffn_grads", grads[1])
        (grows,) = out_phase.end(grows)
        phase = Phase(grad_line[1], outs[0])
        exdown_grad = dot_tn(act, grows)
        (exdown_grad,) = phase.end(exdown_grad)
        run(grad_line[1])
        grad_ffn = [flow.held for flow in grad_line]
        outs[1] = collect("outputs", made1[:4])
    exgate_grad = jnp.transpose(exgate_grad)[None]
    exup_grad = jnp.transpose(exup_grad)[None]
    exdown_grad = exdown_grad[None]
    dsgut, dsd = state["dsgut"], state["dsd"]

    ffn_hat, ffn_inverse = jnp.stack(ffn_hat), jnp.stack(ffn_inverse)
    grad_two, ffngain_term = norm_back(jnp.stack(grad_ffn), ffn_hat, ffn_inverse, gain_ffn)
    grad_residual = cotangent.astype(F32) + grad_two
    grad_attention = grad_residual.astype(BF16)
    shared_term = jnp.concatenate([dsgut.reshape(2, hidden_pad, width), dsd[None]], axis=0)
    shared_term = shared_term[:, :hidden_each].astype(BF16)
    shared_term = jnp.transpose(
        shared_term.reshape(3, hidden_each, lines, 2, shard), (2, 3, 0, 1, 4)
    )

    gres_flow = Plane("attention_grads", grad_attention[0], grad_attention[1])
    if serial:
        run(gres_flow)
    else:
        Phase(gres_flow).end()
        run(outs[0])
        out_line = [lines_of("outputs", outs[0]), None]
        Phase(gres_flow, out_line[0]).end()
        run(gres_flow)
    gres = gres_flow.held
    token = gres[0]
    if not serial:
        shared_sent = Sends(
            "shared_grads",
            [pick(shared_term, line ^ k) for k in range(1, lines)],
            "seq",
            [2 * k for k in range(1, lines)],
        )
        window = Phase(outs[1], shared_sent)

    per_batch = [(*gres[2 * b : 2 * b + 2], *keys[b], *saved[b]) for b in range(batches)]
    groups = [[b] for b in range(batches)] if serial else [list(range(batches))]
    calls = [
        attend_back(
            pack, here, marks, [orders[b] for b in g], cos_b, sin_b, first_weights, out_weights,
            [per_batch[b] for b in g], token,
        )
        for g in groups
    ]
    if serial:
        gparts = [v for c in calls for v in c[0]]
        gkeys = [jnp.concatenate(v, axis=1) for v in zip(*[c[1] for c in calls])]
        dweights = [
            sum(v.astype(F32) for v in t).astype(BF16) for t in zip(*[c[2] for c in calls])
        ]
        shared_sent = Sends(
            "shared_grads",
            [pick(shared_term, line ^ k) for k in range(1, lines)],
            "seq",
            [2 * k for k in range(1, lines)],
        )
        run(shared_sent)
    else:
        made = window.end(*[v for group_of in calls[0] for v in group_of])
        gparts, gkeys, dweights = made[: 2 * batches], made[-4:-2], made[-2:]
    weight_core = core_send("weight_grads", [dweights[1]])
    key_core = core_send("key_grads", [gkeys[1]])
    late = None if serial else outs[1]
    gkey, dweight_own = Phase(key_core, weight_core).end(gkeys[0], dweights[0])
    both = [
        (
            gkey[:, :, r * each : (r + 1) * each].astype(F32)
            + key_core.held[0][:, :, r * each : (r + 1) * each].astype(F32)
        ).astype(BF16)
        for r in range(head_count)
    ]
    key_plane = head_send("key_grads", both[1:])
    weight_both = (dweight_own.astype(F32) + weight_core.held[0].astype(F32)).astype(BF16)
    weight_line = LineSum("weight_grads", weight_both)
    ends = [both[0], *gparts]
    if late is not None and late.more:
        ends += [v for pair in late.held for v in pair]
    both0, *ends = Phase(key_plane, weight_line).end(*ends)
    gparts = ends[: 2 * batches]
    if late is not None and late.more:
        late.held = [ends[-4:-2], ends[-2:]]
    total = both0.astype(F32)
    for value in key_plane.held:
        total = total + value.astype(F32)
    key_line = LineSum("key_grads", total.astype(BF16))
    normed_sum = PlaneSum("normed_grads", gparts[:2], gparts[2:])
    Phase(key_line, normed_sum, late).end()
    while key_line.more:
        Phase(key_line, normed_sum, None if serial else out_line[0]).end()
    run(normed_sum)
    own_tiled = [jnp.tile(t, (batches, 1)) for t in (own_cos, own_sin)]
    grad_latent, latgain_term = key_back(
        key_line.held.reshape(batches * each, WIDE), own_latent, gain_lat, *own_tiled
    )
    latent_send = head_send(
        "latent_grads", [grad_latent.reshape(batches, each, WIDE)] * (head_count - 1)
    )
    if serial:
        run(latent_send)
    else:
        run(outs[1])
        out_line[1] = lines_of("outputs", outs[1])
        Phase(latent_send).end()
    weights_phase = Phase(weight_line)
    inputs_grad, attngain_term = inputs_back(
        *normed_sum.held, grad_latent, latent_t, inputs.reshape(batches * each, width),
        gain_attn, grad_residual.reshape(batches * each, width),
    )
    inputs_grad = inputs_grad.reshape(batches, each, width)

    share = (RANK + RDIM) // head_count
    latent_own, latent_other = latent_back(
        here,
        [grad_latent.reshape(batches, each, WIDE)] + latent_send.held,
        [kept_b[0] for kept_b in saved],
        (attngain_term, ffngain_term.reshape(1, width), latgain_term),
        lines,
        share,
    )
    latent_core = core_send("latent_grads", [latent_other])
    shared_held = jnp.stack([pick(shared_term, line)] + shared_sent.held)
    shared_core = core_send("shared_grads", [pick(shared_held, core ^ 1, 1)])
    (latent_own,) = Phase(latent_core, shared_core).end(latent_own)
    (latent_own,) = weights_phase.end(latent_own)
    both = (latent_own.astype(F32) + latent_core.held[0].astype(F32)).astype(BF16)
    latent_line = LineSum("latent_grads", both)
    Phase(latent_line, None if serial else out_line[1]).end()
    (latent_mine,) = run(latent_line)
    latent_mine = latent_mine.astype(BF16)
    latent_last = head_send("latent_grads", [latent_mine] * (head_count - 1))
    (latent_mine,) = Phase(latent_last).end(latent_mine)
    if serial:
        run(weight_line)
    else:
        run(weight_line, out_line[0], out_line[1])
    latent_parts = [latent_mine] + latent_last.held
    dweight = weight_line.held
    query_grad = jnp.concatenate(
        [dweight[i * shard : (i + 1) * shard] for i in range(pack.query_parts)], axis=1
    )
    nope = heads * HDIM
    query_grad = jnp.concatenate(
        [
            query_grad[:, :nope].reshape(-1, heads, HDIM),
            query_grad[:, nope : nope + heads * HALF].reshape(-1, heads, HALF),
            query_grad[:, nope + heads * HALF :].reshape(-1, heads, HALF),
        ],
        axis=-1,
    ).reshape(-1, heads * QDIM)
    expand_grad = jnp.concatenate(
        [
            dweight[pack.expand_at + i * pack.rank : pack.expand_at + (i + 1) * pack.rank]
            for i in range(pack.expand_parts)
        ],
        axis=1,
    )
    outproj_grad = dweight[pack.out_at :]

    latent_grad = jnp.zeros((head_count, share, shard), BF16)
    gain_grad = 0.0
    for k in range(head_count):
        latent_grad = lax.dynamic_update_slice_in_dim(
            latent_grad, latent_parts[k][None, :share], head_index ^ k, 0
        )
        gain_grad = gain_grad + latent_parts[k][share:].astype(F32)
    latent_grad = jnp.transpose(latent_grad.reshape(RANK + RDIM, shard)).astype(F32)
    attngain_grad = gain_grad[0]
    ffngain_grad = gain_grad[1]
    lat_grads = gain_grad[2 : 2 + RANK // shard].reshape(RANK)
    latgain_grad = lax.dynamic_slice_in_dim(lat_grads, seq_index * n_lat, n_lat)

    kept, came = pick(shared_held, core, 1), shared_core.held[0]
    paired = jnp.where(core == 0, jnp.stack([kept, came], 1), jnp.stack([came, kept], 1))
    shared_grad = jnp.zeros(paired.shape, BF16)
    for k in range(lines):
        shared_grad = lax.dynamic_update_slice_in_dim(shared_grad, paired[k : k + 1], line ^ k, 0)
    shared_grad = jnp.transpose(shared_grad, (2, 0, 1, 3, 4)).reshape(3, -1, shard).astype(F32)
    shgate_grad = jnp.transpose(shared_grad[0])
    shup_grad = jnp.transpose(shared_grad[1])
    shdown_grad = shared_grad[2]

    if not serial:
        outs = [flow.held for flow in out_line]
    output = (jnp.stack(residual) + jnp.stack(outs)).astype(BF16)

    return (
        output,
        inputs_grad,
        query_grad,
        latent_grad,
        expand_grad,
        outproj_grad,
        shgate_grad,
        shup_grad,
        shdown_grad,
        exgate_grad,
        exup_grad,
        exdown_grad,
        attngain_grad,
        latgain_grad,
        ffngain_grad,
    )


def solution(mesh):
    own = P(None, ("seq", "head"), None)
    stack = P(("seq", "head"), None, None)
    return jax.shard_map(
        local,
        mesh=mesh,
        in_specs=(
            own,
            own,
            P(None, "seq", None),
            P(None, "seq", None),
            P("seq"),
            P("seq"),
            P("seq"),
            P("seq", "head"),
            P("seq", None),
            P("seq", "head"),
            P("head", "seq"),
            P("seq", "head"),
            P("seq", "head"),
            P("head", "seq"),
            stack,
            stack,
            stack,
        ),
        out_specs=(
            own,
            own,
            P("seq", "head"),
            P("seq", None),
            P("seq", "head"),
            P("head", "seq"),
            P("seq", "head"),
            P("seq", "head"),
            P("head", "seq"),
            stack,
            stack,
            stack,
            P("seq"),
            P("seq"),
            P("seq"),
        ),
        check_vma=False,
    )
```

time: 1030 us -> 848 us (0.82)
  waiting for transfers between devices: 408 us -> 239 us
  starting transfers between devices: 240 us -> 170 us
  other arithmetic: 90.4 us -> 127 us
  local copies, waits for them, and re-layouts: 74.2 us -> 93.7 us
    ppermute x123 -> x141, waiting for transfers between devices: 408 us -> 239 us  [swap(): return lax.ppermute(value, axis, [(i, i ^ mask) for i in range(size)])]
    ppermute x123 -> x141, starting transfers between devices: 240 us -> 170 us  [swap(): return lax.ppermute(value, axis, [(i, i ^ mask) for i in range(size)])]
    unnamed x223 -> x433, local copies, waits for them, and re-layouts: 23.9 us -> 57.8 us
    slice x37 -> x12, local copies, waits for them, and re-layouts: 18.3 us -> 3.13 us  [the longest x1 1.06 us: local(): xs_flow = Plane('inputs', inputs[0], inputs[1])]
    reshape x16 -> x15, other arithmetic: 6.18 us -> 18.5 us  [the longest x8 9.94 us: join(): return jnp.stack([held, got], axis=1).reshape((-1,) + held.shape[1:])]
    convert_element_type x32 -> x25, other arithmetic: 28.8 us -> 39.9 us  [the longest x10 17.9 us: add_halves(): (first[i].astype(F32) + second[i].astype(F32)).astype(BF16)]
    pallas_call x8 -> x61, Pallas kernels: 164 us -> 170 us  [the longest x4 115 us: feed(): pl.pallas_call(functools.partial(feed_kernel, orders, per, side, len(earl...]
    dot_general x5 -> x3, matrix products: 29.1 us -> 32.1 us  [dot_tn(): lax.dot_general(a, b, (((0,), (0,)), ((), ())), preferred_element_type=F32)]
  transfers between devices with their start and end apart: 123 -> 141, of which waited for: 50 -> 52; matrix products, arithmetic and copies ran while one was open for 17% -> 20% of each run, Pallas kernels for 16% -> 20%
where the time goes in v2:
time: 848 us; the launch traced here: 836 us
  waiting for transfers between devices  239 us (28%)
  starting transfers between devices  170 us (20%)
  Pallas kernels  170 us (20%)
  other arithmetic  127 us (15%)
  local copies, waits for them, and re-layouts  93.7 us (11%)
  matrix products  32.3 us (4%)
    ppermute x141, waiting for transfers between devices, swap(): return lax.ppermute(value, axis, [(i, i ^ mask) for i in range(size)])  239 us
    ppermute x141, starting transfers between devices, swap(): return lax.ppermute(value, axis, [(i, i ^ mask) for i in range(size)])  170 us
    pallas_call x4, Pallas kernels, feed(): pl.pallas_call(functools.partial(feed_kernel, orders, per, side, len(earl...  115 us
    unnamed x433, local copies, waits for them, and re-layouts  57.8 us
    dot_general x3, matrix products, dot_tn(): lax.dot_general(a, b, (((0,), (0,)), ((), ())), preferred_element_type=F32)  32.1 us
    pallas_call x1, Pallas kernels, attend_back(): pl.pallas_call(functools.partial(attend_back_kernel, pack, heads, bool(ma...  25.4 us
    concatenate x14, other arithmetic, take(): jnp.concatenate([v, g], axis=0)  24.2 us
    convert_element_type x10, other arithmetic, add_halves(): (first[i].astype(F32) + second[i].astype(F32)).astype(BF16)  17.9 us
  transfers between devices with their start and end apart: 141, of which 52 were waited for; matrix products, arithmetic and copies ran while one was open for 20% of the time, Pallas kernels for 20%

profile of v2, /device:TPU:0, one launch (start us, length us, event | category | flops | bytes accessed | tf_op | source)
XLA Modules:
  0.0 836.1 jit_solution(12257693356692254753)
XLA Ops:
  121.0 10.6 %collective-permute-done.27.refs_2_ = bf16[1,560,256]{2,1,0:T(8,128)(2,1)S(1)} collective-permute-done((bf16[1,560,256]{2,1,0:T(8,128)(2,1)S(1)}, bf16[1,560,256]{2,1,0:T(8,128)(2,1)S(1)}, u32[]{:S(2)}, u32[]{:S(2)}) %collective-permute-start.27) | collective-permute-done | bytes 286752 | tf_op jit(solution)/shard_map/output_weights/ppermute | solution.py:59
  142.3 8.1 attend.2
  150.4 8.3 collective-permute-done.30.refs_0_
  178.2 7.9 attend.3
  212.8 7.1 collective-permute-done.47.refs_3_
  229.1 12.1 %collective-permute-done.50.refs_1_ = bf16[1,64,2048]{2,1,0:T(8,128)(2,1)S(1)} collective-permute-done((bf16[1,64,2048]{2,1,0:T(8,128)(2,1)S(1)}, bf16[1,64,2048]{2,1,0:T(8,128)(2,1)S(1)}, u32[]{:S(2)}, u32[]{:S(2)}) %collective-permute-start.50) | collective-permute-done | bytes 262176 | tf_op jit(solution)/shard_map/ffn_rows/ppermute | solution.py:59
  243.5 10.8 %collective-permute-done.49.refs_0_ = bf16[2,64,2048]{2,1,0:T(8,128)(2,1)S(1)} collective-permute-done((bf16[2,64,2048]{2,1,0:T(8,128)(2,1)S(1)}, bf16[2,64,2048]{2,1,0:T(8,128)(2,1)S(1)}, u32[]{:S(2)}, u32[]{:S(2)}) %collective-permute-start.49) | collective-permute-done | bytes 524320 | tf_op jit(solution)/shard_map/ffn_rows/ppermute | solution.py:59
  260.0 8.4 %collective-permute-done.57.refs_2_ = bf16[2,64,2048]{2,1,0:T(8,128)(2,1)S(1)} collective-permute-done((bf16[2,64,2048]{2,1,0:T(8,128)(2,1)S(1)}, bf16[2,64,2048]{2,1,0:T(8,128)(2,1)S(1)}, u32[]{:S(2)}, u32[]{:S(2)}) %collective-permute-start.57) | collective-permute-done | bytes 524320 | tf_op jit(solution)/shard_map/ffn_rows/ppermute | solution.py:59
  289.3 9.9 %collective-permute-done.62.refs_3_ = bf16[2,3,88,256]{3,2,1,0:T(8,128)(2,1)S(1)} collective-permute-done((bf16[2,3,88,256]{3,2,1,0:T(8,128)(2,1)S(1)}, bf16[2,3,88,256]{3,2,1,0:T(8,128)(2,1)S(1)}, u32[]{:S(2)}, u32[]{:S(2)}) %collective-permute-start.62) | collective-permute-done | bytes 270368 | tf_op jit(solution)/shard_map/shared_weights/ppermute | solution.py:59
  313.0 28.3 %feed.4 = (bf16[2,8,128,2048]{3,2,1,0:T(8,128)(2,1)}, bf16[2,8,128,2048]{3,2,1,0:T(8,128)(2,1)}, bf16[2,8,128,704]{3,2,1,0:T(8,128)(2,1)}, bf16[2,8,128,704]{3,2...) custom-call(s32[4,1,256]{2,1,0:T(1,128)} %get-tuple-element.793.refs, ...), custom_call_target="tpu_custom_call" | custom-call | flops 24000000000 | bytes 40000000 | tf_op jit(solution)/shard_map/feed/pallas_call | solution.py:1074
  357.0 15.2 %collective-permute-done.74.refs_1_ = bf16[2,4,32,2048]{3,2,1,0:T(8,128)(2,1)} collective-permute-done((bf16[2,4,32,2048]{3,2,1,0:T(8,128)(2,1)}, bf16[2,4,32,2048]{3,2,1,0:T(8,128)(2,1)}, u32[]{:S(2)}, u32[]{:S(2)}) %collective-permute-start.74) | collective-permute-done | bytes 1048608 | tf_op jit(solution)/shard_map/cotangents/ppermute | solution.py:59
  374.8 29.4 %feed.5 = (bf16[2,8,128,2048]{3,2,1,0:T(8,128)(2,1)}, bf16[2,8,128,2048]{3,2,1,0:T(8,128)(2,1)}, bf16[2,8,128,704]{3,2,1,0:T(8,128)(2,1)}, bf16[2,8,128,704]{3,2...) custom-call(s32[4,1,256]{2,1,0:T(1,128)} %get-tuple-element.789.refs, ...), custom_call_target="tpu_custom_call", output_to_operand_aliasing={{0}: (17, {}), {1}: (18, {}), {2}: (19, {}), {3}: (20, {}),... | custom-call | flops 24000000000 | bytes 40000000 | tf_op jit(solution)/shard_map/feed/pallas_call | solution.py:1074
  414.1 28.0 %feed.6 = (bf16[2,8,128,2048]{3,2,1,0:T(8,128)(2,1)}, bf16[2,8,128,2048]{3,2,1,0:T(8,128)(2,1)}, bf16[2,8,128,704]{3,2,1,0:T(8,128)(2,1)}, bf16[2,8,128,704]{3,2...) custom-call(s32[4,1,256]{2,1,0:T(1,128)} %get-tuple-element.792.refs, ...), custom_call_target="tpu_custom_call", output_to_operand_aliasing={{0}: (15, {}), {1}: (16, {}), {2}: (17, {}), {3}: (18, {}),... | custom-call | flops 24000000000 | bytes 40000000 | tf_op jit(solution)/shard_map/feed/pallas_call | solution.py:1074
  455.8 29.7 %feed.7 = (bf16[2,8,128,2048]{3,2,1,0:T(8,128)(2,1)}, bf16[2,8,128,2048]{3,2,1,0:T(8,128)(2,1)}, bf16[2,8,128,704]{3,2,1,0:T(8,128)(2,1)}, bf16[2,8,128,704]{3,2...) custom-call(s32[4,1,256]{2,1,0:T(1,128)} %get-tuple-element.788.refs, ...), custom_call_target="tpu_custom_call", output_to_operand_aliasing={{0}: (17, {}), {1}: (18, {}), {2}: (19, {}), {3}: (20, {}),... | custom-call | flops 24000000000 | bytes 40000000 | tf_op jit(solution)/shard_map/feed/pallas_call | solution.py:1074
  504.2 11.4 %fusion.88.refs_3_ = f32[704,2048]{1,0:T(8,128)} fusion(bf16[2048,704]{1,0:T(8,128)(2,1)} %after.3, bf16[2048,2048]{1,0:T(8,128)(2,1)} %bitcast.596), kind=kOutput, calls=%fused_computation.324 | convolution fusion | flops 5905580032 | bytes 17039360 | tf_op jit(solution)/shard_map/dot_general | solution.py:37
  529.5 10.2 %fusion.89.refs_3_ = f32[704,2048]{1,0:T(8,128)} fusion(bf16[2048,704]{1,0:T(8,128)(2,1)S(1)} %copy-done.95, bf16[2048,2048]{1,0:T(8,128)(2,1)} %bitcast.597), kind=kOutput, calls=%fused_computation.325 | convolution fusion | flops 5905580032 | bytes 17039360 | tf_op jit(solution)/shard_map/dot_general | solution.py:37
  547.3 10.4 %fusion.90.refs_3_ = f32[704,2048]{1,0:T(8,128)} fusion(bf16[2048,704]{1,0:T(8,128)(2,1)S(1)} %copy-done.94, bf16[2048,2048]{1,0:T(8,128)(2,1)} %get-tuple-element.528), kind=kOutput, calls=%fused_computation.326 | convolution fusion | flops 5905580032 | bytes 17039360 | tf_op jit(solution)/shard_map/dot_general | solution.py:37
  562.6 10.7 %collective-permute-done.102.refs_0_ = bf16[1,64,2048]{2,1,0:T(8,128)(2,1)S(1)} collective-permute-done((bf16[1,64,2048]{2,1,0:T(8,128)(2,1)S(1)}, bf16[1,64,2048]{2,1,0:T(8,128)(2,1)S(1)}, u32[]{:S(2)}, u32[]{:S(2)}) %collective-permute-start.102) | collective-permute-done | bytes 262176 | tf_op jit(solution)/shard_map/ffn_grads/ppermute | solution.py:59
  608.7 25.4 %attend_back.1 = (bf16[2,64,2048]{2,1,0:T(8,128)(2,1)}, bf16[2,64,2048]{2,1,0:T(8,128)(2,1)}, bf16[2,64,2048]{2,1,0:T(8,128)(2,1)}, bf16[2,64,2048]{2,1,0:T(8,12...) custom-call(s32[2]{0:T(128)} %copy-done.48, ...), custom_call_target="tpu_custom_call" | custom-call | flops 32000000000 | bytes 30000000 | tf_op jit(solution)/shard_map/attend_back/pallas_call | solution.py:767
  669.1 9.1 %collective-permute-done.115.refs_0_ = bf16[4,2,64,640]{3,2,1,0:T(8,128)(2,1)S(1)} collective-permute-done((bf16[4,2,64,640]{3,2,1,0:T(8,128)(2,1)S(1)}, bf16[4,2,64,640]{3,2,1,0:T(8,128)(2,1)S(1)}, u32[]{:S(2)}, u32[]{:S(2)}) %collective-permute-start.115) | collective-permute-done | bytes 655392 | tf_op jit(solution)/shard_map/key_grads/ppermute | solution.py:59
  678.7 13.5 %collective-permute-done.117.refs_2_ = bf16[4,2,64,640]{3,2,1,0:T(8,128)(2,1)S(1)} collective-permute-done((bf16[4,2,64,640]{3,2,1,0:T(8,128)(2,1)S(1)}, bf16[4,2,64,640]{3,2,1,0:T(8,128)(2,1)S(1)}, u32[]{:S(2)}, u32[]{:S(2)}) %collective-permute-start.117) | collective-permute-done | bytes 655392 | tf_op jit(solution)/shard_map/key_grads/ppermute | solution.py:59
  714.5 21.1 %collective-permute-start.127 = (bf16[1,64,2048]{2,1,0:T(8,128)(2,1)}, bf16[1,64,2048]{2,1,0:T(8,128)(2,1)S(1)}, u32[]{:S(2)}, u32[]{:S(2)}) collective-permute-start(bf16[1,64,2048]{2,1,0:T(8,128)(2,1)} %slice_bitcast_fusion.22), channel_id=1, source_target_pairs={{0,4},{1,5},{2,6},{3,7},{4,0},{5,1},{6,2},{7,3},{8,12},{9,13},{10,... | collective-permute-start | bytes 786440 | tf_op jit(solution)/shard_map/outputs/ppermute | solution.py:59
  740.6 8.8 %collective-permute-start.124 = (bf16[1,2,64,640]{3,2,1,0:T(8,128)(2,1)S(1)}, bf16[1,2,64,640]{3,2,1,0:T(8,128)(2,1)}, u32[]{:S(2)}, u32[]{:S(2)}) collective-permute-start(bf16[1,2,64,640]{3,2,1,0:T(8,128)(2,1)S(1)} %slice_bitcast_fusion.31), channel_id=1, source_target_pairs={{0,4},{1,5},{2,6},{3,7},{4,0},{5,1},{6,2},{7,3},{8,12},{9,13},{10,... | collective-permute-start | bytes 491528 | tf_op jit(solution)/shard_map/key_grads/ppermute | solution.py:59
  753.8 14.5 %collective-permute-done.124.refs_0_ = bf16[1,2,64,640]{3,2,1,0:T(8,128)(2,1)} collective-permute-done((bf16[1,2,64,640]{3,2,1,0:T(8,128)(2,1)S(1)}, bf16[1,2,64,640]{3,2,1,0:T(8,128)(2,1)}, u32[]{:S(2)}, u32[]{:S(2)}) %collective-permute-start.124) | collective-permute-done | bytes 163872 | tf_op jit(solution)/shard_map/key_grads/ppermute | solution.py:59
  (985 shorter events, 483.3 us)
Async XLA Ops:
  307.9 33.4 %collective-permute-start.67 = (bf16[1,4,32,2048]{3,2,1,0:T(8,128)(2,1)}, bf16[1,4,32,2048]{3,2,1,0:T(8,128)(2,1)S(1)}, u32[]{:S(2)}, u32[]{:S(2)}) collective-permute-start(bf16[1,4,32,2048]{3,2,1,0:T(8,128)(2,1)} %get-tuple-element.731), channel_id=1, source_target_pairs={{0,8},{8,0},{16,24},{24,16},{1,9},{9,1},{17,25},{25,17},{2,10},{10... | collective-permute-start | bytes 1572872 | tf_op jit(solution)/shard_map/cotangents/ppermute | solution.py:59
  308.6 32.7 %collective-permute-start.68 = (bf16[1,4,32,2048]{3,2,1,0:T(8,128)(2,1)}, bf16[1,4,32,2048]{3,2,1,0:T(8,128)(2,1)}, u32[]{:S(2)}, u32[]{:S(2)}) collective-permute-start(bf16[1,4,32,2048]{3,2,1,0:T(8,128)(2,1)} %get-tuple-element.730), channel_id=1, source_target_pairs={{0,16},{8,24},{16,0},{24,8},{1,17},{9,25},{17,1},{25,9},{2,18},{10... | collective-permute-start | bytes 1572872 | tf_op jit(solution)/shard_map/cotangents/ppermute | solution.py:59
  350.9 53.9 %collective-permute-start.83 = (bf16[2,4,32,2048]{3,2,1,0:T(8,128)(2,1)}, bf16[2,4,32,2048]{3,2,1,0:T(8,128)(2,1)}, u32[]{:S(2)}, u32[]{:S(2)}) collective-permute-start(bf16[2,4,32,2048]{3,2,1,0:T(8,128)(2,1)} %pad_maximum_fusion.16.refs_8_), channel_id=1, source_target_pairs={{0,1},{1,0},{2,3},{3,2},{4,5},{5,4},{6,7},{7,6},{8,9},{9,8},{10,11... | collective-permute-start | bytes 3145736 | tf_op jit(solution)/shard_map/cotangents/ppermute | solution.py:59
  355.5 49.4 %collective-permute-start.81 = (bf16[2,4,32,2048]{3,2,1,0:T(8,128)(2,1)}, bf16[2,4,32,2048]{3,2,1,0:T(8,128)(2,1)}, u32[]{:S(2)}, u32[]{:S(2)}) collective-permute-start(bf16[2,4,32,2048]{3,2,1,0:T(8,128)(2,1)} %pad_maximum_fusion.15.refs_6_), channel_id=1, source_target_pairs={{0,1},{1,0},{2,3},{3,2},{4,5},{5,4},{6,7},{7,6},{8,9},{9,8},{10,11... | collective-permute-start | bytes 3145736 | tf_op jit(solution)/shard_map/cotangents/ppermute | solution.py:59
  356.0 48.2 %collective-permute-start.72 = (bf16[2,4,32,2048]{3,2,1,0:T(8,128)(2,1)}, bf16[2,4,32,2048]{3,2,1,0:T(8,128)(2,1)}, u32[]{:S(2)}, u32[]{:S(2)}) collective-permute-start(bf16[2,4,32,2048]{3,2,1,0:T(8,128)(2,1)} %pad_maximum_fusion.14.refs_4_), channel_id=1, source_target_pairs={{0,8},{8,0},{16,24},{24,16},{1,9},{9,1},{17,25},{25,17},{2,10},{10... | collective-permute-start | bytes 3145736 | tf_op jit(solution)/shard_map/ffn_rows/ppermute | solution.py:59
  372.2 33.1 %collective-permute-start.87 = (bf16[2,4,32,2048]{3,2,1,0:T(8,128)(2,1)}, bf16[2,4,32,2048]{3,2,1,0:T(8,128)(2,1)}, u32[]{:S(2)}, u32[]{:S(2)}) collective-permute-start(bf16[2,4,32,2048]{3,2,1,0:T(8,128)(2,1)} %pad_maximum_fusion.14.refs_4_), channel_id=1, source_target_pairs={{0,1},{1,0},{2,3},{3,2},{4,5},{5,4},{6,7},{7,6},{8,9},{9,8},{10,11... | collective-permute-start | bytes 3145736 | tf_op jit(solution)/shard_map/ffn_rows/ppermute | solution.py:59
  407.2 35.0 %collective-permute-start.79 = (bf16[2,4,32,2048]{3,2,1,0:T(8,128)(2,1)}, bf16[2,4,32,2048]{3,2,1,0:T(8,128)(2,1)}, u32[]{:S(2)}, u32[]{:S(2)}) collective-permute-start(bf16[2,4,32,2048]{3,2,1,0:T(8,128)(2,1)} %get-tuple-element.468), channel_id=1, source_target_pairs={{0,16},{8,24},{16,0},{24,8},{1,17},{9,25},{17,1},{25,9},{2,18},{10... | collective-permute-start | bytes 3145736 | tf_op jit(solution)/shard_map/ffn_grads/ppermute | solution.py:59
  410.2 32.0 %collective-permute-start.80 = (bf16[2,4,32,2048]{3,2,1,0:T(8,128)(2,1)}, bf16[2,4,32,2048]{3,2,1,0:T(8,128)(2,1)}, u32[]{:S(2)}, u32[]{:S(2)}) collective-permute-start(bf16[2,4,32,2048]{3,2,1,0:T(8,128)(2,1)} %get-tuple-element.469), channel_id=1, source_target_pairs={{0,8},{8,0},{16,24},{24,16},{1,9},{9,1},{17,25},{25,17},{2,10},{10... | collective-permute-start | bytes 3145736 | tf_op jit(solution)/shard_map/ffn_grads/ppermute | solution.py:59
  442.8 54.5 %collective-permute-start.77 = (bf16[2,4,32,2048]{3,2,1,0:T(8,128)(2,1)}, bf16[2,4,32,2048]{3,2,1,0:T(8,128)(2,1)}, u32[]{:S(2)}, u32[]{:S(2)}) collective-permute-start(bf16[2,4,32,2048]{3,2,1,0:T(8,128)(2,1)} %get-tuple-element.462), channel_id=1, source_target_pairs={{0,16},{8,24},{16,0},{24,8},{1,17},{9,25},{17,1},{25,9},{2,18},{10... | collective-permute-start | bytes 3145736 | tf_op jit(solution)/shard_map/outputs/ppermute | solution.py:59
  443.9 53.4 %collective-permute-start.78 = (bf16[2,4,32,2048]{3,2,1,0:T(8,128)(2,1)}, bf16[2,4,32,2048]{3,2,1,0:T(8,128)(2,1)}, u32[]{:S(2)}, u32[]{:S(2)}) collective-permute-start(bf16[2,4,32,2048]{3,2,1,0:T(8,128)(2,1)} %get-tuple-element.463), channel_id=1, source_target_pairs={{0,8},{8,0},{16,24},{24,16},{1,9},{9,1},{17,25},{25,17},{2,10},{10... | collective-permute-start | bytes 3145736 | tf_op jit(solution)/shard_map/outputs/ppermute | solution.py:59
  447.2 38.3 %collective-permute-start.92 = (bf16[1,4,32,2048]{3,2,1,0:T(8,128)(2,1)}, bf16[1,4,32,2048]{3,2,1,0:T(8,128)(2,1)S(1)}, u32[]{:S(2)}, u32[]{:S(2)}) collective-permute-start(bf16[1,4,32,2048]{3,2,1,0:T(8,128)(2,1)} %add_convert_fusion.29), channel_id=1, source_target_pairs={{0,16},{8,24},{16,0},{24,8},{1,17},{9,25},{17,1},{25,9},{2,18},{10... | collective-permute-start | bytes 1572872 | tf_op jit(solution)/shard_map/ffn_grads/ppermute | solution.py:59
  449.8 35.7 %collective-permute-start.91 = (bf16[1,4,32,2048]{3,2,1,0:T(8,128)(2,1)}, bf16[1,4,32,2048]{3,2,1,0:T(8,128)(2,1)}, u32[]{:S(2)}, u32[]{:S(2)}) collective-permute-start(bf16[1,4,32,2048]{3,2,1,0:T(8,128)(2,1)} %add_convert_fusion.30), channel_id=1, source_target_pairs={{0,8},{8,0},{16,24},{24,16},{1,9},{9,1},{17,25},{25,17},{2,10},{10... | collective-permute-start | bytes 1572872 | tf_op jit(solution)/shard_map/ffn_grads/ppermute | solution.py:59
  500.5 57.3 %collective-permute-start.101 = (bf16[1,4,32,2048]{3,2,1,0:T(8,128)(2,1)}, bf16[1,4,32,2048]{3,2,1,0:T(8,128)(2,1)}, u32[]{:S(2)}, u32[]{:S(2)}) collective-permute-start(bf16[1,4,32,2048]{3,2,1,0:T(8,128)(2,1)} %add_convert_fusion.17), channel_id=1, source_target_pairs={{0,16},{8,24},{16,0},{24,8},{1,17},{9,25},{17,1},{25,9},{2,18},{10... | collective-permute-start | bytes 1572872 | tf_op jit(solution)/shard_map/outputs/ppermute | solution.py:59
  503.2 54.6 %collective-permute-start.100 = (bf16[1,4,32,2048]{3,2,1,0:T(8,128)(2,1)}, bf16[1,4,32,2048]{3,2,1,0:T(8,128)(2,1)}, u32[]{:S(2)}, u32[]{:S(2)}) collective-permute-start(bf16[1,4,32,2048]{3,2,1,0:T(8,128)(2,1)} %add_convert_fusion.18), channel_id=1, source_target_pairs={{0,8},{8,0},{16,24},{24,16},{1,9},{9,1},{17,25},{25,17},{2,10},{10... | collective-permute-start | bytes 1572872 | tf_op jit(solution)/shard_map/outputs/ppermute | solution.py:59
  598.1 36.0 %collective-permute-start.110 = (bf16[2,3,88,256]{3,2,1,0:T(8,128)(2,1)}, bf16[2,3,88,256]{3,2,1,0:T(8,128)(2,1)}, u32[]{:S(2)}, u32[]{:S(2)}) collective-permute-start(bf16[2,3,88,256]{3,2,1,0:T(8,128)(2,1)} %bitcast.469), channel_id=1, source_target_pairs={{0,2},{1,3},{2,0},{3,1},{4,6},{5,7},{6,4},{7,5},{8,10},{9,11},{10,... | collective-permute-start | bytes 811016 | tf_op jit(solution)/shard_map/shared_grads/ppermute | solution.py:59
  598.9 35.2 %collective-permute-start.111 = (bf16[2,3,88,256]{3,2,1,0:T(8,128)(2,1)}, bf16[2,3,88,256]{3,2,1,0:T(8,128)(2,1)}, u32[]{:S(2)}, u32[]{:S(2)}) collective-permute-start(bf16[2,3,88,256]{3,2,1,0:T(8,128)(2,1)} %bitcast.468), channel_id=1, source_target_pairs={{0,4},{1,5},{2,6},{3,7},{4,0},{5,1},{6,2},{7,3},{8,12},{9,13},{10,... | collective-permute-start | bytes 811016 | tf_op jit(solution)/shard_map/shared_grads/ppermute | solution.py:59
  601.8 32.3 %collective-permute-start.112 = (bf16[2,3,88,256]{3,2,1,0:T(8,128)(2,1)}, bf16[2,3,88,256]{3,2,1,0:T(8,128)(2,1)}, u32[]{:S(2)}, u32[]{:S(2)}) collective-permute-start(bf16[2,3,88,256]{3,2,1,0:T(8,128)(2,1)} %bitcast.467), channel_id=1, source_target_pairs={{0,6},{1,7},{2,4},{3,5},{4,2},{5,3},{6,0},{7,1},{8,14},{9,15},{10,... | collective-permute-start | bytes 811016 | tf_op jit(solution)/shard_map/shared_grads/ppermute | solution.py:59
  647.7 44.5 %collective-permute-start.118 = (bf16[2,1536,256]{2,1,0:T(8,128)(2,1)S(1)}, bf16[2,1536,256]{2,1,0:T(8,128)(2,1)S(1)}, u32[]{:S(2)}, u32[]{:S(2)}) collective-permute-start(bf16[2,1536,256]{2,1,0:T(8,128)(2,1)S(1)} %slice_bitcast_fusion.1), channel_id=1, source_target_pairs={{0,2},{1,3},{2,0},{3,1},{4,6},{5,7},{6,4},{7,5},{8,10},{9,11},{10,... | collective-permute-start | bytes 4718600 | tf_op jit(solution)/shard_map/weight_grads/ppermute | solution.py:59
  699.6 36.0 %collective-permute-start.121 = (bf16[2,64,2048]{2,1,0:T(8,128)(2,1)}, bf16[2,64,2048]{2,1,0:T(8,128)(2,1)}, u32[]{:S(2)}, u32[]{:S(2)}) collective-permute-start(bf16[2,64,2048]{2,1,0:T(8,128)(2,1)} %get-tuple-element.582), channel_id=1, source_target_pairs={{0,8},{8,0},{16,24},{24,16},{1,9},{9,1},{17,25},{25,17},{2,10},{10... | collective-permute-start | bytes 1572872 | tf_op jit(solution)/shard_map/normed_grads/ppermute | solution.py:59
  701.2 34.4 %collective-permute-start.122 = (bf16[1,4,32,2048]{3,2,1,0:T(8,128)(2,1)}, bf16[1,4,32,2048]{3,2,1,0:T(8,128)(2,1)}, u32[]{:S(2)}, u32[]{:S(2)}) collective-permute-start(bf16[1,4,32,2048]{3,2,1,0:T(8,128)(2,1)} %get-tuple-element.583), channel_id=1, source_target_pairs={{0,8},{8,0},{16,24},{24,16},{1,9},{9,1},{17,25},{25,17},{2,10},{10... | collective-permute-start | bytes 1572872 | tf_op jit(solution)/shard_map/outputs/ppermute | solution.py:59
  701.6 34.0 %collective-permute-start.123 = (bf16[1,4,32,2048]{3,2,1,0:T(8,128)(2,1)}, bf16[1,4,32,2048]{3,2,1,0:T(8,128)(2,1)}, u32[]{:S(2)}, u32[]{:S(2)}) collective-permute-start(bf16[1,4,32,2048]{3,2,1,0:T(8,128)(2,1)} %get-tuple-element.584), channel_id=1, source_target_pairs={{0,16},{8,24},{16,0},{24,8},{1,17},{9,25},{17,1},{25,9},{2,18},{10... | collective-permute-start | bytes 1572872 | tf_op jit(solution)/shard_map/outputs/ppermute | solution.py:59
  706.9 86.7 %collective-permute-start.133 = (bf16[4,3,88,256]{3,2,1,0:T(8,128)(2,1)}, bf16[4,3,88,256]{3,2,1,0:T(8,128)(2,1)}, u32[]{:S(2)}, u32[]{:S(2)}) collective-permute-start(bf16[4,3,88,256]{3,2,1,0:T(8,128)(2,1)} %get-tuple-element.719), channel_id=1, source_target_pairs={{0,1},{1,0},{2,3},{3,2},{4,5},{5,4},{6,7},{7,6},{8,9},{9,8},{10,11... | collective-permute-start | bytes 1622024 | tf_op jit(solution)/shard_map/shared_grads/ppermute | solution.py:59
  714.5 39.2 %collective-permute-start.127 = (bf16[1,64,2048]{2,1,0:T(8,128)(2,1)}, bf16[1,64,2048]{2,1,0:T(8,128)(2,1)S(1)}, u32[]{:S(2)}, u32[]{:S(2)}) collective-permute-start(bf16[1,64,2048]{2,1,0:T(8,128)(2,1)} %slice_bitcast_fusion.22), channel_id=1, source_target_pairs={{0,4},{1,5},{2,6},{3,7},{4,0},{5,1},{6,2},{7,3},{8,12},{9,13},{10,... | collective-permute-start | bytes 786440 | tf_op jit(solution)/shard_map/outputs/ppermute | solution.py:59
  753.7 41.3 %collective-permute-start.128 = (bf16[1,1536,256]{2,1,0:T(8,128)(2,1)}, bf16[1,1536,256]{2,1,0:T(8,128)(2,1)}, u32[]{:S(2)}, u32[]{:S(2)}) collective-permute-start(bf16[1,1536,256]{2,1,0:T(8,128)(2,1)} %slice_bitcast_fusion.3), channel_id=1, source_target_pairs={{0,4},{1,5},{2,6},{3,7},{4,0},{5,1},{6,2},{7,3},{8,12},{9,13},{10,... | collective-permute-start | bytes 2359304 | tf_op jit(solution)/shard_map/weight_grads/ppermute | solution.py:59
  (327 other events, 3145.4 us)

commit v3 on v2

--- a/solution.py
+++ b/solution.py
@@ -162,8 +162,8 @@
 
 
 class Plane:
-    def __init__(self, name, first, second):
-        self.name, self.held = name, [first[None], second[None]]
+    def __init__(self, name, first, second, hold=False):
+        self.name, self.held, self.hold = name, [first[None], second[None]], hold
         self.rest = bits_of(lax.axis_size("head"))
 
     def send(self):
@@ -275,10 +275,15 @@
         self.sent = [flow.send() for flow in self.flows]
 
     def end(self, *others):
-        flat = [v for got in self.sent for v in got] + list(others)
+        planes = [f for f in self.flows if isinstance(f, Plane) and f.hold and len(f.rest) == 1]
+        flat = [v for got in self.sent for v in got]
+        flat += [v for flow in planes for v in flow.held] + list(others)
         flat = list(sync(*flat))
-        for flow, got in zip(self.flows, self.sent):
-            flow.take([flat.pop(0) for _ in got])
+        sent = [[flat.pop(0) for _ in got] for got in self.sent]
+        for flow in planes:
+            flow.held = [flat.pop(0) for _ in flow.held]
+        for flow, got in zip(self.flows, sent):
+            flow.take(got)
         return flat
 
 
@@ -1284,8 +1289,8 @@
         ffn_hat.append(hat_b)
         return Line("ffn_rows", (hat_b * gain_ffn).astype(BF16))
 
-    def halves_of(name, value):
-        return Plane(name, value[:, :half], value[:, half:])
+    def halves_of(name, value, hold=False):
+        return Plane(name, value[:, :half], value[:, half:], hold)
 
     def keep(b, att):
         saved[b] = (*saved[b][:2], att, saved[b][3])
@@ -1343,8 +1348,8 @@
         run(row_planes[0])
         row_core = [core_send("ffn_rows", row_planes[0].held), None]
         cot_late, row_late = Phase(row_core[0]).end(cot_late, row_late)
-        cots[1] = halves_of("cotangents", cot_late)
-        row_planes[1] = halves_of("ffn_rows", row_late)
+        cots[1] = halves_of("cotangents", cot_late, True)
+        row_planes[1] = halves_of("ffn_rows", row_late, True)
     hidden_each = shared_gate.shape[1] // seq_count
     hidden_pad = -(-hidden_each // 128) * 128
     sgut, sdown = shared_whole(here, [pick(paired, line)] + shared_moves.held, hidden_pad)
@@ -1544,9 +1549,9 @@
         total = total + value.astype(F32)
     key_line = LineSum("key_grads", total.astype(BF16))
     normed_sum = PlaneSum("normed_grads", gparts[:2], gparts[2:])
-    Phase(key_line, normed_sum, late).end()
+    Phase(key_line, normed_sum, None if serial else out_line[0]).end()
     while key_line.more:
-        Phase(key_line, normed_sum, None if serial else out_line[0]).end()
+        Phase(key_line, normed_sum, late).end()
     run(normed_sum)
     own_tiled = [jnp.tile(t, (batches, 1)) for t in (own_cos, own_sin)]
     grad_latent, latgain_term = key_back(

time: 848 us -> 835 us (0.985)
  waiting for transfers between devices: 239 us -> 230 us
    ppermute x141, waiting for transfers between devices: 239 us -> 230 us  [swap(): return lax.ppermute(value, axis, [(i, i ^ mask) for i in range(size)])]
    unnamed x433 -> x435, local copies, waits for them, and re-layouts: 57.8 us -> 55.4 us
  transfers between devices with their start and end apart: 141 -> 141, of which waited for: 52 -> 55; matrix products, arithmetic and copies ran while one was open for 20% -> 21% of each run, Pallas kernels for 20% -> 21%
where the time goes in v3:
time: 835 us; the launch traced here: 823 us
  waiting for transfers between devices  230 us (28%)
  Pallas kernels  170 us (20%)
  starting transfers between devices  168 us (20%)
  other arithmetic  128 us (15%)
  local copies, waits for them, and re-layouts  91.6 us (11%)
  matrix products  32.3 us (4%)
    ppermute x141, waiting for transfers between devices, swap(): return lax.ppermute(value, axis, [(i, i ^ mask) for i in range(size)])  230 us
    ppermute x141, starting transfers between devices, swap(): return lax.ppermute(value, axis, [(i, i ^ mask) for i in range(size)])  168 us
    pallas_call x4, Pallas kernels, feed(): pl.pallas_call(functools.partial(feed_kernel, orders, per, side, len(earl...  115 us
    unnamed x435, local copies, waits for them, and re-layouts  55.4 us
    dot_general x3, matrix products, dot_tn(): lax.dot_general(a, b, (((0,), (0,)), ((), ())), preferred_element_type=F32)  32.1 us
    pallas_call x1, Pallas kernels, attend_back(): pl.pallas_call(functools.partial(attend_back_kernel, pack, heads, bool(ma...  25.4 us
    concatenate x14, other arithmetic, take(): jnp.concatenate([v, g], axis=0)  24.2 us
    convert_element_type x10, other arithmetic, add_halves(): (first[i].astype(F32) + second[i].astype(F32)).astype(BF16)  17.8 us
  transfers between devices with their start and end apart: 141, of which 55 were waited for; matrix products, arithmetic and copies ran while one was open for 21% of the time, Pallas kernels for 21%

profile of v3, /device:TPU:0, one launch (start us, length us, event | category | flops | bytes accessed | tf_op | source)
XLA Modules:
  0.0 823.2 jit_solution(3807100602465327756)
XLA Ops:
  121.0 10.6 %collective-permute-done.27.refs_2_ = bf16[1,560,256]{2,1,0:T(8,128)(2,1)S(1)} collective-permute-done((bf16[1,560,256]{2,1,0:T(8,128)(2,1)S(1)}, bf16[1,560,256]{2,1,0:T(8,128)(2,1)S(1)}, u32[]{:S(2)}, u32[]{:S(2)}) %collective-permute-start.27) | collective-permute-done | bytes 286752 | tf_op jit(solution)/shard_map/output_weights/ppermute | solution.py:59
  142.3 8.1 attend.2
  150.4 8.3 %collective-permute-done.30.refs_0_ = bf16[2,560,256]{2,1,0:T(8,128)(2,1)S(1)} collective-permute-done((bf16[2,560,256]{2,1,0:T(8,128)(2,1)}, bf16[2,560,256]{2,1,0:T(8,128)(2,1)S(1)}, u32[]{:S(2)}, u32[]{:S(2)}) %collective-permute-start.30) | collective-permute-done | bytes 573472 | tf_op jit(solution)/shard_map/output_weights/ppermute | solution.py:59
  178.2 7.9 attend.3
  229.1 12.1 %collective-permute-done.50.refs_1_ = bf16[1,64,2048]{2,1,0:T(8,128)(2,1)S(1)} collective-permute-done((bf16[1,64,2048]{2,1,0:T(8,128)(2,1)S(1)}, bf16[1,64,2048]{2,1,0:T(8,128)(2,1)S(1)}, u32[]{:S(2)}, u32[]{:S(2)}) %collective-permute-start.50) | collective-permute-done | bytes 262176 | tf_op jit(solution)/shard_map/ffn_rows/ppermute | solution.py:59
  243.5 10.8 %collective-permute-done.49.refs_0_ = bf16[2,64,2048]{2,1,0:T(8,128)(2,1)S(1)} collective-permute-done((bf16[2,64,2048]{2,1,0:T(8,128)(2,1)S(1)}, bf16[2,64,2048]{2,1,0:T(8,128)(2,1)S(1)}, u32[]{:S(2)}, u32[]{:S(2)}) %collective-permute-start.49) | collective-permute-done | bytes 524320 | tf_op jit(solution)/shard_map/ffn_rows/ppermute | solution.py:59
  259.9 8.4 %collective-permute-done.57.refs_2_ = bf16[2,64,2048]{2,1,0:T(8,128)(2,1)S(1)} collective-permute-done((bf16[2,64,2048]{2,1,0:T(8,128)(2,1)S(1)}, bf16[2,64,2048]{2,1,0:T(8,128)(2,1)S(1)}, u32[]{:S(2)}, u32[]{:S(2)}) %collective-permute-start.57) | collective-permute-done | bytes 524320 | tf_op jit(solution)/shard_map/ffn_rows/ppermute | solution.py:59
  289.4 9.9 %collective-permute-done.62.refs_3_ = bf16[2,3,88,256]{3,2,1,0:T(8,128)(2,1)S(1)} collective-permute-done((bf16[2,3,88,256]{3,2,1,0:T(8,128)(2,1)S(1)}, bf16[2,3,88,256]{3,2,1,0:T(8,128)(2,1)S(1)}, u32[]{:S(2)}, u32[]{:S(2)}) %collective-permute-start.62) | collective-permute-done | bytes 270368 | tf_op jit(solution)/shard_map/shared_weights/ppermute | solution.py:59
  313.0 28.3 %feed.4 = (bf16[2,8,128,2048]{3,2,1,0:T(8,128)(2,1)}, bf16[2,8,128,2048]{3,2,1,0:T(8,128)(2,1)}, bf16[2,8,128,704]{3,2,1,0:T(8,128)(2,1)}, bf16[2,8,128,704]{3,2...) custom-call(s32[4,1,256]{2,1,0:T(1,128)} %get-tuple-element.801.refs, ...), custom_call_target="tpu_custom_call" | custom-call | flops 24000000000 | bytes 40000000 | tf_op jit(solution)/shard_map/feed/pallas_call | solution.py:1079
  357.9 29.3 %feed.5 = (bf16[2,8,128,2048]{3,2,1,0:T(8,128)(2,1)}, bf16[2,8,128,2048]{3,2,1,0:T(8,128)(2,1)}, bf16[2,8,128,704]{3,2,1,0:T(8,128)(2,1)}, bf16[2,8,128,704]{3,2...) custom-call(s32[4,1,256]{2,1,0:T(1,128)} %get-tuple-element.797.refs, ...), custom_call_target="tpu_custom_call", output_to_operand_aliasing={{0}: (17, {}), {1}: (18, {}), {2}: (19, {}), {3}: (20, {}),... | custom-call | flops 24000000000 | bytes 40000000 | tf_op jit(solution)/shard_map/feed/pallas_call | solution.py:1079
  387.3 7.7 collective-permute-done.72.refs_1_
  411.1 28.1 %feed.6 = (bf16[2,8,128,2048]{3,2,1,0:T(8,128)(2,1)}, bf16[2,8,128,2048]{3,2,1,0:T(8,128)(2,1)}, bf16[2,8,128,704]{3,2,1,0:T(8,128)(2,1)}, bf16[2,8,128,704]{3,2...) custom-call(s32[4,1,256]{2,1,0:T(1,128)} %get-tuple-element.800.refs, ...), custom_call_target="tpu_custom_call", output_to_operand_aliasing={{0}: (15, {}), {1}: (16, {}), {2}: (17, {}), {3}: (18, {}),... | custom-call | flops 24000000000 | bytes 40000000 | tf_op jit(solution)/shard_map/feed/pallas_call | solution.py:1079
  452.8 29.7 %feed.7 = (bf16[2,8,128,2048]{3,2,1,0:T(8,128)(2,1)}, bf16[2,8,128,2048]{3,2,1,0:T(8,128)(2,1)}, bf16[2,8,128,704]{3,2,1,0:T(8,128)(2,1)}, bf16[2,8,128,704]{3,2...) custom-call(s32[4,1,256]{2,1,0:T(1,128)} %get-tuple-element.796.refs, ...), custom_call_target="tpu_custom_call", output_to_operand_aliasing={{0}: (17, {}), {1}: (18, {}), {2}: (19, {}), {3}: (20, {}),... | custom-call | flops 24000000000 | bytes 40000000 | tf_op jit(solution)/shard_map/feed/pallas_call | solution.py:1079
  501.1 11.4 %fusion.88.refs_3_ = f32[704,2048]{1,0:T(8,128)} fusion(bf16[2048,704]{1,0:T(8,128)(2,1)} %after.3, bf16[2048,2048]{1,0:T(8,128)(2,1)} %bitcast.596), kind=kOutput, calls=%fused_computation.324 | convolution fusion | flops 5905580032 | bytes 17039360 | tf_op jit(solution)/shard_map/dot_general | solution.py:37
  526.8 10.2 %fusion.89.refs_3_ = f32[704,2048]{1,0:T(8,128)} fusion(bf16[2048,704]{1,0:T(8,128)(2,1)S(1)} %copy-done.94, bf16[2048,2048]{1,0:T(8,128)(2,1)} %bitcast.597), kind=kOutput, calls=%fused_computation.325 | convolution fusion | flops 5905580032 | bytes 17039360 | tf_op jit(solution)/shard_map/dot_general | solution.py:37
  544.2 10.4 %fusion.90.refs_3_ = f32[704,2048]{1,0:T(8,128)} fusion(bf16[2048,704]{1,0:T(8,128)(2,1)S(1)} %copy-done.93, bf16[2048,2048]{1,0:T(8,128)(2,1)} %get-tuple-element.536), kind=kOutput, calls=%fused_computation.326 | convolution fusion | flops 5905580032 | bytes 17039360 | tf_op jit(solution)/shard_map/dot_general | solution.py:37
  559.4 10.8 %collective-permute-done.102.refs_0_ = bf16[1,64,2048]{2,1,0:T(8,128)(2,1)S(1)} collective-permute-done((bf16[1,64,2048]{2,1,0:T(8,128)(2,1)S(1)}, bf16[1,64,2048]{2,1,0:T(8,128)(2,1)S(1)}, u32[]{:S(2)}, u32[]{:S(2)}) %collective-permute-start.102) | collective-permute-done | bytes 262176 | tf_op jit(solution)/shard_map/ffn_grads/ppermute | solution.py:59
  605.6 25.4 %attend_back.1 = (bf16[2,64,2048]{2,1,0:T(8,128)(2,1)}, bf16[2,64,2048]{2,1,0:T(8,128)(2,1)}, bf16[2,64,2048]{2,1,0:T(8,128)(2,1)}, bf16[2,64,2048]{2,1,0:T(8,12...) custom-call(s32[2]{0:T(128)} %copy-done.48, ...), custom_call_target="tpu_custom_call" | custom-call | flops 32000000000 | bytes 30000000 | tf_op jit(solution)/shard_map/attend_back/pallas_call | solution.py:772
  634.1 16.8 %collective-permute-start.122 = (bf16[1,64,2048]{2,1,0:T(8,128)(2,1)}, bf16[1,64,2048]{2,1,0:T(8,128)(2,1)S(1)}, u32[]{:S(2)}, u32[]{:S(2)}) collective-permute-start(bf16[1,64,2048]{2,1,0:T(8,128)(2,1)} %slice_bitcast_fusion.22), channel_id=1, source_target_pairs={{0,4},{1,5},{2,6},{3,7},{4,0},{5,1},{6,2},{7,3},{8,12},{9,13},{10,... | collective-permute-start | bytes 786440 | tf_op jit(solution)/shard_map/outputs/ppermute | solution.py:59
  654.7 10.4 %collective-permute-start.118 = (bf16[2,1536,256]{2,1,0:T(8,128)(2,1)S(1)}, bf16[2,1536,256]{2,1,0:T(8,128)(2,1)S(1)}, u32[]{:S(2)}, u32[]{:S(2)}) collective-permute-start(bf16[2,1536,256]{2,1,0:T(8,128)(2,1)S(1)} %slice_bitcast_fusion.1), channel_id=1, source_target_pairs={{0,2},{1,3},{2,0},{3,1},{4,6},{5,7},{6,4},{7,5},{8,10},{9,11},{10,... | collective-permute-start | bytes 4718600 | tf_op jit(solution)/shard_map/weight_grads/ppermute | solution.py:59
  679.6 9.2 %collective-permute-done.115.refs_0_ = bf16[4,2,64,640]{3,2,1,0:T(8,128)(2,1)S(1)} collective-permute-done((bf16[4,2,64,640]{3,2,1,0:T(8,128)(2,1)S(1)}, bf16[4,2,64,640]{3,2,1,0:T(8,128)(2,1)S(1)}, u32[]{:S(2)}, u32[]{:S(2)}) %collective-permute-start.115) | collective-permute-done | bytes 655392 | tf_op jit(solution)/shard_map/key_grads/ppermute | solution.py:59
  688.8 13.3 %collective-permute-done.116.refs_1_ = bf16[4,2,64,640]{3,2,1,0:T(8,128)(2,1)S(1)} collective-permute-done((bf16[4,2,64,640]{3,2,1,0:T(8,128)(2,1)S(1)}, bf16[4,2,64,640]{3,2,1,0:T(8,128)(2,1)S(1)}, u32[]{:S(2)}, u32[]{:S(2)}) %collective-permute-start.116) | collective-permute-done | bytes 655392 | tf_op jit(solution)/shard_map/key_grads/ppermute | solution.py:59
  730.5 7.6 collective-permute-start.123
  771.7 7.1 collective-permute-done.128.refs_0_
  (987 shorter events, 487.7 us)
Async XLA Ops:
  224.4 29.9 %collective-permute-start.51 = (bf16[2,4,32,2048]{3,2,1,0:T(8,128)(2,1)}, bf16[2,4,32,2048]{3,2,1,0:T(8,128)(2,1)}, u32[]{:S(2)}, u32[]{:S(2)}) collective-permute-start(bf16[2,4,32,2048]{3,2,1,0:T(8,128)(2,1)} %get-tuple-element.400.refs_6_), channel_id=1, source_target_pairs={{0,1},{1,0},{2,3},{3,2},{4,5},{5,4},{6,7},{7,6},{8,9},{9,8},{10,11... | collective-permute-start | bytes 3145736 | tf_op jit(solution)/shard_map/cotangents/ppermute | solution.py:59
  307.9 33.4 %collective-permute-start.67 = (bf16[1,4,32,2048]{3,2,1,0:T(8,128)(2,1)}, bf16[1,4,32,2048]{3,2,1,0:T(8,128)(2,1)S(1)}, u32[]{:S(2)}, u32[]{:S(2)}) collective-permute-start(bf16[1,4,32,2048]{3,2,1,0:T(8,128)(2,1)} %get-tuple-element.739), channel_id=1, source_target_pairs={{0,8},{8,0},{16,24},{24,16},{1,9},{9,1},{17,25},{25,17},{2,10},{10... | collective-permute-start | bytes 1572872 | tf_op jit(solution)/shard_map/cotangents/ppermute | solution.py:59
  308.6 32.7 %collective-permute-start.68 = (bf16[1,4,32,2048]{3,2,1,0:T(8,128)(2,1)}, bf16[1,4,32,2048]{3,2,1,0:T(8,128)(2,1)}, u32[]{:S(2)}, u32[]{:S(2)}) collective-permute-start(bf16[1,4,32,2048]{3,2,1,0:T(8,128)(2,1)} %get-tuple-element.738), channel_id=1, source_target_pairs={{0,16},{8,24},{16,0},{24,8},{1,17},{9,25},{17,1},{25,9},{2,18},{10... | collective-permute-start | bytes 1572872 | tf_op jit(solution)/shard_map/cotangents/ppermute | solution.py:59
  310.6 30.7 %collective-permute-start.69 = (bf16[1,4,32,2048]{3,2,1,0:T(8,128)(2,1)}, bf16[1,4,32,2048]{3,2,1,0:T(8,128)(2,1)}, u32[]{:S(2)}, u32[]{:S(2)}) collective-permute-start(bf16[1,4,32,2048]{3,2,1,0:T(8,128)(2,1)} %get-tuple-element.737), channel_id=1, source_target_pairs={{0,8},{8,0},{16,24},{24,16},{1,9},{9,1},{17,25},{25,17},{2,10},{10... | collective-permute-start | bytes 1572872 | tf_op jit(solution)/shard_map/ffn_rows/ppermute | solution.py:59
  347.1 40.1 %collective-permute-start.74 = (bf16[2,4,32,2048]{3,2,1,0:T(8,128)(2,1)}, bf16[2,4,32,2048]{3,2,1,0:T(8,128)(2,1)}, u32[]{:S(2)}, u32[]{:S(2)}) collective-permute-start(bf16[2,4,32,2048]{3,2,1,0:T(8,128)(2,1)} %pad_maximum_fusion.16.refs_3_), channel_id=1, source_target_pairs={{0,8},{8,0},{16,24},{24,16},{1,9},{9,1},{17,25},{25,17},{2,10},{10... | collective-permute-start | bytes 3145736 | tf_op jit(solution)/shard_map/cotangents/ppermute | solution.py:59
  350.0 37.2 %collective-permute-start.73 = (bf16[2,4,32,2048]{3,2,1,0:T(8,128)(2,1)}, bf16[2,4,32,2048]{3,2,1,0:T(8,128)(2,1)}, u32[]{:S(2)}, u32[]{:S(2)}) collective-permute-start(bf16[2,4,32,2048]{3,2,1,0:T(8,128)(2,1)} %pad_maximum_fusion.15.refs_2_), channel_id=1, source_target_pairs={{0,16},{8,24},{16,0},{24,8},{1,17},{9,25},{17,1},{25,9},{2,18},{10... | collective-permute-start | bytes 3145736 | tf_op jit(solution)/shard_map/cotangents/ppermute | solution.py:59
  353.3 41.7 %collective-permute-start.72 = (bf16[2,4,32,2048]{3,2,1,0:T(8,128)(2,1)}, bf16[2,4,32,2048]{3,2,1,0:T(8,128)(2,1)}, u32[]{:S(2)}, u32[]{:S(2)}) collective-permute-start(bf16[2,4,32,2048]{3,2,1,0:T(8,128)(2,1)} %pad_maximum_fusion.14.refs_3_), channel_id=1, source_target_pairs={{0,8},{8,0},{16,24},{24,16},{1,9},{9,1},{17,25},{25,17},{2,10},{10... | collective-permute-start | bytes 3145736 | tf_op jit(solution)/shard_map/ffn_rows/ppermute | solution.py:59
  356.5 41.0 %collective-permute-start.71 = (bf16[2,4,32,2048]{3,2,1,0:T(8,128)(2,1)}, bf16[2,4,32,2048]{3,2,1,0:T(8,128)(2,1)}, u32[]{:S(2)}, u32[]{:S(2)}) collective-permute-start(bf16[2,4,32,2048]{3,2,1,0:T(8,128)(2,1)} %pad_maximum_fusion.13.refs_2_), channel_id=1, source_target_pairs={{0,16},{8,24},{16,0},{24,8},{1,17},{9,25},{17,1},{25,9},{2,18},{10... | collective-permute-start | bytes 3145736 | tf_op jit(solution)/shard_map/ffn_rows/ppermute | solution.py:59
  406.6 32.6 %collective-permute-start.79 = (bf16[2,4,32,2048]{3,2,1,0:T(8,128)(2,1)}, bf16[2,4,32,2048]{3,2,1,0:T(8,128)(2,1)}, u32[]{:S(2)}, u32[]{:S(2)}) collective-permute-start(bf16[2,4,32,2048]{3,2,1,0:T(8,128)(2,1)} %get-tuple-element.476), channel_id=1, source_target_pairs={{0,16},{8,24},{16,0},{24,8},{1,17},{9,25},{17,1},{25,9},{2,18},{10... | collective-permute-start | bytes 3145736 | tf_op jit(solution)/shard_map/ffn_grads/ppermute | solution.py:59
  407.6 31.6 %collective-permute-start.80 = (bf16[2,4,32,2048]{3,2,1,0:T(8,128)(2,1)}, bf16[2,4,32,2048]{3,2,1,0:T(8,128)(2,1)}, u32[]{:S(2)}, u32[]{:S(2)}) collective-permute-start(bf16[2,4,32,2048]{3,2,1,0:T(8,128)(2,1)} %get-tuple-element.477), channel_id=1, source_target_pairs={{0,8},{8,0},{16,24},{24,16},{1,9},{9,1},{17,25},{25,17},{2,10},{10... | collective-permute-start | bytes 3145736 | tf_op jit(solution)/shard_map/ffn_grads/ppermute | solution.py:59
  439.8 54.0 %collective-permute-start.77 = (bf16[2,4,32,2048]{3,2,1,0:T(8,128)(2,1)}, bf16[2,4,32,2048]{3,2,1,0:T(8,128)(2,1)}, u32[]{:S(2)}, u32[]{:S(2)}) collective-permute-start(bf16[2,4,32,2048]{3,2,1,0:T(8,128)(2,1)} %get-tuple-element.466), channel_id=1, source_target_pairs={{0,16},{8,24},{16,0},{24,8},{1,17},{9,25},{17,1},{25,9},{2,18},{10... | collective-permute-start | bytes 3145736 | tf_op jit(solution)/shard_map/outputs/ppermute | solution.py:59
  440.8 53.1 %collective-permute-start.78 = (bf16[2,4,32,2048]{3,2,1,0:T(8,128)(2,1)}, bf16[2,4,32,2048]{3,2,1,0:T(8,128)(2,1)}, u32[]{:S(2)}, u32[]{:S(2)}) collective-permute-start(bf16[2,4,32,2048]{3,2,1,0:T(8,128)(2,1)} %get-tuple-element.467), channel_id=1, source_target_pairs={{0,8},{8,0},{16,24},{24,16},{1,9},{9,1},{17,25},{25,17},{2,10},{10... | collective-permute-start | bytes 3145736 | tf_op jit(solution)/shard_map/outputs/ppermute | solution.py:59
  443.7 38.8 %collective-permute-start.92 = (bf16[1,4,32,2048]{3,2,1,0:T(8,128)(2,1)}, bf16[1,4,32,2048]{3,2,1,0:T(8,128)(2,1)S(1)}, u32[]{:S(2)}, u32[]{:S(2)}) collective-permute-start(bf16[1,4,32,2048]{3,2,1,0:T(8,128)(2,1)} %add_convert_fusion.29), channel_id=1, source_target_pairs={{0,16},{8,24},{16,0},{24,8},{1,17},{9,25},{17,1},{25,9},{2,18},{10... | collective-permute-start | bytes 1572872 | tf_op jit(solution)/shard_map/ffn_grads/ppermute | solution.py:59
  447.1 35.5 %collective-permute-start.91 = (bf16[1,4,32,2048]{3,2,1,0:T(8,128)(2,1)}, bf16[1,4,32,2048]{3,2,1,0:T(8,128)(2,1)}, u32[]{:S(2)}, u32[]{:S(2)}) collective-permute-start(bf16[1,4,32,2048]{3,2,1,0:T(8,128)(2,1)} %add_convert_fusion.30), channel_id=1, source_target_pairs={{0,8},{8,0},{16,24},{24,16},{1,9},{9,1},{17,25},{25,17},{2,10},{10... | collective-permute-start | bytes 1572872 | tf_op jit(solution)/shard_map/ffn_grads/ppermute | solution.py:59
  497.1 57.6 %collective-permute-start.101 = (bf16[1,4,32,2048]{3,2,1,0:T(8,128)(2,1)}, bf16[1,4,32,2048]{3,2,1,0:T(8,128)(2,1)}, u32[]{:S(2)}, u32[]{:S(2)}) collective-permute-start(bf16[1,4,32,2048]{3,2,1,0:T(8,128)(2,1)} %add_convert_fusion.17), channel_id=1, source_target_pairs={{0,16},{8,24},{16,0},{24,8},{1,17},{9,25},{17,1},{25,9},{2,18},{10... | collective-permute-start | bytes 1572872 | tf_op jit(solution)/shard_map/outputs/ppermute | solution.py:59
  500.4 54.3 %collective-permute-start.100 = (bf16[1,4,32,2048]{3,2,1,0:T(8,128)(2,1)}, bf16[1,4,32,2048]{3,2,1,0:T(8,128)(2,1)}, u32[]{:S(2)}, u32[]{:S(2)}) collective-permute-start(bf16[1,4,32,2048]{3,2,1,0:T(8,128)(2,1)} %add_convert_fusion.18), channel_id=1, source_target_pairs={{0,8},{8,0},{16,24},{24,16},{1,9},{9,1},{17,25},{25,17},{2,10},{10... | collective-permute-start | bytes 1572872 | tf_op jit(solution)/shard_map/outputs/ppermute | solution.py:59
  595.4 35.7 %collective-permute-start.110 = (bf16[2,3,88,256]{3,2,1,0:T(8,128)(2,1)}, bf16[2,3,88,256]{3,2,1,0:T(8,128)(2,1)}, u32[]{:S(2)}, u32[]{:S(2)}) collective-permute-start(bf16[2,3,88,256]{3,2,1,0:T(8,128)(2,1)} %bitcast.469), channel_id=1, source_target_pairs={{0,2},{1,3},{2,0},{3,1},{4,6},{5,7},{6,4},{7,5},{8,10},{9,11},{10,... | collective-permute-start | bytes 811016 | tf_op jit(solution)/shard_map/shared_grads/ppermute | solution.py:59
  596.1 35.0 %collective-permute-start.111 = (bf16[2,3,88,256]{3,2,1,0:T(8,128)(2,1)}, bf16[2,3,88,256]{3,2,1,0:T(8,128)(2,1)}, u32[]{:S(2)}, u32[]{:S(2)}) collective-permute-start(bf16[2,3,88,256]{3,2,1,0:T(8,128)(2,1)} %bitcast.468), channel_id=1, source_target_pairs={{0,4},{1,5},{2,6},{3,7},{4,0},{5,1},{6,2},{7,3},{8,12},{9,13},{10,... | collective-permute-start | bytes 811016 | tf_op jit(solution)/shard_map/shared_grads/ppermute | solution.py:59
  599.1 32.0 %collective-permute-start.112 = (bf16[2,3,88,256]{3,2,1,0:T(8,128)(2,1)}, bf16[2,3,88,256]{3,2,1,0:T(8,128)(2,1)}, u32[]{:S(2)}, u32[]{:S(2)}) collective-permute-start(bf16[2,3,88,256]{3,2,1,0:T(8,128)(2,1)} %bitcast.467), channel_id=1, source_target_pairs={{0,6},{1,7},{2,4},{3,5},{4,2},{5,3},{6,0},{7,1},{8,14},{9,15},{10,... | collective-permute-start | bytes 811016 | tf_op jit(solution)/shard_map/shared_grads/ppermute | solution.py:59
  634.1 82.2 %collective-permute-start.122 = (bf16[1,64,2048]{2,1,0:T(8,128)(2,1)}, bf16[1,64,2048]{2,1,0:T(8,128)(2,1)S(1)}, u32[]{:S(2)}, u32[]{:S(2)}) collective-permute-start(bf16[1,64,2048]{2,1,0:T(8,128)(2,1)} %slice_bitcast_fusion.22), channel_id=1, source_target_pairs={{0,4},{1,5},{2,6},{3,7},{4,0},{5,1},{6,2},{7,3},{8,12},{9,13},{10,... | collective-permute-start | bytes 786440 | tf_op jit(solution)/shard_map/outputs/ppermute | solution.py:59
  654.7 47.4 %collective-permute-start.118 = (bf16[2,1536,256]{2,1,0:T(8,128)(2,1)S(1)}, bf16[2,1536,256]{2,1,0:T(8,128)(2,1)S(1)}, u32[]{:S(2)}, u32[]{:S(2)}) collective-permute-start(bf16[2,1536,256]{2,1,0:T(8,128)(2,1)S(1)} %slice_bitcast_fusion.1), channel_id=1, source_target_pairs={{0,2},{1,3},{2,0},{3,1},{4,6},{5,7},{6,4},{7,5},{8,10},{9,11},{10,... | collective-permute-start | bytes 4718600 | tf_op jit(solution)/shard_map/weight_grads/ppermute | solution.py:59
  671.9 30.2 %collective-permute-start.116 = (bf16[4,2,64,640]{3,2,1,0:T(8,128)(2,1)S(1)}, bf16[4,2,64,640]{3,2,1,0:T(8,128)(2,1)S(1)}, u32[]{:S(2)}, u32[]{:S(2)}) collective-permute-start(bf16[4,2,64,640]{3,2,1,0:T(8,128)(2,1)S(1)} %get-tuple-element.708), channel_id=1, source_target_pairs={{0,16},{8,24},{16,0},{24,8},{1,17},{9,25},{17,1},{25,9},{2,18},{10... | collective-permute-start | bytes 1966088 | tf_op jit(solution)/shard_map/key_grads/ppermute | solution.py:59
  740.0 31.0 %collective-permute-start.133 = (bf16[4,3,88,256]{3,2,1,0:T(8,128)(2,1)}, bf16[4,3,88,256]{3,2,1,0:T(8,128)(2,1)}, u32[]{:S(2)}, u32[]{:S(2)}) collective-permute-start(bf16[4,3,88,256]{3,2,1,0:T(8,128)(2,1)} %get-tuple-element.727), channel_id=1, source_target_pairs={{0,1},{1,0},{2,3},{3,2},{4,5},{5,4},{6,7},{7,6},{8,9},{9,8},{10,11... | collective-permute-start | bytes 1622024 | tf_op jit(solution)/shard_map/shared_grads/ppermute | solution.py:59
  740.0 38.9 %collective-permute-start.128 = (bf16[1,1536,256]{2,1,0:T(8,128)(2,1)}, bf16[1,1536,256]{2,1,0:T(8,128)(2,1)}, u32[]{:S(2)}, u32[]{:S(2)}) collective-permute-start(bf16[1,1536,256]{2,1,0:T(8,128)(2,1)} %slice_bitcast_fusion.3), channel_id=1, source_target_pairs={{0,4},{1,5},{2,6},{3,7},{4,0},{5,1},{6,2},{7,3},{8,12},{9,13},{10,... | collective-permute-start | bytes 2359304 | tf_op jit(solution)/shard_map/weight_grads/ppermute | solution.py:59
  (328 other events, 2937.3 us)
